TPU v7x, 512 devices: a whole 4x8x8 slice. The times are simulated.
512 devices in a mesh: row: 4 (over x_hi, core), col: 16 (over z, x_lo), rep: 8 (over y).
Axes of the slice: x: 4 (x_hi: 2, x_lo: 2; x = x_hi * 2 + x_lo), y: 8, z: 8, core: 2. Of those that a mesh axis runs over, the one named last changes fastest.
Arguments:
- amplitudes: bfloat16 [1024, 327680], P(('row', 'col', 'rep')), may hold values from -24 to 24
- integrals: bfloat16 [327680, 1024], P(('col', 'rep'), 'row'), may hold values from -0.009765625 to 0.009765625
Outputs:
- ladder: float32 [1024, 1024], P(('row', 'col', 'rep'))
All inputs are finite; a program needn't handle non-finite values.
Results may differ from a plain program's by a relative error of at most 0.0003.
Values may be sent and summed in bfloat16 or wider, within the bound.
No kernel may reach another device: no remote copies, remote signals or barrier semaphores. Data moves between devices by JAX's collectives and lax.ppermute only.
A program may use at most 64 MiB of HBM per device.

v0:
```python
import jax
import jax.numpy as jnp
from jax import lax
from jax.sharding import PartitionSpec as P


def shards(amplitudes, integrals):
    blocks = lax.all_to_all(amplitudes, ("col", "rep"), split_axis=1, concat_axis=0, tiled=True)
    gathered = lax.all_gather(integrals, "row", axis=1, tiled=True)
    contracted = lax.psum_scatter(
        jnp.dot(blocks, gathered, preferred_element_type=jnp.float32),
        ("col", "rep"),
        scatter_dimension=0,
        tiled=True,
    )
    return 0.5 * contracted


def solution(mesh):
    in_specs = (P(("row", "col", "rep"), None), P(("col", "rep"), "row"))
    out_specs = P(("row", "col", "rep"), None)
    return jax.shard_map(shards, mesh=mesh, in_specs=in_specs, out_specs=out_specs, check_vma=False)
```

profile of v0, /device:TPU:4, one launch (start us, length us, event | category | flops | bytes accessed | tf_op | source)
XLA Modules:
  0.0 1283.7 jit_solution(8320892417724589441)
XLA Ops:
  6.5 0.0 copy-start
  6.5 0.0 all-gather.2.cloned.1.call-start
  6.5 0.7 all-gather.2.cloned.1.call-update
  7.3 0.0 all-reduce.3.cloned.1.call-start
  7.3 0.5 copy-done
  7.9 54.6 %all_to_all.19 = bf16[2,128,2560]{2,0,1:T(2,128)(2,1)S(1)} all-to-all(bf16[2,128,2560]{2,0,1:T(2,128)(2,1)S(1)} %bitcast.6), channel_id=1, replica_groups=mesh['row'=4,'col'=16,'rep'=8] {'col','rep'}, dimensions={1} | all-to-all | bytes 2621440 | tf_op jit(solution)/shard_map/all_to_all | solution.py:8
  62.4 0.5 all_to_all.17
  62.9 11.5 all-gather.2.cloned.1.call-done
  74.4 5.0 fusion
  79.4 0.0 all-reduce.3.cloned.1.call-update
  79.4 1.3 dynamic-slice
  81.4 1194.1 %all-reduce.3.cloned.1.call-done = f32[256,1024]{1,0:T(8,128)} async-done(((f32[256,1024]{1,0:T(8,128)}), f32[256,1024]{1,0:T(8,128)}) %all-reduce.3.cloned.1.call-update) | async-done | bytes 1048592
  1275.5 1.4 dynamic-slice_multiply_fusion
Async XLA Ops:
  6.5 1.3 copy-start
  6.5 67.9 %all-gather.2.cloned.1.call-start = ((), (), s32[]{:S(2)}) async-start(), calls=%async_computation.1 | async-start | bytes 6553600 | tf_op jit(solution)/shard_map/all_gather | solution.py:9
  7.3 1268.2 %all-reduce.3.cloned.1.call-start = ((), (), s32[]{:S(2)}) async-start(), calls=%async_computation.2 | async-start | bytes 2097152
Sparse Core Ops, SparseCore 0:
  9.5 64.9 all-gather.1
  79.6 1195.8 all-reduce.2
where the time goes:
time: 1280 us
  waiting for transfers between devices  1210 us (95%)
  blocking collectives  54.6 us (4%)
  between operations  14.1 us (1%)
    unnamed x3, waiting for transfers between devices  1190 us
    all_to_all x1, blocking collectives, shards(): lax.all_to_all(amplitudes, ('col', 'rep'), split_axis=1, concat_axis=0, t...  54.6 us
  transfers between devices with their start and end apart: 2, of which 2 were waited for; matrix products, arithmetic and copies ran while one was open for 0% of the time, Pallas kernels for 0%

commit v1 on v0

v1 whole, which is shorter than its diff:
```python
import jax
import jax.numpy as jnp
from jax import lax
from jax.sharding import Mesh, PartitionSpec as P


def pairs(a, b):
    moves = []
    for xh in range(2):
        for core in range(2):
            for xl in range(2):
                source = (xh * 2 + core) * 2 + xl
                target = ((xh ^ a) * 2 + xl) * 2 + (core ^ b)
                moves.append((source, target))
    return moves


def shards(amplitudes, integrals):
    pieces = [lax.ppermute(integrals, ("xh", "core", "xl"), pairs(a, b)) for a, b in ((1, 0), (1, 1), (0, 0), (0, 1))]
    blocks = lax.all_to_all(amplitudes, ("z", "core", "y"), split_axis=1, concat_axis=0, tiled=True)
    far0, far1, near0, near1 = [jnp.dot(blocks, p, preferred_element_type=jnp.float32) for p in pieces]
    core, xh, xl = lax.axis_index("core"), lax.axis_index("xh"), lax.axis_index("xl")
    partial = jnp.concatenate([near0, near1, far0, far1], axis=1).reshape(8, 2, 16, 1024)
    mine = lax.dynamic_index_in_dim(partial, core, 1, False)
    other = lax.dynamic_index_in_dim(partial, 1 - core, 1, False)
    both = mine + lax.ppermute(other, "core", [(0, 1), (1, 0)])
    parts = lax.all_to_all(both.reshape(128, 1024), ("z", "y"), split_axis=0, concat_axis=0, tiled=True)
    total = 0.5 * parts.reshape(64, 2, 1024).sum(0)
    total = total.reshape(2, 2, 2, 256)
    total = jnp.where(xh == 1, total[:, ::-1], total)
    total = jnp.where(xl == 1, total[:, :, ::-1], total)
    return total.reshape(2, 1024)


def solution(mesh):
    fine = Mesh(mesh.devices.reshape(2, 2, 8, 2, 8), ("xh", "core", "z", "xl", "y"))
    rows = P(("xh", "core", "z", "xl", "y"), None)
    in_specs = (rows, P(("z", "xl", "y"), ("xh", "core")))
    return jax.shard_map(shards, mesh=fine, in_specs=in_specs, out_specs=rows, check_vma=False)
```

time: 1280 us -> 129 us (0.10)
  the two profiles are of different devices: /device:TPU:4 before, /device:TPU:6 now
where the time goes in v1:
time: 129 us; the launch traced here: 127 us
  waiting for transfers between devices  71.9 us (56%)
  starting transfers between devices  44.5 us (34%)
  matrix products  7.76 us (6%)
  local copies, waits for them, and re-layouts  2.73 us (2%)
    ppermute x4, waiting for transfers between devices, shards(): lax.ppermute(integrals, ('xh', 'core', 'xl'), pairs(a, b))  26.7 us
    all_to_all x1, waiting for transfers between devices, shards(): lax.all_to_all(amplitudes, ('z', 'core', 'y'), split_axis=1, concat_axis=...  23.4 us
    all_to_all x1, waiting for transfers between devices, shards(): lax.all_to_all(both.reshape(128, 1024), ('z', 'y'), split_axis=0, concat_...  19.9 us
    all_to_all x1, starting transfers between devices, shards(): lax.all_to_all(amplitudes, ('z', 'core', 'y'), split_axis=1, concat_axis=...  17.8 us
    all_to_all x1, starting transfers between devices, shards(): lax.all_to_all(both.reshape(128, 1024), ('z', 'y'), split_axis=0, concat_...  12.9 us
    ppermute x4, starting transfers between devices, shards(): lax.ppermute(integrals, ('xh', 'core', 'xl'), pairs(a, b))  11.9 us
    dot_general x4, matrix products, shards(): jnp.dot(blocks, p, preferred_element_type=jnp.float32)  7.76 us
  transfers between devices with their start and end apart: 7, of which 4 were waited for; matrix products, arithmetic and copies ran while one was open for 5% of the time, Pallas kernels for 0%

profile of v1, /device:TPU:6, one launch (start us, length us, event | category | flops | bytes accessed | tf_op | source)
XLA Modules:
  0.0 127.4 jit_solution(4242500035396718982)
XLA Ops:
  0.0 17.8 %all-to-all-start = ((bf16[2,128,2560]{2,0,1:T(2,128)(2,1)}), bf16[2,128,2560]{2,0,1:T(2,128)(2,1)S(1)}, u32[]{:S(2)}, u32[]{:S(2)}) async-start(bf16[2,128,2560]{2,0,1:T(2,128)(2,1)} %bitcast.18), calls=%async_computation | async-start | bytes 2621440 | tf_op jit(solution)/shard_map/all_to_all | solution.py:20
  17.8 2.5 %collective-permute-start.3 = (bf16[2560,256]{1,0:T(8,128)(2,1)}, bf16[2560,256]{1,0:T(8,128)(2,1)}, u32[]{:S(2)}, u32[]{:S(2)}) collective-permute-start(bf16[2560,256]{1,0:T(8,128)(2,1)} %param.3), channel_id=1, source_target_pairs={{0,264},{8,392},{128,256},{136,384},{256,8},{264,136},{384,0},{392... | collective-permute-start | bytes 3932168 | tf_op jit(solution)/shard_map/ppermute | solution.py:19
  20.4 4.5 %collective-permute-start.2 = (bf16[2560,256]{1,0:T(8,128)(2,1)}, bf16[2560,256]{1,0:T(8,128)(2,1)}, u32[]{:S(2)}, u32[]{:S(2)}) collective-permute-start(bf16[2560,256]{1,0:T(8,128)(2,1)} %param.3), channel_id=1, source_target_pairs={{0,256},{8,384},{128,264},{136,392},{256,0},{264,128},{384,8},{392... | collective-permute-start | bytes 3932168 | tf_op jit(solution)/shard_map/ppermute | solution.py:19
  24.9 1.9 %collective-permute-start.1 = (bf16[2560,256]{1,0:T(8,128)(2,1)}, bf16[2560,256]{1,0:T(8,128)(2,1)}, u32[]{:S(2)}, u32[]{:S(2)}) collective-permute-start(bf16[2560,256]{1,0:T(8,128)(2,1)} %param.3), channel_id=1, source_target_pairs={{0,8},{8,136},{128,0},{136,128},{256,264},{264,392},{384,256},{392... | collective-permute-start | bytes 3932168 | tf_op jit(solution)/shard_map/ppermute | solution.py:19
  26.8 2.9 %collective-permute-start = (bf16[2560,256]{1,0:T(8,128)(2,1)}, bf16[2560,256]{1,0:T(8,128)(2,1)}, u32[]{:S(2)}, u32[]{:S(2)}) collective-permute-start(bf16[2560,256]{1,0:T(8,128)(2,1)} %param.3), channel_id=1, source_target_pairs={{0,0},{8,128},{128,8},{136,136},{256,256},{264,384},{384,264},{392... | collective-permute-start | bytes 3932168 | tf_op jit(solution)/shard_map/ppermute | solution.py:19
  29.7 23.4 %all-to-all-done = bf16[2,128,2560]{2,0,1:T(2,128)(2,1)S(1)} async-done(((bf16[2,128,2560]{2,0,1:T(2,128)(2,1)}), bf16[2,128,2560]{2,0,1:T(2,128)(2,1)S(1)}, u32[]{:S(2)}, u32[]{:S(2)}) %all-to-all-start) | async-done | bytes 1310752 | tf_op jit(solution)/shard_map/all_to_all | solution.py:20
  53.1 0.5 all_to_all.23
  53.7 26.7 %collective-permute-done.3 = bf16[2560,256]{1,0:T(8,128)(2,1)} collective-permute-done((bf16[2560,256]{1,0:T(8,128)(2,1)}, bf16[2560,256]{1,0:T(8,128)(2,1)}, u32[]{:S(2)}, u32[]{:S(2)}) %collective-permute-start.3) | collective-permute-done | bytes 1310752 | tf_op jit(solution)/shard_map/ppermute | solution.py:19
  80.4 1.9 %fusion.3 = f32[256,256]{0,1:T(8,128)S(1)} fusion(bf16[256,2560]{1,0:T(8,128)(2,1)S(1)} %all_to_all.23, bf16[2560,256]{1,0:T(8,128)(2,1)} %collective-permute-done.3), kind=kOutput, calls=%fused_computation.8 | convolution fusion | flops 335544320 | bytes 2883584 | tf_op jit(solution)/shard_map/dot_general | solution.py:21
  82.4 1.9 %fusion.2 = f32[256,256]{0,1:T(8,128)S(1)} fusion(bf16[256,2560]{1,0:T(8,128)(2,1)S(1)} %all_to_all.23, bf16[2560,256]{1,0:T(8,128)(2,1)} %collective-permute-done.2), kind=kOutput, calls=%fused_computation.7 | convolution fusion | flops 335544320 | bytes 2883584 | tf_op jit(solution)/shard_map/dot_general | solution.py:21
  84.3 1.9 %fusion.1 = f32[256,256]{0,1:T(8,128)S(1)} fusion(bf16[256,2560]{1,0:T(8,128)(2,1)S(1)} %all_to_all.23, bf16[2560,256]{1,0:T(8,128)(2,1)} %collective-permute-done.1), kind=kOutput, calls=%fused_computation.6 | convolution fusion | flops 335544320 | bytes 2883584 | tf_op jit(solution)/shard_map/dot_general | solution.py:21
  86.3 1.9 %fusion = f32[256,256]{0,1:T(8,128)S(1)} fusion(bf16[256,2560]{1,0:T(8,128)(2,1)S(1)} %all_to_all.23, bf16[2560,256]{1,0:T(8,128)(2,1)} %collective-permute-done), kind=kOutput, calls=%fused_computation.5 | convolution fusion | flops 335544320 | bytes 2883584 | tf_op jit(solution)/shard_map/dot_general | solution.py:21
  88.2 0.1 pad_maximum_fusion
  88.3 0.3 copy.4
  88.6 0.1 dynamic-slice_bitcast_fusion
  88.7 1.9 %collective-permute-start.4 = (f32[8,16,1024]{2,1,0:T(8,128)S(1)}, f32[8,16,1024]{2,1,0:T(8,128)S(1)}, u32[]{:S(2)}, u32[]{:S(2)}) collective-permute-start(f32[8,16,1024]{2,1,0:T(8,128)S(1)} %dynamic-slice_bitcast_fusion), channel_id=1, source_target_pairs={{0,128},{128,0},{1,129},{129,1},{2,130},{130,2},{3,131},{131,3},{4... | collective-permute-start | bytes 1572872 | tf_op jit(solution)/shard_map/ppermute | solution.py:26
  90.6 1.9 %collective-permute-done.4 = f32[8,16,1024]{2,1,0:T(8,128)S(1)} collective-permute-done((f32[8,16,1024]{2,1,0:T(8,128)S(1)}, f32[8,16,1024]{2,1,0:T(8,128)S(1)}, u32[]{:S(2)}, u32[]{:S(2)}) %collective-permute-start.4) | collective-permute-done | bytes 524320 | tf_op jit(solution)/shard_map/ppermute | solution.py:26
  92.5 0.1 bitcast_add_fusion
  92.6 1.1 all_to_all.24
  93.7 12.9 %all-to-all-start.1 = ((f32[64,2,1024]{2,1,0:T(2,128)}), f32[64,2,1024]{2,1,0:T(2,128)S(1)}, u32[]{:S(2)}, u32[]{:S(2)}) async-start(f32[64,2,1024]{2,1,0:T(2,128)} %all_to_all.24), calls=%async_computation.1 | async-start | bytes 1048576 | tf_op jit(solution)/shard_map/all_to_all | solution.py:27
  106.6 19.9 %all-to-all-done.1 = f32[64,2,1024]{2,1,0:T(2,128)S(1)} async-done(((f32[64,2,1024]{2,1,0:T(2,128)}), f32[64,2,1024]{2,1,0:T(2,128)S(1)}, u32[]{:S(2)}, u32[]{:S(2)}) %all-to-all-start.1) | async-done | bytes 524320 | tf_op jit(solution)/shard_map/all_to_all | solution.py:27
  126.4 0.2 reduce_sum.11
  126.7 0.1 rev.7
  126.8 0.6 reshape.18
  (6 shorter events, 0.0 us)
Async XLA Ops:
  0.0 53.1 %all-to-all-start = ((bf16[2,128,2560]{2,0,1:T(2,128)(2,1)}), bf16[2,128,2560]{2,0,1:T(2,128)(2,1)S(1)}, u32[]{:S(2)}, u32[]{:S(2)}) async-start(bf16[2,128,2560]{2,0,1:T(2,128)(2,1)} %bitcast.18), calls=%async_computation | async-start | bytes 2621440 | tf_op jit(solution)/shard_map/all_to_all | solution.py:20
  17.8 62.6 %collective-permute-start.3 = (bf16[2560,256]{1,0:T(8,128)(2,1)}, bf16[2560,256]{1,0:T(8,128)(2,1)}, u32[]{:S(2)}, u32[]{:S(2)}) collective-permute-start(bf16[2560,256]{1,0:T(8,128)(2,1)} %param.3), channel_id=1, source_target_pairs={{0,264},{8,392},{128,256},{136,384},{256,8},{264,136},{384,0},{392... | collective-permute-start | bytes 3932168 | tf_op jit(solution)/shard_map/ppermute | solution.py:19
  20.4 62.0 %collective-permute-start.2 = (bf16[2560,256]{1,0:T(8,128)(2,1)}, bf16[2560,256]{1,0:T(8,128)(2,1)}, u32[]{:S(2)}, u32[]{:S(2)}) collective-permute-start(bf16[2560,256]{1,0:T(8,128)(2,1)} %param.3), channel_id=1, source_target_pairs={{0,256},{8,384},{128,264},{136,392},{256,0},{264,128},{384,8},{392... | collective-permute-start | bytes 3932168 | tf_op jit(solution)/shard_map/ppermute | solution.py:19
  24.9 59.4 %collective-permute-start.1 = (bf16[2560,256]{1,0:T(8,128)(2,1)}, bf16[2560,256]{1,0:T(8,128)(2,1)}, u32[]{:S(2)}, u32[]{:S(2)}) collective-permute-start(bf16[2560,256]{1,0:T(8,128)(2,1)} %param.3), channel_id=1, source_target_pairs={{0,8},{8,136},{128,0},{136,128},{256,264},{264,392},{384,256},{392... | collective-permute-start | bytes 3932168 | tf_op jit(solution)/shard_map/ppermute | solution.py:19
  26.8 59.5 %collective-permute-start = (bf16[2560,256]{1,0:T(8,128)(2,1)}, bf16[2560,256]{1,0:T(8,128)(2,1)}, u32[]{:S(2)}, u32[]{:S(2)}) collective-permute-start(bf16[2560,256]{1,0:T(8,128)(2,1)} %param.3), channel_id=1, source_target_pairs={{0,0},{8,128},{128,8},{136,136},{256,256},{264,384},{384,264},{392... | collective-permute-start | bytes 3932168 | tf_op jit(solution)/shard_map/ppermute | solution.py:19
  88.7 3.8 %collective-permute-start.4 = (f32[8,16,1024]{2,1,0:T(8,128)S(1)}, f32[8,16,1024]{2,1,0:T(8,128)S(1)}, u32[]{:S(2)}, u32[]{:S(2)}) collective-permute-start(f32[8,16,1024]{2,1,0:T(8,128)S(1)} %dynamic-slice_bitcast_fusion), channel_id=1, source_target_pairs={{0,128},{128,0},{1,129},{129,1},{2,130},{130,2},{3,131},{131,3},{4... | collective-permute-start | bytes 1572872 | tf_op jit(solution)/shard_map/ppermute | solution.py:26
  93.7 32.8 %all-to-all-start.1 = ((f32[64,2,1024]{2,1,0:T(2,128)}), f32[64,2,1024]{2,1,0:T(2,128)S(1)}, u32[]{:S(2)}, u32[]{:S(2)}) async-start(f32[64,2,1024]{2,1,0:T(2,128)} %all_to_all.24), calls=%async_computation.1 | async-start | bytes 1048576 | tf_op jit(solution)/shard_map/all_to_all | solution.py:27

commit v2 on v0

v2 whole, which is shorter than its diff:
```python
import jax
import jax.numpy as jnp
from jax import lax
from jax.experimental import pallas as pl
from jax.experimental.pallas import tpu as pltpu
from jax.sharding import Mesh, PartitionSpec as P

RING = ("xh", "xl")
RIGHT = [(i, (i + 1) % 4) for i in range(4)]
LEFT = [(i, (i + 3) % 4) for i in range(4)]
SWAP = [(0, 1), (1, 0)]
VMEM = pl.BlockSpec(memory_space=pltpu.VMEM)
ANY = pl.BlockSpec(memory_space=pl.ANY)


def fetch(across, blocks, held, sems):
    core, xh, xl = lax.axis_index("core"), lax.axis_index("xh"), lax.axis_index("xl")
    here, left, right, far_top, far_low = blocks
    wanted = 1 - core if across else core

    @pl.when(xl == wanted)
    def _():
        pltpu.make_async_copy(here, held.at[xh], sems.at[xh]).start()
        pltpu.make_async_copy(far_top, held.at[1 - xh, :1280], sems.at[1 - xh]).start()
        pltpu.make_async_copy(far_low, held.at[1 - xh, 1280:], sems.at[1 - xh]).start()

    @pl.when(xl != wanted)
    def _():
        pltpu.make_async_copy(right, held.at[lax.rem(xh + xl, 2)], sems.at[lax.rem(xh + xl, 2)]).start()
        pltpu.make_async_copy(left, held.at[lax.rem(xh + 1 - xl, 2)], sems.at[lax.rem(xh + 1 - xl, 2)]).start()

    return [pltpu.make_async_copy(here, held.at[place], sems.at[place]) for place in range(2)]


def first_half(rows_ref, here, left, right, far_top, far_low, sum_ref, held, sems):
    copies = fetch(False, (here, left, right, far_top, far_low), held, sems)
    for xh in range(2):
        copies[xh].wait()
        sum_ref[:, 256 * xh : 256 * xh + 256] = jnp.dot(rows_ref[...], held[xh], preferred_element_type=jnp.float32)


def second_half(sum_ref, rows_ref, here, left, right, far_top, far_low, mine_ref, theirs_ref, held, sems):
    core = lax.axis_index("core")
    copies = fetch(True, (here, left, right, far_top, far_low), held, sems)
    for xh in range(2):
        copies[xh].wait()
        total = jnp.dot(rows_ref[...], held[xh], preferred_element_type=jnp.float32)
        total = total + sum_ref[:, 256 * xh : 256 * xh + 256]
        total = total.reshape(8, 2, 16, 256)
        first, second = total[:, 0].reshape(128, 256), total[:, 1].reshape(128, 256)
        mine = jnp.where(core == 0, first, second)
        theirs = jnp.where(core == 0, second, first)
        for half in range(2):
            place = pl.ds(2 * xh + half, 128, stride=4)
            mine_ref[place, :] = mine[:, 128 * half : 128 * half + 128]
            theirs_ref[place, :] = theirs[:, 128 * half : 128 * half + 128]


def call(kernel, n_vmem, shapes):
    return pl.pallas_call(
        kernel,
        out_shape=[jax.ShapeDtypeStruct(shape, jnp.float32) for shape in shapes],
        in_specs=[VMEM] * n_vmem + [ANY] * 5,
        out_specs=[VMEM] * len(shapes),
        scratch_shapes=[pltpu.VMEM((2, 2560, 256), jnp.bfloat16), pltpu.SemaphoreType.DMA((2,))],
        compiler_params=pltpu.CompilerParams(vmem_limit_bytes=LIMIT),
        cost_estimate=pl.CostEstimate(flops=FLOPS, bytes_accessed=2**22, transcendentals=0),
    )


def halves(left, right, top_ref, low_ref, sems):
    top = pltpu.make_async_copy(left.at[:1280], top_ref, sems.at[0])
    low = pltpu.make_async_copy(right.at[1280:], low_ref, sems.at[1])
    top.start()
    low.start()
    top.wait()
    low.wait()


def halved(left, right):
    return pl.pallas_call(
        halves,
        out_shape=[jax.ShapeDtypeStruct((1280, 256), jnp.bfloat16)] * 2,
        in_specs=[ANY, ANY],
        out_specs=[ANY, ANY],
        scratch_shapes=[pltpu.SemaphoreType.DMA((2,))],
        compiler_params=pltpu.CompilerParams(vmem_limit_bytes=LIMIT),
        cost_estimate=pl.CostEstimate(flops=G_FLOPS, bytes_accessed=2**21, transcendentals=0),
    )(left, right)


G_FLOPS = 4 * 10**10
LIMIT = 16 * 2**20
FLOPS = 4 * 10**10


def shards(amplitudes, integrals):
    core = lax.axis_index("core")
    left = lax.ppermute(integrals, RING, RIGHT)
    right = lax.ppermute(integrals, RING, LEFT)
    far_from = halved(left, right)
    far_top = lax.ppermute(far_from[0], RING, RIGHT)
    far_low = lax.ppermute(far_from[1], RING, LEFT)
    blocks = (integrals, left, right, far_top, far_low)
    own = lax.all_to_all(amplitudes, ("z", "core", "y"), split_axis=1, concat_axis=0, tiled=True)
    own, _, _ = lax.optimization_barrier((own, *far_from))
    other = lax.ppermute(own, "core", SWAP)
    (half_sum,) = call(first_half, 1, [(256, 512)])(own, *blocks)
    mine, theirs = call(second_half, 2, [(512, 128)] * 2)(half_sum, other, *blocks)
    got = lax.ppermute(theirs, "core", SWAP)
    mine, got = mine.reshape(64, 8, 128), got.reshape(64, 8, 128)
    first, second = jnp.where(core == 0, mine, got), jnp.where(core == 0, got, mine)
    partial = jnp.concatenate([first, second], axis=1)
    parts = lax.all_to_all(partial, ("z", "y"), split_axis=0, concat_axis=0, tiled=True)
    total = 0.5 * jnp.sum(parts, axis=0)
    return total.reshape(2, 2, 2, 256).transpose(1, 2, 0, 3).reshape(2, 1024)


def solution(mesh):
    fine = Mesh(mesh.devices.reshape(2, 2, 8, 2, 8), ("xh", "core", "z", "xl", "y"))
    rows = P(("xh", "core", "z", "xl", "y"), None)
    in_specs = (rows, P(("z", "xl", "y"), ("xh", "core")))
    return jax.shard_map(shards, mesh=fine, in_specs=in_specs, out_specs=rows, check_vma=False)
```

time: 1280 us -> 107 us (0.08)
  the two profiles are of different devices: /device:TPU:4 before, /device:TPU:6 now
where the time goes in v2:
time: 107 us; the launch traced here: 106 us
  starting transfers between devices  34.3 us (32%)
  blocking collectives  29.7 us (28%)
  waiting for transfers between devices  29 us (27%)
  local copies, waits for them, and re-layouts  6.88 us (6%)
  Pallas kernels  6.05 us (6%)
    all_to_all x1, blocking collectives, shards(): lax.all_to_all(partial, ('z', 'y'), split_axis=0, concat_axis=0, tiled=True)  29.7 us
    all_to_all x1, waiting for transfers between devices, shards(): lax.all_to_all(amplitudes, ('z', 'core', 'y'), split_axis=1, concat_axis=...  16 us
    all_to_all x1, starting transfers between devices, shards(): lax.all_to_all(amplitudes, ('z', 'core', 'y'), split_axis=1, concat_axis=...  14.4 us
    ppermute x1, waiting for transfers between devices, shards(): left = lax.ppermute(integrals, RING, RIGHT)  8.47 us
    ppermute x1, starting transfers between devices, shards(): left = lax.ppermute(integrals, RING, RIGHT)  7.75 us
    ppermute x1, starting transfers between devices, shards(): far_low = lax.ppermute(far_from[1], RING, LEFT)  3.47 us
    all_to_all x1, local copies, waits for them, and re-layouts, shards(): lax.all_to_all(amplitudes, ('z', 'core', 'y'), split_axis=1, concat_axis=...  3.29 us
    ppermute x1, waiting for transfers between devices, shards(): right = lax.ppermute(integrals, RING, LEFT)  3.14 us
  transfers between devices with their start and end apart: 7, of which 4 were waited for; matrix products, arithmetic and copies ran while one was open for 0% of the time, Pallas kernels for 3%

profile of v2, /device:TPU:6, one launch (start us, length us, event | category | flops | bytes accessed | tf_op | source)
XLA Modules:
  0.0 106.2 jit_solution(5551681880196837274)
XLA Ops:
  0.0 7.8 %collective-permute-start = (bf16[2560,256]{1,0:T(8,128)(2,1)}, bf16[2560,256]{1,0:T(8,128)(2,1)S(1)}, u32[]{:S(2)}, u32[]{:S(2)}) collective-permute-start(bf16[2560,256]{1,0:T(8,128)(2,1)} %here.3), channel_id=1, source_target_pairs={{0,8},{8,256},{256,264},{264,0},{1,9},{9,257},{257,265},{265,1},{2... | collective-permute-start | bytes 3932168 | tf_op jit(solution)/shard_map/ppermute | solution.py:99
  7.8 1.9 %collective-permute-start.1 = (bf16[2560,256]{1,0:T(8,128)(2,1)}, bf16[2560,256]{1,0:T(8,128)(2,1)S(1)}, u32[]{:S(2)}, u32[]{:S(2)}) collective-permute-start(bf16[2560,256]{1,0:T(8,128)(2,1)} %here.3), channel_id=1, source_target_pairs={{0,264},{8,0},{256,8},{264,256},{1,265},{9,1},{257,9},{265,257},{2... | collective-permute-start | bytes 3932168 | tf_op jit(solution)/shard_map/ppermute | solution.py:100
  9.7 14.4 %all-to-all-start = ((bf16[2,128,2560]{2,0,1:T(2,128)(2,1)}), bf16[2,128,2560]{2,0,1:T(2,128)(2,1)}, u32[]{:S(2)}, u32[]{:S(2)}) async-start(bf16[2,128,2560]{2,0,1:T(2,128)(2,1)} %bitcast.7), calls=%async_computation | async-start | bytes 2621440 | tf_op jit(solution)/shard_map/all_to_all | solution.py:105
  24.1 8.5 %collective-permute-done.left = bf16[2560,256]{1,0:T(8,128)(2,1)S(1)} collective-permute-done((bf16[2560,256]{1,0:T(8,128)(2,1)}, bf16[2560,256]{1,0:T(8,128)(2,1)S(1)}, u32[]{:S(2)}, u32[]{:S(2)}) %collective-permute-start) | collective-permute-done | bytes 1310752 | tf_op jit(solution)/shard_map/ppermute | solution.py:99
  32.6 3.1 %collective-permute-done.1.right = bf16[2560,256]{1,0:T(8,128)(2,1)S(1)} collective-permute-done((bf16[2560,256]{1,0:T(8,128)(2,1)}, bf16[2560,256]{1,0:T(8,128)(2,1)S(1)}, u32[]{:S(2)}, u32[]{:S(2)}) %collective-permute-start.1) | collective-permute-done | bytes 1310752 | tf_op jit(solution)/shard_map/ppermute | solution.py:100
  35.8 1.1 %shard_map.28 = (bf16[1280,256]{1,0:T(8,128)(2,1)}, bf16[1280,256]{1,0:T(8,128)(2,1)}) custom-call(bf16[2560,256]{1,0:T(8,128)(2,1)S(1)} %collective-permute-done.left, bf16[2560,256]{1,0:T(8,128)(2,1)S(1)} %collective-permute-done.1.right), custom_call_target="tpu_custom_call" | custom-call | flops 40000000000 | bytes 2097152 | tf_op jit(solution)/shard_map/pallas_call | solution.py:81
  36.9 0.3 copy-done.3
  37.2 2.4 %collective-permute-start.2 = (bf16[1280,256]{1,0:T(8,128)(2,1)}, bf16[1280,256]{1,0:T(8,128)(2,1)S(1)}, u32[]{:S(2)}, u32[]{:S(2)}) collective-permute-start(bf16[1280,256]{1,0:T(8,128)(2,1)} %get-tuple-element.10), channel_id=1, source_target_pairs={{0,8},{8,256},{256,264},{264,0},{1,9},{9,257},{257,265},{265,1},{2... | collective-permute-start | bytes 1966088 | tf_op jit(solution)/shard_map/ppermute | solution.py:102
  39.6 3.5 %collective-permute-start.3 = (bf16[1280,256]{1,0:T(8,128)(2,1)}, bf16[1280,256]{1,0:T(8,128)(2,1)}, u32[]{:S(2)}, u32[]{:S(2)}) collective-permute-start(bf16[1280,256]{1,0:T(8,128)(2,1)} %get-tuple-element.11), channel_id=1, source_target_pairs={{0,264},{8,0},{256,8},{264,256},{1,265},{9,1},{257,9},{265,257},{2... | collective-permute-start | bytes 1966088 | tf_op jit(solution)/shard_map/ppermute | solution.py:103
  43.1 16.0 %all-to-all-done = bf16[2,128,2560]{2,0,1:T(2,128)(2,1)} async-done(((bf16[2,128,2560]{2,0,1:T(2,128)(2,1)}), bf16[2,128,2560]{2,0,1:T(2,128)(2,1)}, u32[]{:S(2)}, u32[]{:S(2)}) %all-to-all-start) | async-done | bytes 1310752 | tf_op jit(solution)/shard_map/all_to_all | solution.py:105
  59.1 3.3 %all_to_all.20.rows_ref = bf16[256,2560]{1,0:T(8,128)(2,1)S(1)} reshape(bf16[128,2,2560]{2,1,0:T(2,128)(2,1)} %bitcast.1) | data formatting | bytes 2621440 | tf_op jit(solution)/shard_map/all_to_all | solution.py:105
  62.4 2.3 %collective-permute-start.4 = (bf16[256,2560]{1,0:T(8,128)(2,1)S(1)}, bf16[256,2560]{1,0:T(8,128)(2,1)S(1)}, u32[]{:S(2)}, u32[]{:S(2)}) collective-permute-start(bf16[256,2560]{1,0:T(8,128)(2,1)S(1)} %all_to_all.20.rows_ref), channel_id=1, source_target_pairs={{0,128},{128,0},{1,129},{129,1},{2,130},{130,2},{3,131},{131,3},{4... | collective-permute-start | bytes 3932168 | tf_op jit(solution)/shard_map/ppermute | solution.py:107
  64.7 0.0 collective-permute-done.2.far_top
  64.7 0.0 collective-permute-done.3.far_low
  64.8 1.3 %copy-done.2 = bf16[2560,256]{1,0:T(8,128)(2,1)S(1)} copy-done((bf16[2560,256]{1,0:T(8,128)(2,1)S(1)}, bf16[2560,256]{1,0:T(8,128)(2,1)}, u32[]{:S(2)}) %copy-start.2) | copy-done | bytes 1310744
  66.1 1.3 %copy-done.4 = bf16[2560,256]{1,0:T(8,128)(2,1)S(1)} copy-done((bf16[2560,256]{1,0:T(8,128)(2,1)S(1)}, bf16[2560,256]{1,0:T(8,128)(2,1)}, u32[]{:S(2)}) %copy-start.4) | copy-done | bytes 1310744
  67.4 1.8 %shard_map.29.sum_ref = f32[256,512]{1,0:T(8,128)S(1)} custom-call(bf16[256,2560]{1,0:T(8,128)(2,1)S(1)} %all_to_all.20.rows_ref, bf16[2560,256]{1,0:T(8,128)(2,1)S(1)} %copy-done, bf16[2560,256]{1,0:T(8,128)(2,1)S(1)} %copy-done.2, bf16[2560,256]{1,0:T(8,128)(2,1)S(1)} %copy-done.4, bf16[1280,256]{1,0:T(8,128)(2,1)S(1)} %collective-permute-done.2.far_top, ...), custom_call_target="tpu_custom_call" | custom-call | flops 40000000000 | bytes 4194304 | tf_op jit(solution)/shard_map/pallas_call | solution.py:108
  69.2 0.0 collective-permute-done.4.rows_ref
  69.3 3.1 %shard_map.30 = (f32[512,128]{1,0:T(8,128)S(1)}, f32[512,128]{1,0:T(8,128)S(1)}) custom-call(f32[256,512]{1,0:T(8,128)S(1)} %shard_map.29.sum_ref, bf16[256,2560]{1,0:T(8,128)(2,1)S(1)} %collective-permute-done.4.rows_ref, bf16[2560,256]{1,0:T(8,128)(2,1)S(1)} %copy-done, bf16[2560,256]{1,0:T(8,128)(2,1)S(1)} %copy-done.2, bf16[2560,256]{1,0:T(8,128)(2,1)S(1)} %copy-done.4, ...), custom_call_target="tpu_custom_call" | custom-call | flops 40000000000 | bytes 4194304 | tf_op jit(solution)/shard_map/pallas_call | solution.py:109
  72.3 2.0 %collective-permute-start.5 = (f32[512,128]{1,0:T(8,128)S(1)}, f32[512,128]{1,0:T(8,128)S(1)}, u32[]{:S(2)}, u32[]{:S(2)}) collective-permute-start(f32[512,128]{1,0:T(8,128)S(1)} %get-tuple-element.14), channel_id=1, source_target_pairs={{0,128},{128,0},{1,129},{129,1},{2,130},{130,2},{3,131},{131,3},{4... | collective-permute-start | bytes 786440 | tf_op jit(solution)/shard_map/ppermute | solution.py:110
  74.4 1.4 %collective-permute-done.5 = f32[512,128]{1,0:T(8,128)S(1)} collective-permute-done((f32[512,128]{1,0:T(8,128)S(1)}, f32[512,128]{1,0:T(8,128)S(1)}, u32[]{:S(2)}, u32[]{:S(2)}) %collective-permute-start.5) | collective-permute-done | bytes 262176 | tf_op jit(solution)/shard_map/ppermute | solution.py:110
  75.8 29.7 %all_to_all.24 = f32[64,16,128]{2,1,0:T(8,128)S(1)} all-to-all(f32[64,16,128]{2,1,0:T(8,128)S(1)} %pad_maximum_fusion), channel_id=1, replica_groups=mesh['xh'=2,'core'=2,'z'=8,'xl'=2,'y'=8] {'z','y'}, dimensions={0} | all-to-all | bytes 1048576 | tf_op jit(solution)/shard_map/all_to_all | solution.py:114
  105.5 0.1 reduce_sum.9
  105.6 0.6 reshape.16
  (12 shorter events, 0.1 us)
Async XLA Ops:
  0.0 32.6 %collective-permute-start = (bf16[2560,256]{1,0:T(8,128)(2,1)}, bf16[2560,256]{1,0:T(8,128)(2,1)S(1)}, u32[]{:S(2)}, u32[]{:S(2)}) collective-permute-start(bf16[2560,256]{1,0:T(8,128)(2,1)} %here.3), channel_id=1, source_target_pairs={{0,8},{8,256},{256,264},{264,0},{1,9},{9,257},{257,265},{265,1},{2... | collective-permute-start | bytes 3932168 | tf_op jit(solution)/shard_map/ppermute | solution.py:99
  7.8 28.0 %collective-permute-start.1 = (bf16[2560,256]{1,0:T(8,128)(2,1)}, bf16[2560,256]{1,0:T(8,128)(2,1)S(1)}, u32[]{:S(2)}, u32[]{:S(2)}) collective-permute-start(bf16[2560,256]{1,0:T(8,128)(2,1)} %here.3), channel_id=1, source_target_pairs={{0,264},{8,0},{256,8},{264,256},{1,265},{9,1},{257,9},{265,257},{2... | collective-permute-start | bytes 3932168 | tf_op jit(solution)/shard_map/ppermute | solution.py:100
  9.7 49.4 %all-to-all-start = ((bf16[2,128,2560]{2,0,1:T(2,128)(2,1)}), bf16[2,128,2560]{2,0,1:T(2,128)(2,1)}, u32[]{:S(2)}, u32[]{:S(2)}) async-start(bf16[2,128,2560]{2,0,1:T(2,128)(2,1)} %bitcast.7), calls=%async_computation | async-start | bytes 2621440 | tf_op jit(solution)/shard_map/all_to_all | solution.py:105
  32.6 4.3 %copy-start.1 = (bf16[2560,256]{1,0:T(8,128)(2,1)}, bf16[2560,256]{1,0:T(8,128)(2,1)S(1)}, u32[]{:S(2)}) copy-start(bf16[2560,256]{1,0:T(8,128)(2,1)S(1)} %collective-permute-done.left) | copy-start | bytes 3932164
  35.8 1.5 %copy-start.3 = (bf16[2560,256]{1,0:T(8,128)(2,1)}, bf16[2560,256]{1,0:T(8,128)(2,1)S(1)}, u32[]{:S(2)}) copy-start(bf16[2560,256]{1,0:T(8,128)(2,1)S(1)} %collective-permute-done.1.right) | copy-start | bytes 3932164
  37.2 27.5 %collective-permute-start.2 = (bf16[1280,256]{1,0:T(8,128)(2,1)}, bf16[1280,256]{1,0:T(8,128)(2,1)S(1)}, u32[]{:S(2)}, u32[]{:S(2)}) collective-permute-start(bf16[1280,256]{1,0:T(8,128)(2,1)} %get-tuple-element.10), channel_id=1, source_target_pairs={{0,8},{8,256},{256,264},{264,0},{1,9},{9,257},{257,265},{265,1},{2... | collective-permute-start | bytes 1966088 | tf_op jit(solution)/shard_map/ppermute | solution.py:102
  39.6 25.1 %collective-permute-start.3 = (bf16[1280,256]{1,0:T(8,128)(2,1)}, bf16[1280,256]{1,0:T(8,128)(2,1)}, u32[]{:S(2)}, u32[]{:S(2)}) collective-permute-start(bf16[1280,256]{1,0:T(8,128)(2,1)} %get-tuple-element.11), channel_id=1, source_target_pairs={{0,264},{8,0},{256,8},{264,256},{1,265},{9,1},{257,9},{265,257},{2... | collective-permute-start | bytes 1966088 | tf_op jit(solution)/shard_map/ppermute | solution.py:103
  59.1 5.6 %copy-start = (bf16[2560,256]{1,0:T(8,128)(2,1)S(1)}, bf16[2560,256]{1,0:T(8,128)(2,1)}, u32[]{:S(2)}) copy-start(bf16[2560,256]{1,0:T(8,128)(2,1)} %here.3) | copy-start | bytes 3932164
  62.4 6.8 %collective-permute-start.4 = (bf16[256,2560]{1,0:T(8,128)(2,1)S(1)}, bf16[256,2560]{1,0:T(8,128)(2,1)S(1)}, u32[]{:S(2)}, u32[]{:S(2)}) collective-permute-start(bf16[256,2560]{1,0:T(8,128)(2,1)S(1)} %all_to_all.20.rows_ref), channel_id=1, source_target_pairs={{0,128},{128,0},{1,129},{129,1},{2,130},{130,2},{3,131},{131,3},{4... | collective-permute-start | bytes 3932168 | tf_op jit(solution)/shard_map/ppermute | solution.py:107
  64.8 1.3 %copy-start.2 = (bf16[2560,256]{1,0:T(8,128)(2,1)S(1)}, bf16[2560,256]{1,0:T(8,128)(2,1)}, u32[]{:S(2)}) copy-start(bf16[2560,256]{1,0:T(8,128)(2,1)} %copy-done.1) | copy-start | bytes 3932164
  66.1 1.3 %copy-start.4 = (bf16[2560,256]{1,0:T(8,128)(2,1)S(1)}, bf16[2560,256]{1,0:T(8,128)(2,1)}, u32[]{:S(2)}) copy-start(bf16[2560,256]{1,0:T(8,128)(2,1)} %copy-done.3) | copy-start | bytes 3932164
  72.3 3.4 %collective-permute-start.5 = (f32[512,128]{1,0:T(8,128)S(1)}, f32[512,128]{1,0:T(8,128)S(1)}, u32[]{:S(2)}, u32[]{:S(2)}) collective-permute-start(f32[512,128]{1,0:T(8,128)S(1)} %get-tuple-element.14), channel_id=1, source_target_pairs={{0,128},{128,0},{1,129},{129,1},{2,130},{130,2},{3,131},{131,3},{4... | collective-permute-start | bytes 786440 | tf_op jit(solution)/shard_map/ppermute | solution.py:110

commit v3 on v0

v3 whole, which is shorter than its diff:
```python
import jax
import jax.numpy as jnp
from jax import lax
from jax.experimental import pallas as pl
from jax.experimental.pallas import tpu as pltpu
from jax.sharding import Mesh, PartitionSpec as P

RING = ("xh", "xl")
RIGHT = [(i, (i + 1) % 4) for i in range(4)]
LEFT = [(i, (i + 3) % 4) for i in range(4)]
SWAP = [(0, 1), (1, 0)]
VMEM = pl.BlockSpec(memory_space=pltpu.VMEM)
LIMIT = 20 * 2**20
H_LIMIT = 8 * 2**20
G_FLOPS = 2 * 10**10
FLOPS = 10**11


def keep(first, second, first_ref, second_ref):
    first_ref[...] = first[...]
    second_ref[...] = second[...]


def kept(first, second):
    return pl.pallas_call(
        keep,
        out_shape=[jax.ShapeDtypeStruct(first.shape, first.dtype)] * 2,
        in_specs=[VMEM, VMEM],
        out_specs=[VMEM, VMEM],
        compiler_params=pltpu.CompilerParams(vmem_limit_bytes=H_LIMIT),
        cost_estimate=pl.CostEstimate(flops=G_FLOPS, bytes_accessed=2**21, transcendentals=0),
    )(first, second)


def halves(blocks, top_ref, low_ref):
    top_ref[...] = blocks[:1280]
    low_ref[...] = blocks[1280:]


def halved(blocks):
    return pl.pallas_call(
        halves,
        out_shape=[jax.ShapeDtypeStruct((1280, 256), jnp.bfloat16)] * 2,
        in_specs=[VMEM],
        out_specs=[VMEM, VMEM],
        compiler_params=pltpu.CompilerParams(vmem_limit_bytes=H_LIMIT),
    )(blocks)


def multiply(across, rows, blocks, sum_ref):
    core, xh, xl = lax.axis_index("core"), lax.axis_index("xh"), lax.axis_index("xl")
    here, left, right, far = blocks[:2], blocks[2:4], blocks[4:6], blocks[6:]
    wanted = 1 - core if across else core

    def dot(halves):
        top = jnp.dot(rows[:, :1280], halves[0][...], preferred_element_type=jnp.float32)
        return top + jnp.dot(rows[:, 1280:], halves[1][...], preferred_element_type=jnp.float32)

    @pl.when(xl == wanted)
    def _():
        sum_ref[xh] = dot(here)
        sum_ref[1 - xh] = dot(far)

    @pl.when(xl != wanted)
    def _():
        sum_ref[lax.rem(xh + xl, 2)] = dot(right)
        sum_ref[lax.rem(xh + 1 - xl, 2)] = dot(left)


def first_half(pieces, *refs):
    *blocks, sum_ref, rows = refs
    rows[...] = pieces[...].reshape(256, 2560)
    multiply(False, rows, blocks, sum_ref)


def second_half(first_ref, pieces, *refs):
    *blocks, mine_ref, theirs_ref, rows, sum_ref = refs
    core = lax.axis_index("core")
    rows[...] = pieces[...].reshape(256, 2560)
    multiply(True, rows, blocks, sum_ref)
    for xh in range(2):
        total = (first_ref[xh] + sum_ref[xh]).reshape(8, 2, 16, 256)
        first, second = total[:, 0].reshape(128, 256), total[:, 1].reshape(128, 256)
        mine = jnp.where(core == 0, first, second)
        theirs = jnp.where(core == 0, second, first)
        for half in range(2):
            place = pl.ds(2 * xh + half, 128, stride=4)
            mine_ref[place, :] = mine[:, 128 * half : 128 * half + 128]
            theirs_ref[place, :] = theirs[:, 128 * half : 128 * half + 128]


def first_sums(pieces, *blocks):
    return pl.pallas_call(
        first_half,
        out_shape=jax.ShapeDtypeStruct((2, 256, 256), jnp.float32),
        in_specs=[VMEM] * 9,
        out_specs=VMEM,
        scratch_shapes=[pltpu.VMEM((256, 2560), jnp.bfloat16)],
        compiler_params=pltpu.CompilerParams(vmem_limit_bytes=LIMIT),
        cost_estimate=pl.CostEstimate(flops=FLOPS, bytes_accessed=2**22, transcendentals=0),
    )(pieces, *blocks)


def second_sums(first, pieces, *blocks):
    return pl.pallas_call(
        second_half,
        out_shape=[jax.ShapeDtypeStruct((512, 128), jnp.float32)] * 2,
        in_specs=[VMEM] * 10,
        out_specs=[VMEM] * 2,
        scratch_shapes=[pltpu.VMEM((256, 2560), jnp.bfloat16), pltpu.VMEM((2, 256, 256), jnp.float32)],
        compiler_params=pltpu.CompilerParams(vmem_limit_bytes=LIMIT),
        cost_estimate=pl.CostEstimate(flops=10**9, bytes_accessed=2**22, transcendentals=0),
    )(first, pieces, *blocks)


def shards(amplitudes, integrals):
    core = lax.axis_index("core")
    top, low = halved(integrals)
    left_top = lax.ppermute(top, RING, RIGHT)
    right_low = lax.ppermute(low, RING, LEFT)
    left_low = lax.ppermute(low, RING, RIGHT)
    right_top = lax.ppermute(top, RING, LEFT)
    left_top, right_low = kept(left_top, right_low)
    far_top = lax.ppermute(left_top, RING, RIGHT)
    far_low = lax.ppermute(right_low, RING, LEFT)
    raw = lax.all_to_all(amplitudes.reshape(2, 128, 2560), ("z", "core", "y"), split_axis=1, concat_axis=1, tiled=True)
    raw, _, _ = lax.optimization_barrier((raw, left_top, right_low))
    raw_other = lax.ppermute(raw, "core", SWAP)
    blocks = (top, low, left_top, left_low, right_top, right_low, far_top, far_low)
    first = first_sums(raw.transpose(1, 0, 2), *blocks)
    mine, theirs = second_sums(first, raw_other.transpose(1, 0, 2), *blocks)
    got = lax.ppermute(theirs, "core", SWAP)
    mine, got = mine.reshape(64, 8, 128), got.reshape(64, 8, 128)
    first, second = jnp.where(core == 0, mine, got), jnp.where(core == 0, got, mine)
    partial = jnp.concatenate([first, second], axis=1)
    parts = lax.all_to_all(partial, ("z", "y"), split_axis=0, concat_axis=0, tiled=True)
    total = 0.5 * jnp.sum(parts, axis=0)
    return total.reshape(2, 2, 2, 256).transpose(1, 2, 0, 3).reshape(2, 1024)


def solution(mesh):
    fine = Mesh(mesh.devices.reshape(2, 2, 8, 2, 8), ("xh", "core", "z", "xl", "y"))
    rows = P(("xh", "core", "z", "xl", "y"), None)
    in_specs = (rows, P(("z", "xl", "y"), ("xh", "core")))
    return jax.shard_map(shards, mesh=fine, in_specs=in_specs, out_specs=rows, check_vma=False)
```

time: 1280 us -> 105 us (0.08)
  the two profiles are of different devices: /device:TPU:4 before, /device:TPU:6 now
where the time goes in v3:
time: 105 us
  starting transfers between devices  40.5 us (39%)
  blocking collectives  31.9 us (30%)
  waiting for transfers between devices  21.7 us (21%)
  Pallas kernels  8.31 us (8%)
  local copies, waits for them, and re-layouts  1.95 us (2%)
    all_to_all x1, blocking collectives, shards(): lax.all_to_all(partial, ('z', 'y'), split_axis=0, concat_axis=0, tiled=True)  31.9 us
    all_to_all x1, waiting for transfers between devices, shards(): lax.all_to_all(amplitudes.reshape(2, 128, 2560), ('z', 'core', 'y'), spli...  20.3 us
    all_to_all x1, starting transfers between devices, shards(): lax.all_to_all(amplitudes.reshape(2, 128, 2560), ('z', 'core', 'y'), spli...  14 us
    ppermute x1, starting transfers between devices, shards(): left_top = lax.ppermute(top, RING, RIGHT)  7.76 us
    ppermute x1, starting transfers between devices, shards(): far_top = lax.ppermute(left_top, RING, RIGHT)  4.8 us
    ppermute x1, starting transfers between devices, shards(): left_low = lax.ppermute(low, RING, RIGHT)  3.6 us
    pallas_call x1, Pallas kernels, second_sums(): pl.pallas_call(second_half, out_shape=[jax.ShapeDtypeStruct((512, 128), j...  2.95 us
    pallas_call x1, Pallas kernels, first_sums(): pl.pallas_call(first_half, out_shape=jax.ShapeDtypeStruct((2, 256, 256),...  2.87 us
  transfers between devices with their start and end apart: 9, of which 2 were waited for; matrix products, arithmetic and copies ran while one was open for 0% of the time, Pallas kernels for 5%

profile of v3, /device:TPU:6, one launch (start us, length us, event | category | flops | bytes accessed | tf_op | source)
XLA Modules:
  0.0 104.7 jit_solution(15492912359880367600)
XLA Ops:
  0.0 1.3 %copy-done = bf16[2560,256]{1,0:T(8,128)(2,1)S(1)} copy-done((bf16[2560,256]{1,0:T(8,128)(2,1)S(1)}, bf16[2560,256]{1,0:T(8,128)(2,1)}, u32[]{:S(2)}) %copy-start) | copy-done | bytes 1310744
  1.3 0.1 shard_map.28
  1.4 7.8 %collective-permute-start = (bf16[1280,256]{1,0:T(8,128)(2,1)S(1)}, bf16[1280,256]{1,0:T(8,128)(2,1)}, u32[]{:S(2)}, u32[]{:S(2)}) collective-permute-start(bf16[1280,256]{1,0:T(8,128)(2,1)S(1)} %get-tuple-element.12.refs_0_), channel_id=1, source_target_pairs={{0,8},{8,256},{256,264},{264,0},{1,9},{9,257},{257,265},{265,1},{2... | collective-permute-start | bytes 1966088 | tf_op jit(solution)/shard_map/ppermute | solution.py:119
  9.2 1.9 %collective-permute-start.1 = (bf16[1280,256]{1,0:T(8,128)(2,1)S(1)}, bf16[1280,256]{1,0:T(8,128)(2,1)}, u32[]{:S(2)}, u32[]{:S(2)}) collective-permute-start(bf16[1280,256]{1,0:T(8,128)(2,1)S(1)} %get-tuple-element.13.refs_1_), channel_id=1, source_target_pairs={{0,264},{8,0},{256,8},{264,256},{1,265},{9,1},{257,9},{265,257},{2... | collective-permute-start | bytes 1966088 | tf_op jit(solution)/shard_map/ppermute | solution.py:120
  11.1 14.0 %all-to-all-start = ((bf16[2,128,2560]{2,0,1:T(2,128)(2,1)}), bf16[2,128,2560]{2,0,1:T(2,128)(2,1)S(1)}, u32[]{:S(2)}, u32[]{:S(2)}) async-start(bf16[2,128,2560]{2,0,1:T(2,128)(2,1)} %bitcast.10), calls=%async_computation | async-start | bytes 2621440 | tf_op jit(solution)/shard_map/all_to_all | solution.py:126
  25.1 3.6 %collective-permute-start.2 = (bf16[1280,256]{1,0:T(8,128)(2,1)S(1)}, bf16[1280,256]{1,0:T(8,128)(2,1)S(1)}, u32[]{:S(2)}, u32[]{:S(2)}) collective-permute-start(bf16[1280,256]{1,0:T(8,128)(2,1)S(1)} %get-tuple-element.13.refs_1_), channel_id=1, source_target_pairs={{0,8},{8,256},{256,264},{264,0},{1,9},{9,257},{257,265},{265,1},{2... | collective-permute-start | bytes 1966088 | tf_op jit(solution)/shard_map/ppermute | solution.py:121
  28.7 2.2 %collective-permute-start.3 = (bf16[1280,256]{1,0:T(8,128)(2,1)S(1)}, bf16[1280,256]{1,0:T(8,128)(2,1)}, u32[]{:S(2)}, u32[]{:S(2)}) collective-permute-start(bf16[1280,256]{1,0:T(8,128)(2,1)S(1)} %get-tuple-element.12.refs_0_), channel_id=1, source_target_pairs={{0,264},{8,0},{256,8},{264,256},{1,265},{9,1},{257,9},{265,257},{2... | collective-permute-start | bytes 1966088 | tf_op jit(solution)/shard_map/ppermute | solution.py:122
  31.0 0.0 collective-permute-done.first
  31.0 0.0 collective-permute-done.1.second
  31.0 2.4 %shard_map.29 = (bf16[1280,256]{1,0:T(8,128)(2,1)}, bf16[1280,256]{1,0:T(8,128)(2,1)}) custom-call(bf16[1280,256]{1,0:T(8,128)(2,1)} %collective-permute-done.first, bf16[1280,256]{1,0:T(8,128)(2,1)} %collective-permute-done.1.second), custom_call_target="tpu_custom_call" | custom-call | flops 20000000000 | bytes 2097152 | tf_op jit(solution)/shard_map/pallas_call | solution.py:25
  33.4 4.8 %collective-permute-start.4 = (bf16[1280,256]{1,0:T(8,128)(2,1)}, bf16[1280,256]{1,0:T(8,128)(2,1)}, u32[]{:S(2)}, u32[]{:S(2)}) collective-permute-start(bf16[1280,256]{1,0:T(8,128)(2,1)} %get-tuple-element.14.refs_2_), channel_id=1, source_target_pairs={{0,8},{8,256},{256,264},{264,0},{1,9},{9,257},{257,265},{265,1},{2... | collective-permute-start | bytes 1966088 | tf_op jit(solution)/shard_map/ppermute | solution.py:124
  38.2 1.9 %collective-permute-start.5 = (bf16[1280,256]{1,0:T(8,128)(2,1)}, bf16[1280,256]{1,0:T(8,128)(2,1)}, u32[]{:S(2)}, u32[]{:S(2)}) collective-permute-start(bf16[1280,256]{1,0:T(8,128)(2,1)} %get-tuple-element.15.refs_5_), channel_id=1, source_target_pairs={{0,264},{8,0},{256,8},{264,256},{1,265},{9,1},{257,9},{265,257},{2... | collective-permute-start | bytes 1966088 | tf_op jit(solution)/shard_map/ppermute | solution.py:125
  40.1 20.3 %all-to-all-done = bf16[2,128,2560]{2,0,1:T(2,128)(2,1)S(1)} async-done(((bf16[2,128,2560]{2,0,1:T(2,128)(2,1)}), bf16[2,128,2560]{2,0,1:T(2,128)(2,1)S(1)}, u32[]{:S(2)}, u32[]{:S(2)}) %all-to-all-start) | async-done | bytes 1310752 | tf_op jit(solution)/shard_map/all_to_all | solution.py:126
  60.4 2.3 %collective-permute-start.6 = (bf16[2,128,2560]{2,0,1:T(2,128)(2,1)S(1)}, bf16[2,128,2560]{2,0,1:T(2,128)(2,1)S(1)}, u32[]{:S(2)}, u32[]{:S(2)}) collective-permute-start(bf16[2,128,2560]{2,0,1:T(2,128)(2,1)S(1)} %all-to-all-done), channel_id=1, source_target_pairs={{0,128},{128,0},{1,129},{129,1},{2,130},{130,2},{3,131},{131,3},{4... | collective-permute-start | bytes 3932168 | tf_op jit(solution)/shard_map/ppermute | solution.py:128
  62.7 0.0 collective-permute-done.2.refs_3_
  62.8 0.0 collective-permute-done.4.refs_6_
  62.8 0.0 collective-permute-done.5.refs_7_
  62.8 2.9 %shard_map.30.first_ref = f32[2,256,256]{2,1,0:T(8,128)S(1)} custom-call(bf16[128,2,2560]{2,1,0:T(2,128)(2,1)S(1)} %bitcast.9, bf16[1280,256]{1,0:T(8,128)(2,1)S(1)} %get-tuple-element.12.refs_0_, bf16[1280,256]{1,0:T(8,128)(2,1)S(1)} %get-tuple-element.13.refs_1_, bf16[1280,256]{1,0:T(8,128)(2,1)} %get-tuple-element.14.refs_2_, ...), custom_call_target="tpu_custom_call" | custom-call | flops 99999997952 | bytes 4194304 | tf_op jit(solution)/shard_map/pallas_call | solution.py:93
  65.7 2.9 %shard_map.31 = (f32[512,128]{1,0:T(8,128)S(1)}, f32[512,128]{1,0:T(8,128)S(1)}) custom-call(f32[2,256,256]{2,1,0:T(8,128)S(1)} %shard_map.30.first_ref, bf16[128,2,2560]{2,1,0:T(2,128)(2,1)S(1)} %bitcast.8, bf16[1280,256]{1,0:T(8,128)(2,1)S(1)} %get-tuple-element.12.refs_0_, bf16[1280,256]{1,0:T(8,128)(2,1)S(1)} %get-tuple-element.13.refs_1_, ...), custom_call_target="tpu_custom_call" | custom-call | flops 1000000000 | bytes 4194304 | tf_op jit(solution)/shard_map/pallas_call | solution.py:105
  68.6 2.0 %collective-permute-start.7 = (f32[512,128]{1,0:T(8,128)S(1)}, f32[512,128]{1,0:T(8,128)S(1)}, u32[]{:S(2)}, u32[]{:S(2)}) collective-permute-start(f32[512,128]{1,0:T(8,128)S(1)} %get-tuple-element.18), channel_id=1, source_target_pairs={{0,128},{128,0},{1,129},{129,1},{2,130},{130,2},{3,131},{131,3},{4... | collective-permute-start | bytes 786440 | tf_op jit(solution)/shard_map/ppermute | solution.py:132
  70.6 1.4 %collective-permute-done.7 = f32[512,128]{1,0:T(8,128)S(1)} collective-permute-done((f32[512,128]{1,0:T(8,128)S(1)}, f32[512,128]{1,0:T(8,128)S(1)}, u32[]{:S(2)}, u32[]{:S(2)}) %collective-permute-start.7) | collective-permute-done | bytes 262176 | tf_op jit(solution)/shard_map/ppermute | solution.py:132
  72.1 31.9 %all_to_all.10 = f32[64,16,128]{2,1,0:T(8,128)S(1)} all-to-all(f32[64,16,128]{2,1,0:T(8,128)S(1)} %pad_maximum_fusion), channel_id=1, replica_groups=mesh['xh'=2,'core'=2,'z'=8,'xl'=2,'y'=8] {'z','y'}, dimensions={0} | all-to-all | bytes 1048576 | tf_op jit(solution)/shard_map/all_to_all | solution.py:136
  104.0 0.1 reduce_sum.9
  104.1 0.6 reshape.17
  (8 shorter events, 0.1 us)
Async XLA Ops:
  0.0 1.3 %copy-start = (bf16[2560,256]{1,0:T(8,128)(2,1)S(1)}, bf16[2560,256]{1,0:T(8,128)(2,1)}, u32[]{:S(2)}) copy-start(bf16[2560,256]{1,0:T(8,128)(2,1)} %blocks.1) | copy-start | bytes 3932164
  1.4 29.6 %collective-permute-start = (bf16[1280,256]{1,0:T(8,128)(2,1)S(1)}, bf16[1280,256]{1,0:T(8,128)(2,1)}, u32[]{:S(2)}, u32[]{:S(2)}) collective-permute-start(bf16[1280,256]{1,0:T(8,128)(2,1)S(1)} %get-tuple-element.12.refs_0_), channel_id=1, source_target_pairs={{0,8},{8,256},{256,264},{264,0},{1,9},{9,257},{257,265},{265,1},{2... | collective-permute-start | bytes 1966088 | tf_op jit(solution)/shard_map/ppermute | solution.py:119
  9.2 21.8 %collective-permute-start.1 = (bf16[1280,256]{1,0:T(8,128)(2,1)S(1)}, bf16[1280,256]{1,0:T(8,128)(2,1)}, u32[]{:S(2)}, u32[]{:S(2)}) collective-permute-start(bf16[1280,256]{1,0:T(8,128)(2,1)S(1)} %get-tuple-element.13.refs_1_), channel_id=1, source_target_pairs={{0,264},{8,0},{256,8},{264,256},{1,265},{9,1},{257,9},{265,257},{2... | collective-permute-start | bytes 1966088 | tf_op jit(solution)/shard_map/ppermute | solution.py:120
  11.1 49.3 %all-to-all-start = ((bf16[2,128,2560]{2,0,1:T(2,128)(2,1)}), bf16[2,128,2560]{2,0,1:T(2,128)(2,1)S(1)}, u32[]{:S(2)}, u32[]{:S(2)}) async-start(bf16[2,128,2560]{2,0,1:T(2,128)(2,1)} %bitcast.10), calls=%async_computation | async-start | bytes 2621440 | tf_op jit(solution)/shard_map/all_to_all | solution.py:126
  25.1 37.6 %collective-permute-start.2 = (bf16[1280,256]{1,0:T(8,128)(2,1)S(1)}, bf16[1280,256]{1,0:T(8,128)(2,1)S(1)}, u32[]{:S(2)}, u32[]{:S(2)}) collective-permute-start(bf16[1280,256]{1,0:T(8,128)(2,1)S(1)} %get-tuple-element.13.refs_1_), channel_id=1, source_target_pairs={{0,8},{8,256},{256,264},{264,0},{1,9},{9,257},{257,265},{265,1},{2... | collective-permute-start | bytes 1966088 | tf_op jit(solution)/shard_map/ppermute | solution.py:121
  28.7 34.0 %collective-permute-start.3 = (bf16[1280,256]{1,0:T(8,128)(2,1)S(1)}, bf16[1280,256]{1,0:T(8,128)(2,1)}, u32[]{:S(2)}, u32[]{:S(2)}) collective-permute-start(bf16[1280,256]{1,0:T(8,128)(2,1)S(1)} %get-tuple-element.12.refs_0_), channel_id=1, source_target_pairs={{0,264},{8,0},{256,8},{264,256},{1,265},{9,1},{257,9},{265,257},{2... | collective-permute-start | bytes 1966088 | tf_op jit(solution)/shard_map/ppermute | solution.py:122
  33.4 29.4 %collective-permute-start.4 = (bf16[1280,256]{1,0:T(8,128)(2,1)}, bf16[1280,256]{1,0:T(8,128)(2,1)}, u32[]{:S(2)}, u32[]{:S(2)}) collective-permute-start(bf16[1280,256]{1,0:T(8,128)(2,1)} %get-tuple-element.14.refs_2_), channel_id=1, source_target_pairs={{0,8},{8,256},{256,264},{264,0},{1,9},{9,257},{257,265},{265,1},{2... | collective-permute-start | bytes 1966088 | tf_op jit(solution)/shard_map/ppermute | solution.py:124
  38.2 24.6 %collective-permute-start.5 = (bf16[1280,256]{1,0:T(8,128)(2,1)}, bf16[1280,256]{1,0:T(8,128)(2,1)}, u32[]{:S(2)}, u32[]{:S(2)}) collective-permute-start(bf16[1280,256]{1,0:T(8,128)(2,1)} %get-tuple-element.15.refs_5_), channel_id=1, source_target_pairs={{0,264},{8,0},{256,8},{264,256},{1,265},{9,1},{257,9},{265,257},{2... | collective-permute-start | bytes 1966088 | tf_op jit(solution)/shard_map/ppermute | solution.py:125
  60.4 5.2 %collective-permute-start.6 = (bf16[2,128,2560]{2,0,1:T(2,128)(2,1)S(1)}, bf16[2,128,2560]{2,0,1:T(2,128)(2,1)S(1)}, u32[]{:S(2)}, u32[]{:S(2)}) collective-permute-start(bf16[2,128,2560]{2,0,1:T(2,128)(2,1)S(1)} %all-to-all-done), channel_id=1, source_target_pairs={{0,128},{128,0},{1,129},{129,1},{2,130},{130,2},{3,131},{131,3},{4... | collective-permute-start | bytes 3932168 | tf_op jit(solution)/shard_map/ppermute | solution.py:128
  68.6 3.4 %collective-permute-start.7 = (f32[512,128]{1,0:T(8,128)S(1)}, f32[512,128]{1,0:T(8,128)S(1)}, u32[]{:S(2)}, u32[]{:S(2)}) collective-permute-start(f32[512,128]{1,0:T(8,128)S(1)} %get-tuple-element.18), channel_id=1, source_target_pairs={{0,128},{128,0},{1,129},{129,1},{2,130},{130,2},{3,131},{131,3},{4... | collective-permute-start | bytes 786440 | tf_op jit(solution)/shard_map/ppermute | solution.py:132

commit v4 on v3

v4 whole, which is shorter than its diff:
```python
import jax
import jax.numpy as jnp
from jax import lax
from jax.experimental import pallas as pl
from jax.experimental.pallas import tpu as pltpu
from jax.sharding import Mesh, PartitionSpec as P

RING = ("xh", "xl")
RIGHT = [(i, (i + 1) % 4) for i in range(4)]
LEFT = [(i, (i + 3) % 4) for i in range(4)]
SWAP = [(0, 1), (1, 0)]
VMEM = pl.BlockSpec(memory_space=pltpu.VMEM)
LIMIT = 20 * 2**20
H_LIMIT = 8 * 2**20
SPLIT = 2048
G_FLOPS = 10**10
B_FLOPS = 10**10
FLOPS = 10**11


def keep(*refs):
    for source, target in zip(refs[: len(refs) // 2], refs[len(refs) // 2 :]):
        target[...] = source[...]


def kept(flops, *pieces):
    return pl.pallas_call(
        keep,
        out_shape=[jax.ShapeDtypeStruct(piece.shape, piece.dtype) for piece in pieces],
        in_specs=[VMEM] * len(pieces),
        out_specs=[VMEM] * len(pieces),
        compiler_params=pltpu.CompilerParams(vmem_limit_bytes=H_LIMIT),
        cost_estimate=pl.CostEstimate(flops=flops, bytes_accessed=2**21, transcendentals=0),
    )(*pieces)


def halves(blocks, top_ref, low_ref):
    top_ref[...] = blocks[:SPLIT]
    low_ref[...] = blocks[SPLIT:]


def halved(blocks):
    return pl.pallas_call(
        halves,
        out_shape=[jax.ShapeDtypeStruct((rows, 256), jnp.bfloat16) for rows in (SPLIT, 2560 - SPLIT)],
        in_specs=[VMEM],
        out_specs=[VMEM, VMEM],
        compiler_params=pltpu.CompilerParams(vmem_limit_bytes=H_LIMIT),
    )(blocks)


def multiply(across, rows, blocks, sum_ref):
    core, xh, xl = lax.axis_index("core"), lax.axis_index("xh"), lax.axis_index("xl")
    here, left, right, far = blocks[:2], blocks[2:4], blocks[4:6], blocks[6:]
    wanted = 1 - core if across else core

    def dot(halves):
        top = jnp.dot(rows[:, :SPLIT], halves[0][...], preferred_element_type=jnp.float32)
        return top + jnp.dot(rows[:, SPLIT:], halves[1][...], preferred_element_type=jnp.float32)

    @pl.when(xl == wanted)
    def _():
        sum_ref[xh] = dot(here)
        sum_ref[1 - xh] = dot(far)

    @pl.when(xl != wanted)
    def _():
        sum_ref[lax.rem(xh + xl, 2)] = dot(right)
        sum_ref[lax.rem(xh + 1 - xl, 2)] = dot(left)


def first_half(pieces, *refs):
    *blocks, sum_ref, rows = refs
    rows[...] = pieces[...].reshape(256, 2560)
    multiply(False, rows, blocks, sum_ref)


def second_half(first_ref, pieces, *refs):
    *blocks, out_ref, rows, sum_ref = refs
    rows[...] = pieces[...].reshape(256, 2560)
    multiply(True, rows, blocks, sum_ref)
    for xh in range(2):
        total = first_ref[xh] + sum_ref[xh]
        for half in range(2):
            out_ref[pl.ds(2 * xh + half, 256, stride=4), :] = total[:, 128 * half : 128 * half + 128]


def first_sums(pieces, *blocks):
    return pl.pallas_call(
        first_half,
        out_shape=jax.ShapeDtypeStruct((2, 256, 256), jnp.float32),
        in_specs=[VMEM] * 9,
        out_specs=VMEM,
        scratch_shapes=[pltpu.VMEM((256, 2560), jnp.bfloat16)],
        compiler_params=pltpu.CompilerParams(vmem_limit_bytes=LIMIT),
        cost_estimate=pl.CostEstimate(flops=FLOPS, bytes_accessed=2**22, transcendentals=0),
    )(pieces, *blocks)


def second_sums(first, pieces, *blocks):
    return pl.pallas_call(
        second_half,
        out_shape=jax.ShapeDtypeStruct((1024, 128), jnp.float32),
        in_specs=[VMEM] * 10,
        out_specs=VMEM,
        scratch_shapes=[pltpu.VMEM((256, 2560), jnp.bfloat16), pltpu.VMEM((2, 256, 256), jnp.float32)],
        compiler_params=pltpu.CompilerParams(vmem_limit_bytes=LIMIT),
        cost_estimate=pl.CostEstimate(flops=10**9, bytes_accessed=2**22, transcendentals=0),
    )(first, pieces, *blocks)


def shards(amplitudes, integrals):
    top, low = halved(integrals)
    left_top = lax.ppermute(top, RING, RIGHT)
    right_low = lax.ppermute(low, RING, LEFT)
    left_low = lax.ppermute(low, RING, RIGHT)
    right_top = lax.ppermute(top, RING, LEFT)
    (left_top,) = kept(G_FLOPS, left_top)
    (right_low,) = kept(B_FLOPS, right_low)
    far_top = lax.ppermute(left_top, RING, RIGHT)
    far_low = lax.ppermute(right_low, RING, LEFT)
    raw = lax.all_to_all(amplitudes.reshape(2, 128, 2560), ("z", "core", "y"), split_axis=1, concat_axis=1, tiled=True)
    raw, _, _ = lax.optimization_barrier((raw, left_top, right_low))
    raw_other = lax.ppermute(raw, "core", SWAP)
    blocks = (top, low, left_top, left_low, right_top, right_low, far_top, far_low)
    first = first_sums(raw.transpose(1, 0, 2), *blocks)
    partial = second_sums(first, raw_other.transpose(1, 0, 2), *blocks).reshape(128, 8, 128)
    parts = lax.all_to_all(partial, ("z", "core", "y"), split_axis=0, concat_axis=0, tiled=True)
    total = 0.5 * jnp.sum(parts.reshape(8, 2, 8, 8, 128), axis=(0, 2))
    return total.reshape(2, 2, 2, 256).transpose(1, 2, 0, 3).reshape(2, 1024)


def solution(mesh):
    fine = Mesh(mesh.devices.reshape(2, 2, 8, 2, 8), ("xh", "core", "z", "xl", "y"))
    rows = P(("xh", "core", "z", "xl", "y"), None)
    in_specs = (rows, P(("z", "xl", "y"), ("xh", "core")))
    return jax.shard_map(shards, mesh=fine, in_specs=in_specs, out_specs=rows, check_vma=False)
```

time: 105 us -> 106 us (level)
  the two profiles are of different devices: /device:TPU:6 before, /device:TPU:1 now
where the time goes in v4:
time: 106 us; the launch traced here: 105 us
  starting transfers between devices  38.9 us (37%)
  blocking collectives  34.7 us (33%)
  waiting for transfers between devices  19.9 us (19%)
  Pallas kernels  9.45 us (9%)
  local copies, waits for them, and re-layouts  1.95 us (2%)
    all_to_all x1, blocking collectives, shards(): lax.all_to_all(partial, ('z', 'core', 'y'), split_axis=0, concat_axis=0,...  34.7 us
    all_to_all x1, waiting for transfers between devices, shards(): lax.all_to_all(amplitudes.reshape(2, 128, 2560), ('z', 'core', 'y'), spli...  17.9 us
    all_to_all x1, starting transfers between devices, shards(): lax.all_to_all(amplitudes.reshape(2, 128, 2560), ('z', 'core', 'y'), spli...  17.9 us
    ppermute x1, starting transfers between devices, shards(): left_top = lax.ppermute(top, RING, RIGHT)  3.94 us
    ppermute x1, starting transfers between devices, shards(): right_low = lax.ppermute(low, RING, LEFT)  3.37 us
    ppermute x1, starting transfers between devices, shards(): far_low = lax.ppermute(right_low, RING, LEFT)  3.36 us
    ppermute x1, starting transfers between devices, shards(): left_low = lax.ppermute(low, RING, RIGHT)  3.12 us
    ppermute x1, starting transfers between devices, shards(): far_top = lax.ppermute(left_top, RING, RIGHT)  3.11 us
  transfers between devices with their start and end apart: 8, of which 2 were waited for; matrix products, arithmetic and copies ran while one was open for 0% of the time, Pallas kernels for 6%

profile of v4, /device:TPU:1, one launch (start us, length us, event | category | flops | bytes accessed | tf_op | source)
XLA Modules:
  0.0 105.1 jit_solution(11053378227400221458)
XLA Ops:
  0.0 1.3 %copy-done = bf16[2560,256]{1,0:T(8,128)(2,1)S(1)} copy-done((bf16[2560,256]{1,0:T(8,128)(2,1)S(1)}, bf16[2560,256]{1,0:T(8,128)(2,1)}, u32[]{:S(2)}) %copy-start) | copy-done | bytes 1310744
  1.3 0.8 shard_map.28
  2.1 3.9 %collective-permute-start = (bf16[2048,256]{1,0:T(8,128)(2,1)S(1)}, bf16[2048,256]{1,0:T(8,128)(2,1)}, u32[]{:S(2)}, u32[]{:S(2)}) collective-permute-start(bf16[2048,256]{1,0:T(8,128)(2,1)S(1)} %get-tuple-element.8.refs_0_), channel_id=1, source_target_pairs={{0,8},{8,256},{256,264},{264,0},{1,9},{9,257},{257,265},{265,1},{2... | collective-permute-start | bytes 3145736 | tf_op jit(solution)/shard_map/ppermute | solution.py:114
  6.1 17.9 %all-to-all-start = ((bf16[2,128,2560]{2,0,1:T(2,128)(2,1)}), bf16[2,128,2560]{2,0,1:T(2,128)(2,1)S(1)}, u32[]{:S(2)}, u32[]{:S(2)}) async-start(bf16[2,128,2560]{2,0,1:T(2,128)(2,1)} %bitcast.10), calls=%async_computation | async-start | bytes 2621440 | tf_op jit(solution)/shard_map/all_to_all | solution.py:122
  23.9 3.1 %collective-permute-start.2 = (bf16[512,256]{1,0:T(8,128)(2,1)}, bf16[512,256]{1,0:T(8,128)(2,1)}, u32[]{:S(2)}, u32[]{:S(2)}) collective-permute-start(bf16[512,256]{1,0:T(8,128)(2,1)} %get-tuple-element.9.refs_1_), channel_id=1, source_target_pairs={{0,8},{8,256},{256,264},{264,0},{1,9},{9,257},{257,265},{265,1},{2... | collective-permute-start | bytes 786440 | tf_op jit(solution)/shard_map/ppermute | solution.py:116
  27.1 3.4 %collective-permute-start.1 = (bf16[512,256]{1,0:T(8,128)(2,1)}, bf16[512,256]{1,0:T(8,128)(2,1)S(1)}, u32[]{:S(2)}, u32[]{:S(2)}) collective-permute-start(bf16[512,256]{1,0:T(8,128)(2,1)} %get-tuple-element.9.refs_1_), channel_id=1, source_target_pairs={{0,264},{8,0},{256,8},{264,256},{1,265},{9,1},{257,9},{265,257},{2... | collective-permute-start | bytes 786440 | tf_op jit(solution)/shard_map/ppermute | solution.py:115
  30.5 2.2 %collective-permute-start.3 = (bf16[2048,256]{1,0:T(8,128)(2,1)S(1)}, bf16[2048,256]{1,0:T(8,128)(2,1)S(1)}, u32[]{:S(2)}, u32[]{:S(2)}) collective-permute-start(bf16[2048,256]{1,0:T(8,128)(2,1)S(1)} %get-tuple-element.8.refs_0_), channel_id=1, source_target_pairs={{0,264},{8,0},{256,8},{264,256},{1,265},{9,1},{257,9},{265,257},{2... | collective-permute-start | bytes 3145736 | tf_op jit(solution)/shard_map/ppermute | solution.py:117
  32.6 0.0 collective-permute-done.refs_0_
  32.6 2.3 %shard_map.29.refs_2_ = bf16[2048,256]{1,0:T(8,128)(2,1)} custom-call(bf16[2048,256]{1,0:T(8,128)(2,1)} %collective-permute-done.refs_0_), custom_call_target="tpu_custom_call" | custom-call | flops 10000000000 | bytes 2097152 | tf_op jit(solution)/shard_map/pallas_call | solution.py:27
  34.9 3.1 %collective-permute-start.4 = (bf16[2048,256]{1,0:T(8,128)(2,1)}, bf16[2048,256]{1,0:T(8,128)(2,1)}, u32[]{:S(2)}, u32[]{:S(2)}) collective-permute-start(bf16[2048,256]{1,0:T(8,128)(2,1)} %shard_map.29.refs_2_), channel_id=1, source_target_pairs={{0,8},{8,256},{256,264},{264,0},{1,9},{9,257},{257,265},{265,1},{2... | collective-permute-start | bytes 3145736 | tf_op jit(solution)/shard_map/ppermute | solution.py:120
  38.0 0.0 collective-permute-done.1.refs_0_
  38.0 0.7 shard_map.30.refs_5_
  38.7 3.4 %collective-permute-start.5 = (bf16[512,256]{1,0:T(8,128)(2,1)}, bf16[512,256]{1,0:T(8,128)(2,1)}, u32[]{:S(2)}, u32[]{:S(2)}) collective-permute-start(bf16[512,256]{1,0:T(8,128)(2,1)} %shard_map.30.refs_5_), channel_id=1, source_target_pairs={{0,264},{8,0},{256,8},{264,256},{1,265},{9,1},{257,9},{265,257},{2... | collective-permute-start | bytes 786440 | tf_op jit(solution)/shard_map/ppermute | solution.py:121
  42.1 17.9 %all-to-all-done = bf16[2,128,2560]{2,0,1:T(2,128)(2,1)S(1)} async-done(((bf16[2,128,2560]{2,0,1:T(2,128)(2,1)}), bf16[2,128,2560]{2,0,1:T(2,128)(2,1)S(1)}, u32[]{:S(2)}, u32[]{:S(2)}) %all-to-all-start) | async-done | bytes 1310752 | tf_op jit(solution)/shard_map/all_to_all | solution.py:122
  60.1 2.0 %collective-permute-start.6 = (bf16[2,128,2560]{2,0,1:T(2,128)(2,1)S(1)}, bf16[2,128,2560]{2,0,1:T(2,128)(2,1)S(1)}, u32[]{:S(2)}, u32[]{:S(2)}) collective-permute-start(bf16[2,128,2560]{2,0,1:T(2,128)(2,1)S(1)} %all-to-all-done), channel_id=1, source_target_pairs={{0,128},{128,0},{1,129},{129,1},{2,130},{130,2},{3,131},{131,3},{4... | collective-permute-start | bytes 3932168 | tf_op jit(solution)/shard_map/ppermute | solution.py:124
  62.1 0.0 collective-permute-done.2.refs_3_
  62.1 1.9 %collective-permute-done.5.refs_7_ = bf16[512,256]{1,0:T(8,128)(2,1)} collective-permute-done((bf16[512,256]{1,0:T(8,128)(2,1)}, bf16[512,256]{1,0:T(8,128)(2,1)}, u32[]{:S(2)}, u32[]{:S(2)}) %collective-permute-start.5) | collective-permute-done | bytes 262176 | tf_op jit(solution)/shard_map/ppermute | solution.py:121
  64.0 0.0 collective-permute-done.3.refs_4_
  64.0 0.0 collective-permute-done.4.refs_6_
  64.0 2.8 %shard_map.31.first_ref = f32[2,256,256]{2,1,0:T(8,128)S(1)} custom-call(bf16[128,2,2560]{2,1,0:T(2,128)(2,1)S(1)} %bitcast.7, bf16[2048,256]{1,0:T(8,128)(2,1)S(1)} %get-tuple-element.8.refs_0_, bf16[512,256]{1,0:T(8,128)(2,1)} %get-tuple-element.9.refs_1_, bf16[2048,256]{1,0:T(8,128)(2,1)} %shard_map.29.refs_2_, ...), custom_call_target="tpu_custom_call" | custom-call | flops 99999997952 | bytes 4194304 | tf_op jit(solution)/shard_map/pallas_call | solution.py:89
  66.8 2.9 %shard_map.32 = f32[1024,128]{1,0:T(8,128)S(1)} custom-call(f32[2,256,256]{2,1,0:T(8,128)S(1)} %shard_map.31.first_ref, bf16[128,2,2560]{2,1,0:T(2,128)(2,1)S(1)} %bitcast.8, bf16[2048,256]{1,0:T(8,128)(2,1)S(1)} %get-tuple-element.8.refs_0_, bf16[512,256]{1,0:T(8,128)(2,1)} %get-tuple-element.9.refs_1_, bf16[2048,256]{1,0:T(8,128)(2,1)} %shard_map.29.refs_2_, ...), custom_call_target="tpu_custom_call" | custom-call | flops 1000000000 | bytes 4194304 | tf_op jit(solution)/shard_map/pallas_call | solution.py:101
  69.7 34.7 %all_to_all.10 = f32[128,8,128]{2,1,0:T(8,128)S(1)} all-to-all(f32[128,8,128]{2,1,0:T(8,128)S(1)} %bitcast.6), channel_id=1, replica_groups=mesh['xh'=2,'core'=2,'z'=8,'xl'=2,'y'=8] {'z','core','y'}, dimensions={0} | all-to-all | bytes 1048576 | tf_op jit(solution)/shard_map/all_to_all | solution.py:128
  104.4 0.1 reduce_sum.9
  104.5 0.6 reshape.19
  (5 shorter events, 0.0 us)
Async XLA Ops:
  0.0 1.3 %copy-start = (bf16[2560,256]{1,0:T(8,128)(2,1)S(1)}, bf16[2560,256]{1,0:T(8,128)(2,1)}, u32[]{:S(2)}) copy-start(bf16[2560,256]{1,0:T(8,128)(2,1)} %blocks.1) | copy-start | bytes 3932164
  2.1 30.5 %collective-permute-start = (bf16[2048,256]{1,0:T(8,128)(2,1)S(1)}, bf16[2048,256]{1,0:T(8,128)(2,1)}, u32[]{:S(2)}, u32[]{:S(2)}) collective-permute-start(bf16[2048,256]{1,0:T(8,128)(2,1)S(1)} %get-tuple-element.8.refs_0_), channel_id=1, source_target_pairs={{0,8},{8,256},{256,264},{264,0},{1,9},{9,257},{257,265},{265,1},{2... | collective-permute-start | bytes 3145736 | tf_op jit(solution)/shard_map/ppermute | solution.py:114
  6.1 54.0 %all-to-all-start = ((bf16[2,128,2560]{2,0,1:T(2,128)(2,1)}), bf16[2,128,2560]{2,0,1:T(2,128)(2,1)S(1)}, u32[]{:S(2)}, u32[]{:S(2)}) async-start(bf16[2,128,2560]{2,0,1:T(2,128)(2,1)} %bitcast.10), calls=%async_computation | async-start | bytes 2621440 | tf_op jit(solution)/shard_map/all_to_all | solution.py:122
  23.9 38.1 %collective-permute-start.2 = (bf16[512,256]{1,0:T(8,128)(2,1)}, bf16[512,256]{1,0:T(8,128)(2,1)}, u32[]{:S(2)}, u32[]{:S(2)}) collective-permute-start(bf16[512,256]{1,0:T(8,128)(2,1)} %get-tuple-element.9.refs_1_), channel_id=1, source_target_pairs={{0,8},{8,256},{256,264},{264,0},{1,9},{9,257},{257,265},{265,1},{2... | collective-permute-start | bytes 786440 | tf_op jit(solution)/shard_map/ppermute | solution.py:116
  27.1 10.9 %collective-permute-start.1 = (bf16[512,256]{1,0:T(8,128)(2,1)}, bf16[512,256]{1,0:T(8,128)(2,1)S(1)}, u32[]{:S(2)}, u32[]{:S(2)}) collective-permute-start(bf16[512,256]{1,0:T(8,128)(2,1)} %get-tuple-element.9.refs_1_), channel_id=1, source_target_pairs={{0,264},{8,0},{256,8},{264,256},{1,265},{9,1},{257,9},{265,257},{2... | collective-permute-start | bytes 786440 | tf_op jit(solution)/shard_map/ppermute | solution.py:115
  30.5 33.5 %collective-permute-start.3 = (bf16[2048,256]{1,0:T(8,128)(2,1)S(1)}, bf16[2048,256]{1,0:T(8,128)(2,1)S(1)}, u32[]{:S(2)}, u32[]{:S(2)}) collective-permute-start(bf16[2048,256]{1,0:T(8,128)(2,1)S(1)} %get-tuple-element.8.refs_0_), channel_id=1, source_target_pairs={{0,264},{8,0},{256,8},{264,256},{1,265},{9,1},{257,9},{265,257},{2... | collective-permute-start | bytes 3145736 | tf_op jit(solution)/shard_map/ppermute | solution.py:117
  34.9 29.1 %collective-permute-start.4 = (bf16[2048,256]{1,0:T(8,128)(2,1)}, bf16[2048,256]{1,0:T(8,128)(2,1)}, u32[]{:S(2)}, u32[]{:S(2)}) collective-permute-start(bf16[2048,256]{1,0:T(8,128)(2,1)} %shard_map.29.refs_2_), channel_id=1, source_target_pairs={{0,8},{8,256},{256,264},{264,0},{1,9},{9,257},{257,265},{265,1},{2... | collective-permute-start | bytes 3145736 | tf_op jit(solution)/shard_map/ppermute | solution.py:120
  38.7 25.3 %collective-permute-start.5 = (bf16[512,256]{1,0:T(8,128)(2,1)}, bf16[512,256]{1,0:T(8,128)(2,1)}, u32[]{:S(2)}, u32[]{:S(2)}) collective-permute-start(bf16[512,256]{1,0:T(8,128)(2,1)} %shard_map.30.refs_5_), channel_id=1, source_target_pairs={{0,264},{8,0},{256,8},{264,256},{1,265},{9,1},{257,9},{265,257},{2... | collective-permute-start | bytes 786440 | tf_op jit(solution)/shard_map/ppermute | solution.py:121
  60.1 6.8 %collective-permute-start.6 = (bf16[2,128,2560]{2,0,1:T(2,128)(2,1)S(1)}, bf16[2,128,2560]{2,0,1:T(2,128)(2,1)S(1)}, u32[]{:S(2)}, u32[]{:S(2)}) collective-permute-start(bf16[2,128,2560]{2,0,1:T(2,128)(2,1)S(1)} %all-to-all-done), channel_id=1, source_target_pairs={{0,128},{128,0},{1,129},{129,1},{2,130},{130,2},{3,131},{131,3},{4... | collective-permute-start | bytes 3932168 | tf_op jit(solution)/shard_map/ppermute | solution.py:124

commit v5 on v4

v5 whole, which is shorter than its diff:
```python
import jax
import jax.numpy as jnp
from jax import lax
from jax.experimental import pallas as pl
from jax.experimental.pallas import tpu as pltpu
from jax.sharding import Mesh, PartitionSpec as P

RING = ("xh", "xl")
RIGHT = [(i, (i + 1) % 4) for i in range(4)]
LEFT = [(i, (i + 3) % 4) for i in range(4)]
SWAP = [(0, 1), (1, 0)]
VMEM = pl.BlockSpec(memory_space=pltpu.VMEM)
LIMIT = 20 * 2**20
H_LIMIT = 8 * 2**20
SPLIT = 1920
G_FLOPS = 2 * 10**10
B_FLOPS = 10**9
FLOPS = 10**11
N_FLOPS = 4 * 10**9


def keep(*refs):
    for source, target in zip(refs[: len(refs) // 2], refs[len(refs) // 2 :]):
        target[...] = source[...]


def kept(flops, *pieces):
    return pl.pallas_call(
        keep,
        out_shape=[jax.ShapeDtypeStruct(piece.shape, piece.dtype) for piece in pieces],
        in_specs=[VMEM] * len(pieces),
        out_specs=[VMEM] * len(pieces),
        compiler_params=pltpu.CompilerParams(vmem_limit_bytes=H_LIMIT),
        cost_estimate=pl.CostEstimate(flops=flops, bytes_accessed=2**21, transcendentals=0),
    )(*pieces)


def halves(blocks, top_ref, low_ref):
    top_ref[...] = blocks[:SPLIT]
    low_ref[...] = blocks[SPLIT:]


def halved(blocks):
    return pl.pallas_call(
        halves,
        out_shape=[jax.ShapeDtypeStruct((rows, 256), jnp.bfloat16) for rows in (SPLIT, 2560 - SPLIT)],
        in_specs=[VMEM],
        out_specs=[VMEM, VMEM],
        compiler_params=pltpu.CompilerParams(vmem_limit_bytes=H_LIMIT),
    )(blocks)


def times(rows, halves):
    top = jnp.dot(rows[:, :SPLIT], halves[0][...], preferred_element_type=jnp.float32)
    return top + jnp.dot(rows[:, SPLIT:], halves[1][...], preferred_element_type=jnp.float32)


def place():
    xh, xl = lax.axis_index("xh"), lax.axis_index("xl")
    return xh, lax.rem(xh + xl, 2), lax.rem(xh + 1 - xl, 2)


def same():
    return lax.axis_index("xl") == lax.axis_index("core")


def own_near(pieces, *refs):
    here, left, right, rows, sum_ref = refs[:2], refs[2:4], refs[4:6], refs[6], refs[7]
    xh, right_xh, left_xh = place()
    rows[...] = pieces[...].reshape(256, 2560)

    @pl.when(same())
    def _():
        sum_ref[xh] = times(rows, here)
        sum_ref[1 - xh] = jnp.zeros((256, 256), jnp.float32)

    @pl.when(jnp.logical_not(same()))
    def _():
        sum_ref[right_xh] = times(rows, right)
        sum_ref[left_xh] = times(rows, left)


def other_near(first_ref, pieces, *refs):
    here, left, right, rows, sum_ref = refs[:2], refs[2:4], refs[4:6], refs[6], refs[7]
    xh, right_xh, left_xh = place()
    rows[...] = pieces[...].reshape(256, 2560)

    @pl.when(same())
    def _():
        sum_ref[right_xh] = first_ref[right_xh] + times(rows, right)
        sum_ref[left_xh] = first_ref[left_xh] + times(rows, left)

    @pl.when(jnp.logical_not(same()))
    def _():
        sum_ref[xh] = first_ref[xh] + times(rows, here)
        sum_ref[1 - xh] = first_ref[1 - xh]


def with_far(near_ref, own, other, far_top, far_low, out_ref, sum_ref):
    xh = lax.axis_index("xh")
    sum_ref[xh] = near_ref[xh]

    @pl.when(same())
    def _():
        sum_ref[1 - xh] = near_ref[1 - xh] + times(own, (far_top, far_low))

    @pl.when(jnp.logical_not(same()))
    def _():
        sum_ref[1 - xh] = near_ref[1 - xh] + times(other, (far_top, far_low))

    for block in range(2):
        for half in range(2):
            out_ref[pl.ds(2 * block + half, 256, stride=4), :] = sum_ref[block, :, 128 * half : 128 * half + 128]


SUMS = jax.ShapeDtypeStruct((2, 256, 256), jnp.float32)
ROWS = jax.ShapeDtypeStruct((256, 2560), jnp.bfloat16)


def run(kernel, flops, outs, scratch, *operands):
    return pl.pallas_call(
        kernel,
        out_shape=outs,
        in_specs=[VMEM] * len(operands),
        out_specs=[VMEM] * len(outs),
        scratch_shapes=scratch,
        compiler_params=pltpu.CompilerParams(vmem_limit_bytes=LIMIT),
        cost_estimate=pl.CostEstimate(flops=flops, bytes_accessed=2**22, transcendentals=0),
    )(*operands)


def shards(amplitudes, integrals):
    top, low = halved(integrals)
    left_top = lax.ppermute(top, RING, RIGHT)
    right_low = lax.ppermute(low, RING, LEFT)
    left_low = lax.ppermute(low, RING, RIGHT)
    right_top = lax.ppermute(top, RING, LEFT)
    (left_top,) = kept(G_FLOPS, left_top)
    (right_low,) = kept(B_FLOPS, right_low)
    far_top = lax.ppermute(left_top, RING, RIGHT)
    far_low = lax.ppermute(right_low, RING, LEFT)
    raw = lax.all_to_all(amplitudes.reshape(2, 128, 2560), ("z", "core", "y"), split_axis=1, concat_axis=1, tiled=True)
    raw, _, _ = lax.optimization_barrier((raw, left_top, right_low))
    raw_other = lax.ppermute(raw, "core", SWAP)
    near = (top, low, left_top, left_low, right_top, right_low)
    own, first = run(own_near, FLOPS, [ROWS, SUMS], [], raw.transpose(1, 0, 2), *near)
    other, second = run(other_near, N_FLOPS, [ROWS, SUMS], [], first, raw_other.transpose(1, 0, 2), *near)
    partial = jax.ShapeDtypeStruct((1024, 128), jnp.float32)
    scratch = [pltpu.VMEM((2, 256, 256), jnp.float32)]
    (partial,) = run(with_far, 10**9, [partial], scratch, second, own, other, far_top, far_low)
    partial = partial.reshape(128, 8, 128)
    parts = lax.all_to_all(partial, ("z", "core", "y"), split_axis=0, concat_axis=0, tiled=True)
    total = 0.5 * jnp.sum(parts.reshape(8, 2, 8, 8, 128), axis=(0, 2))
    return total.reshape(2, 2, 2, 256).transpose(1, 2, 0, 3).reshape(2, 1024)


def solution(mesh):
    fine = Mesh(mesh.devices.reshape(2, 2, 8, 2, 8), ("xh", "core", "z", "xl", "y"))
    rows = P(("xh", "core", "z", "xl", "y"), None)
    in_specs = (rows, P(("z", "xl", "y"), ("xh", "core")))
    return jax.shard_map(shards, mesh=fine, in_specs=in_specs, out_specs=rows, check_vma=False)
```

time: 106 us -> 103 us (0.972)
    ppermute x1, waiting for transfers between devices: 1.93 us -> 0.01 us  [shards(): far_low = lax.ppermute(right_low, RING, LEFT)]
    ppermute x1, waiting for transfers between devices: 0.01 us -> 1.54 us  [shards(): right_low = lax.ppermute(low, RING, LEFT)]
    ppermute x1, starting transfers between devices: 3.36 us -> 4.57 us  [shards(): far_low = lax.ppermute(right_low, RING, LEFT)]
    ppermute x1, starting transfers between devices: 3.11 us -> 1.91 us  [shards(): far_top = lax.ppermute(left_top, RING, RIGHT)]
    pallas_call x2, Pallas kernels: 2.98 us -> 1.82 us  [kept(): pl.pallas_call(keep, out_shape=[jax.ShapeDtypeStruct(piece.shape, piece.d...]
    pallas_call x2 -> x3, Pallas kernels: 5.69 us -> 6.07 us  [run(): pl.pallas_call(kernel, out_shape=outs, in_specs=[VMEM] * len(operands), o...]
  transfers between devices with their start and end apart: 8 -> 8, of which waited for: 2 -> 2; matrix products, arithmetic and copies ran while one was open for 0% -> 0% of each run, Pallas kernels for 6% -> 7%
where the time goes in v5:
time: 103 us
  starting transfers between devices  39 us (38%)
  blocking collectives  33.7 us (33%)
  waiting for transfers between devices  19.1 us (19%)
  Pallas kernels  8.93 us (9%)
  local copies, waits for them, and re-layouts  1.95 us (2%)
    all_to_all x1, blocking collectives, shards(): lax.all_to_all(partial, ('z', 'core', 'y'), split_axis=0, concat_axis=0,...  33.7 us
    all_to_all x1, starting transfers between devices, shards(): lax.all_to_all(amplitudes.reshape(2, 128, 2560), ('z', 'core', 'y'), spli...  17.9 us
    all_to_all x1, waiting for transfers between devices, shards(): lax.all_to_all(amplitudes.reshape(2, 128, 2560), ('z', 'core', 'y'), spli...  17.6 us
    pallas_call x3, Pallas kernels, run(): pl.pallas_call(kernel, out_shape=outs, in_specs=[VMEM] * len(operands), o...  6.07 us
    ppermute x1, starting transfers between devices, shards(): far_low = lax.ppermute(right_low, RING, LEFT)  4.57 us
    ppermute x1, starting transfers between devices, shards(): left_top = lax.ppermute(top, RING, RIGHT)  3.94 us
    ppermute x1, starting transfers between devices, shards(): right_low = lax.ppermute(low, RING, LEFT)  3.37 us
    ppermute x1, starting transfers between devices, shards(): right_top = lax.ppermute(top, RING, LEFT)  3.18 us
  transfers between devices with their start and end apart: 8, of which 2 were waited for; matrix products, arithmetic and copies ran while one was open for 0% of the time, Pallas kernels for 7%

profile of v5, /device:TPU:1, one launch (start us, length us, event | category | flops | bytes accessed | tf_op | source)
XLA Modules:
  0.0 102.8 jit_solution(10549077724563691874)
XLA Ops:
  0.0 1.3 %copy-done = bf16[2560,256]{1,0:T(8,128)(2,1)S(1)} copy-done((bf16[2560,256]{1,0:T(8,128)(2,1)S(1)}, bf16[2560,256]{1,0:T(8,128)(2,1)}, u32[]{:S(2)}) %copy-start) | copy-done | bytes 1310744
  1.3 1.0 %shard_map.28 = (bf16[1920,256]{1,0:T(8,128)(2,1)}, bf16[640,256]{1,0:T(8,128)(2,1)S(1)}) custom-call(bf16[2560,256]{1,0:T(8,128)(2,1)S(1)} %copy-done), custom_call_target="tpu_custom_call" | custom-call | tf_op jit(solution)/shard_map/pallas_call | solution.py:44
  2.4 3.9 %collective-permute-start = (bf16[1920,256]{1,0:T(8,128)(2,1)}, bf16[1920,256]{1,0:T(8,128)(2,1)S(1)}, u32[]{:S(2)}, u32[]{:S(2)}) collective-permute-start(bf16[1920,256]{1,0:T(8,128)(2,1)} %get-tuple-element.12.refs_0_), channel_id=1, source_target_pairs={{0,8},{8,256},{256,264},{264,0},{1,9},{9,257},{257,265},{265,1},{2... | collective-permute-start | bytes 2949128 | tf_op jit(solution)/shard_map/ppermute | solution.py:134
  6.3 17.9 %all-to-all-start = ((bf16[2,128,2560]{2,0,1:T(2,128)(2,1)}), bf16[2,128,2560]{2,0,1:T(2,128)(2,1)S(1)}, u32[]{:S(2)}, u32[]{:S(2)}) async-start(bf16[2,128,2560]{2,0,1:T(2,128)(2,1)} %bitcast.10), calls=%async_computation | async-start | bytes 2621440 | tf_op jit(solution)/shard_map/all_to_all | solution.py:142
  24.2 3.4 %collective-permute-start.1 = (bf16[640,256]{1,0:T(8,128)(2,1)S(1)}, bf16[640,256]{1,0:T(8,128)(2,1)S(1)}, u32[]{:S(2)}, u32[]{:S(2)}) collective-permute-start(bf16[640,256]{1,0:T(8,128)(2,1)S(1)} %get-tuple-element.13.refs_1_), channel_id=1, source_target_pairs={{0,264},{8,0},{256,8},{264,256},{1,265},{9,1},{257,9},{265,257},{2... | collective-permute-start | bytes 983048 | tf_op jit(solution)/shard_map/ppermute | solution.py:135
  27.6 3.2 %collective-permute-start.3 = (bf16[1920,256]{1,0:T(8,128)(2,1)}, bf16[1920,256]{1,0:T(8,128)(2,1)}, u32[]{:S(2)}, u32[]{:S(2)}) collective-permute-start(bf16[1920,256]{1,0:T(8,128)(2,1)} %get-tuple-element.12.refs_0_), channel_id=1, source_target_pairs={{0,264},{8,0},{256,8},{264,256},{1,265},{9,1},{257,9},{265,257},{2... | collective-permute-start | bytes 2949128 | tf_op jit(solution)/shard_map/ppermute | solution.py:137
  30.8 2.1 %collective-permute-start.2 = (bf16[640,256]{1,0:T(8,128)(2,1)S(1)}, bf16[640,256]{1,0:T(8,128)(2,1)S(1)}, u32[]{:S(2)}, u32[]{:S(2)}) collective-permute-start(bf16[640,256]{1,0:T(8,128)(2,1)S(1)} %get-tuple-element.13.refs_1_), channel_id=1, source_target_pairs={{0,8},{8,256},{256,264},{264,0},{1,9},{9,257},{257,265},{265,1},{2... | collective-permute-start | bytes 983048 | tf_op jit(solution)/shard_map/ppermute | solution.py:136
  32.9 1.5 %collective-permute-done.1.refs_0_ = bf16[640,256]{1,0:T(8,128)(2,1)S(1)} collective-permute-done((bf16[640,256]{1,0:T(8,128)(2,1)S(1)}, bf16[640,256]{1,0:T(8,128)(2,1)S(1)}, u32[]{:S(2)}, u32[]{:S(2)}) %collective-permute-start.1) | collective-permute-done | bytes 327712 | tf_op jit(solution)/shard_map/ppermute | solution.py:135
  34.4 0.8 shard_map.30.refs_5_
  35.2 4.6 %collective-permute-start.6 = (bf16[640,256]{1,0:T(8,128)(2,1)}, bf16[640,256]{1,0:T(8,128)(2,1)S(1)}, u32[]{:S(2)}, u32[]{:S(2)}) collective-permute-start(bf16[640,256]{1,0:T(8,128)(2,1)} %shard_map.30.refs_5_), channel_id=1, source_target_pairs={{0,264},{8,0},{256,8},{264,256},{1,265},{9,1},{257,9},{265,257},{2... | collective-permute-start | bytes 983048 | tf_op jit(solution)/shard_map/ppermute | solution.py:141
  39.8 0.0 collective-permute-done.refs_0_
  39.8 1.1 %shard_map.29.refs_2_ = bf16[1920,256]{1,0:T(8,128)(2,1)} custom-call(bf16[1920,256]{1,0:T(8,128)(2,1)S(1)} %collective-permute-done.refs_0_), custom_call_target="tpu_custom_call" | custom-call | flops 20000000000 | bytes 2097152 | tf_op jit(solution)/shard_map/pallas_call | solution.py:28
  40.8 1.9 %collective-permute-start.5 = (bf16[1920,256]{1,0:T(8,128)(2,1)}, bf16[1920,256]{1,0:T(8,128)(2,1)S(1)}, u32[]{:S(2)}, u32[]{:S(2)}) collective-permute-start(bf16[1920,256]{1,0:T(8,128)(2,1)} %shard_map.29.refs_2_), channel_id=1, source_target_pairs={{0,8},{8,256},{256,264},{264,0},{1,9},{9,257},{257,265},{265,1},{2... | collective-permute-start | bytes 2949128 | tf_op jit(solution)/shard_map/ppermute | solution.py:140
  42.7 17.6 %all-to-all-done = bf16[2,128,2560]{2,0,1:T(2,128)(2,1)S(1)} async-done(((bf16[2,128,2560]{2,0,1:T(2,128)(2,1)}), bf16[2,128,2560]{2,0,1:T(2,128)(2,1)S(1)}, u32[]{:S(2)}, u32[]{:S(2)}) %all-to-all-start) | async-done | bytes 1310752 | tf_op jit(solution)/shard_map/all_to_all | solution.py:142
  60.3 2.0 %collective-permute-start.4 = (bf16[2,128,2560]{2,0,1:T(2,128)(2,1)S(1)}, bf16[2,128,2560]{2,0,1:T(2,128)(2,1)S(1)}, u32[]{:S(2)}, u32[]{:S(2)}) collective-permute-start(bf16[2,128,2560]{2,0,1:T(2,128)(2,1)S(1)} %all-to-all-done), channel_id=1, source_target_pairs={{0,128},{128,0},{1,129},{129,1},{2,130},{130,2},{3,131},{131,3},{4... | collective-permute-start | bytes 3932168 | tf_op jit(solution)/shard_map/ppermute | solution.py:144
  62.3 0.0 collective-permute-done.2.refs_3_
  62.3 0.0 collective-permute-done.3.refs_4_
  62.3 2.9 %shard_map.31 = (bf16[256,2560]{1,0:T(8,128)(2,1)S(1)}, f32[2,256,256]{2,1,0:T(8,128)S(1)}) custom-call(bf16[128,2,2560]{2,1,0:T(2,128)(2,1)S(1)} %bitcast.7, bf16[1920,256]{1,0:T(8,128)(2,1)} %get-tuple-element.12.refs_0_, bf16[640,256]{1,0:T(8,128)(2,1)S(1)} %get-tuple-element.13.refs_1_, bf16[1920,256]{1,0:T(8,128)(2,1)} %shard_map.29.refs_2_, ...), custom_call_target="tpu_custom_call" | custom-call | flops 99999997952 | bytes 4194304 | tf_op jit(solution)/shard_map/pallas_call | solution.py:121
  65.3 2.5 %shard_map.32 = (bf16[256,2560]{1,0:T(8,128)(2,1)S(1)}, f32[2,256,256]{2,1,0:T(8,128)S(1)}) custom-call(f32[2,256,256]{2,1,0:T(8,128)S(1)} %get-tuple-element.15.first_ref, bf16[128,2,2560]{2,1,0:T(2,128)(2,1)S(1)} %bitcast.8, bf16[1920,256]{1,0:T(8,128)(2,1)} %get-tuple-element.12.refs_0_, bf16[640,256]{1,0:T(8,128)(2,1)S(1)} %get-tuple-element.13.refs_1_, ...), custom_call_target="tpu_custom_call" | custom-call | flops 4000000000 | bytes 4194304 | tf_op jit(solution)/shard_map/pallas_call | solution.py:121
  67.8 0.0 collective-permute-done.6.far_low
  67.8 0.6 shard_map.33
  68.5 33.7 %all_to_all.10 = f32[128,8,128]{2,1,0:T(8,128)S(1)} all-to-all(f32[128,8,128]{2,1,0:T(8,128)S(1)} %bitcast.6), channel_id=1, replica_groups=mesh['xh'=2,'core'=2,'z'=8,'xl'=2,'y'=8] {'z','core','y'}, dimensions={0} | all-to-all | bytes 1048576 | tf_op jit(solution)/shard_map/all_to_all | solution.py:152
  102.1 0.1 reduce_sum.9
  102.2 0.6 reshape.19
  (6 shorter events, 0.0 us)
Async XLA Ops:
  0.0 1.3 %copy-start = (bf16[2560,256]{1,0:T(8,128)(2,1)S(1)}, bf16[2560,256]{1,0:T(8,128)(2,1)}, u32[]{:S(2)}) copy-start(bf16[2560,256]{1,0:T(8,128)(2,1)} %blocks.1) | copy-start | bytes 3932164
  2.4 37.4 %collective-permute-start = (bf16[1920,256]{1,0:T(8,128)(2,1)}, bf16[1920,256]{1,0:T(8,128)(2,1)S(1)}, u32[]{:S(2)}, u32[]{:S(2)}) collective-permute-start(bf16[1920,256]{1,0:T(8,128)(2,1)} %get-tuple-element.12.refs_0_), channel_id=1, source_target_pairs={{0,8},{8,256},{256,264},{264,0},{1,9},{9,257},{257,265},{265,1},{2... | collective-permute-start | bytes 2949128 | tf_op jit(solution)/shard_map/ppermute | solution.py:134
  6.3 54.0 %all-to-all-start = ((bf16[2,128,2560]{2,0,1:T(2,128)(2,1)}), bf16[2,128,2560]{2,0,1:T(2,128)(2,1)S(1)}, u32[]{:S(2)}, u32[]{:S(2)}) async-start(bf16[2,128,2560]{2,0,1:T(2,128)(2,1)} %bitcast.10), calls=%async_computation | async-start | bytes 2621440 | tf_op jit(solution)/shard_map/all_to_all | solution.py:142
  24.2 10.2 %collective-permute-start.1 = (bf16[640,256]{1,0:T(8,128)(2,1)S(1)}, bf16[640,256]{1,0:T(8,128)(2,1)S(1)}, u32[]{:S(2)}, u32[]{:S(2)}) collective-permute-start(bf16[640,256]{1,0:T(8,128)(2,1)S(1)} %get-tuple-element.13.refs_1_), channel_id=1, source_target_pairs={{0,264},{8,0},{256,8},{264,256},{1,265},{9,1},{257,9},{265,257},{2... | collective-permute-start | bytes 983048 | tf_op jit(solution)/shard_map/ppermute | solution.py:135
  27.6 34.7 %collective-permute-start.3 = (bf16[1920,256]{1,0:T(8,128)(2,1)}, bf16[1920,256]{1,0:T(8,128)(2,1)}, u32[]{:S(2)}, u32[]{:S(2)}) collective-permute-start(bf16[1920,256]{1,0:T(8,128)(2,1)} %get-tuple-element.12.refs_0_), channel_id=1, source_target_pairs={{0,264},{8,0},{256,8},{264,256},{1,265},{9,1},{257,9},{265,257},{2... | collective-permute-start | bytes 2949128 | tf_op jit(solution)/shard_map/ppermute | solution.py:137
  30.8 31.6 %collective-permute-start.2 = (bf16[640,256]{1,0:T(8,128)(2,1)S(1)}, bf16[640,256]{1,0:T(8,128)(2,1)S(1)}, u32[]{:S(2)}, u32[]{:S(2)}) collective-permute-start(bf16[640,256]{1,0:T(8,128)(2,1)S(1)} %get-tuple-element.13.refs_1_), channel_id=1, source_target_pairs={{0,8},{8,256},{256,264},{264,0},{1,9},{9,257},{257,265},{265,1},{2... | collective-permute-start | bytes 983048 | tf_op jit(solution)/shard_map/ppermute | solution.py:136
  35.2 32.6 %collective-permute-start.6 = (bf16[640,256]{1,0:T(8,128)(2,1)}, bf16[640,256]{1,0:T(8,128)(2,1)S(1)}, u32[]{:S(2)}, u32[]{:S(2)}) collective-permute-start(bf16[640,256]{1,0:T(8,128)(2,1)} %shard_map.30.refs_5_), channel_id=1, source_target_pairs={{0,264},{8,0},{256,8},{264,256},{1,265},{9,1},{257,9},{265,257},{2... | collective-permute-start | bytes 983048 | tf_op jit(solution)/shard_map/ppermute | solution.py:141
  40.8 27.0 %collective-permute-start.5 = (bf16[1920,256]{1,0:T(8,128)(2,1)}, bf16[1920,256]{1,0:T(8,128)(2,1)S(1)}, u32[]{:S(2)}, u32[]{:S(2)}) collective-permute-start(bf16[1920,256]{1,0:T(8,128)(2,1)} %shard_map.29.refs_2_), channel_id=1, source_target_pairs={{0,8},{8,256},{256,264},{264,0},{1,9},{9,257},{257,265},{265,1},{2... | collective-permute-start | bytes 2949128 | tf_op jit(solution)/shard_map/ppermute | solution.py:140
  60.3 5.0 %collective-permute-start.4 = (bf16[2,128,2560]{2,0,1:T(2,128)(2,1)S(1)}, bf16[2,128,2560]{2,0,1:T(2,128)(2,1)S(1)}, u32[]{:S(2)}, u32[]{:S(2)}) collective-permute-start(bf16[2,128,2560]{2,0,1:T(2,128)(2,1)S(1)} %all-to-all-done), channel_id=1, source_target_pairs={{0,128},{128,0},{1,129},{129,1},{2,130},{130,2},{3,131},{131,3},{4... | collective-permute-start | bytes 3932168 | tf_op jit(solution)/shard_map/ppermute | solution.py:144

commit v6 on v5

--- a/solution.py
+++ b/solution.py
@@ -12,8 +12,8 @@
 VMEM = pl.BlockSpec(memory_space=pltpu.VMEM)
 LIMIT = 20 * 2**20
 H_LIMIT = 8 * 2**20
-SPLIT = 1920
-G_FLOPS = 2 * 10**10
+SPLIT = 1792
+G_FLOPS = 18 * 10**9
 B_FLOPS = 10**9
 FLOPS = 10**11
 N_FLOPS = 4 * 10**9
@@ -21,13 +21,13 @@
 
 def keep(*refs):
     for source, target in zip(refs[: len(refs) // 2], refs[len(refs) // 2 :]):
-        target[...] = source[...]
+        target[...] = source[: target.shape[0]]
 
 
-def kept(flops, *pieces):
+def kept(flops, *pieces, rows=None):
     return pl.pallas_call(
         keep,
-        out_shape=[jax.ShapeDtypeStruct(piece.shape, piece.dtype) for piece in pieces],
+        out_shape=[jax.ShapeDtypeStruct((rows or piece.shape[0], 256), piece.dtype) for piece in pieces],
         in_specs=[VMEM] * len(pieces),
         out_specs=[VMEM] * len(pieces),
         compiler_params=pltpu.CompilerParams(vmem_limit_bytes=H_LIMIT),
@@ -51,6 +51,8 @@
 
 
 def times(rows, halves):
+    if len(halves) == 1:
+        return jnp.dot(rows[...], halves[0][...], preferred_element_type=jnp.float32)
     top = jnp.dot(rows[:, :SPLIT], halves[0][...], preferred_element_type=jnp.float32)
     return top + jnp.dot(rows[:, SPLIT:], halves[1][...], preferred_element_type=jnp.float32)
 
@@ -65,7 +67,7 @@
 
 
 def own_near(pieces, *refs):
-    here, left, right, rows, sum_ref = refs[:2], refs[2:4], refs[4:6], refs[6], refs[7]
+    here, left, right, rows, sum_ref = refs[:1], refs[1:2], refs[2:4], refs[4], refs[5]
     xh, right_xh, left_xh = place()
     rows[...] = pieces[...].reshape(256, 2560)
 
@@ -81,7 +83,7 @@
 
 
 def other_near(first_ref, pieces, *refs):
-    here, left, right, rows, sum_ref = refs[:2], refs[2:4], refs[4:6], refs[6], refs[7]
+    here, left, right, rows, sum_ref = refs[:1], refs[1:2], refs[2:4], refs[4], refs[5]
     xh, right_xh, left_xh = place()
     rows[...] = pieces[...].reshape(256, 2560)
 
@@ -131,18 +133,17 @@
 
 def shards(amplitudes, integrals):
     top, low = halved(integrals)
-    left_top = lax.ppermute(top, RING, RIGHT)
+    left = lax.ppermute(integrals, RING, RIGHT)
     right_low = lax.ppermute(low, RING, LEFT)
-    left_low = lax.ppermute(low, RING, RIGHT)
     right_top = lax.ppermute(top, RING, LEFT)
-    (left_top,) = kept(G_FLOPS, left_top)
+    (left_top,) = kept(G_FLOPS, left, rows=SPLIT)
     (right_low,) = kept(B_FLOPS, right_low)
     far_top = lax.ppermute(left_top, RING, RIGHT)
     far_low = lax.ppermute(right_low, RING, LEFT)
     raw = lax.all_to_all(amplitudes.reshape(2, 128, 2560), ("z", "core", "y"), split_axis=1, concat_axis=1, tiled=True)
     raw, _, _ = lax.optimization_barrier((raw, left_top, right_low))
     raw_other = lax.ppermute(raw, "core", SWAP)
-    near = (top, low, left_top, left_low, right_top, right_low)
+    near = (integrals, left, right_top, right_low)
     own, first = run(own_near, FLOPS, [ROWS, SUMS], [], raw.transpose(1, 0, 2), *near)
     other, second = run(other_near, N_FLOPS, [ROWS, SUMS], [], first, raw_other.transpose(1, 0, 2), *near)
     partial = jax.ShapeDtypeStruct((1024, 128), jnp.float32)

time: 103 us -> 104 us (level)
  blocking collectives: 33.7 us -> 36.2 us
  starting transfers between devices: 39 us -> 36.9 us
  Pallas kernels: 8.93 us -> 10.7 us
  local copies, waits for them, and re-layouts: 1.95 us -> 0.64 us
    all_to_all x1, waiting for transfers between devices: 17.6 us -> 13.9 us  [shards(): lax.all_to_all(amplitudes.reshape(2, 128, 2560), ('z', 'core', 'y'), spli...]
    ppermute x1, waiting for transfers between devices: 1.54 us -> 5.17 us  [shards(): right_low = lax.ppermute(low, RING, LEFT)]
    all_to_all x1, blocking collectives: 33.7 us -> 36.2 us  [shards(): lax.all_to_all(partial, ('z', 'core', 'y'), split_axis=0, concat_axis=0,...]
    ppermute x2 -> x1, starting transfers between devices: 6.04 us -> 3.94 us  [shards(): left = lax.ppermute(integrals, RING, RIGHT)]
    unnamed x2, local copies, waits for them, and re-layouts: 1.32 us -> 0.01 us
    pallas_call x2, Pallas kernels: 1.82 us -> 3.09 us  [kept(): pl.pallas_call(keep, out_shape=[jax.ShapeDtypeStruct((rows or piece.shape...]
  transfers between devices with their start and end apart: 8 -> 7, of which waited for: 2 -> 3; matrix products, arithmetic and copies ran while one was open for 0% -> 0% of each run, Pallas kernels for 7% -> 9%
where the time goes in v6:
time: 104 us
  starting transfers between devices  36.9 us (35%)
  blocking collectives  36.2 us (35%)
  waiting for transfers between devices  19.3 us (19%)
  Pallas kernels  10.7 us (10%)
    all_to_all x1, blocking collectives, shards(): lax.all_to_all(partial, ('z', 'core', 'y'), split_axis=0, concat_axis=0,...  36.2 us
    all_to_all x1, starting transfers between devices, shards(): lax.all_to_all(amplitudes.reshape(2, 128, 2560), ('z', 'core', 'y'), spli...  18 us
    all_to_all x1, waiting for transfers between devices, shards(): lax.all_to_all(amplitudes.reshape(2, 128, 2560), ('z', 'core', 'y'), spli...  13.9 us
    pallas_call x3, Pallas kernels, run(): pl.pallas_call(kernel, out_shape=outs, in_specs=[VMEM] * len(operands), o...  6.55 us
    ppermute x1, waiting for transfers between devices, shards(): right_low = lax.ppermute(low, RING, LEFT)  5.17 us
    ppermute x1, starting transfers between devices, shards(): far_low = lax.ppermute(right_low, RING, LEFT)  4.47 us
    ppermute x1, starting transfers between devices, shards(): left = lax.ppermute(integrals, RING, RIGHT)  3.94 us
    ppermute x1, starting transfers between devices, shards(): right_low = lax.ppermute(low, RING, LEFT)  3.36 us
  transfers between devices with their start and end apart: 7, of which 3 were waited for; matrix products, arithmetic and copies ran while one was open for 0% of the time, Pallas kernels for 9%

profile of v6, /device:TPU:1, one launch (start us, length us, event | category | flops | bytes accessed | tf_op | source)
XLA Modules:
  0.0 103.9 jit_solution(9947589178921364477)
XLA Ops:
  0.0 3.9 %collective-permute-start = (bf16[2560,256]{1,0:T(8,128)(2,1)}, bf16[2560,256]{1,0:T(8,128)(2,1)}, u32[]{:S(2)}, u32[]{:S(2)}) collective-permute-start(bf16[2560,256]{1,0:T(8,128)(2,1)} %refs_0_.3), channel_id=1, source_target_pairs={{0,8},{8,256},{256,264},{264,0},{1,9},{9,257},{257,265},{265,1},{2... | collective-permute-start | bytes 3932168 | tf_op jit(solution)/shard_map/ppermute | solution.py:136
  3.9 0.0 copy-start
  4.0 18.0 %all-to-all-start = ((bf16[2,128,2560]{2,0,1:T(2,128)(2,1)}), bf16[2,128,2560]{2,0,1:T(2,128)(2,1)S(1)}, u32[]{:S(2)}, u32[]{:S(2)}) async-start(bf16[2,128,2560]{2,0,1:T(2,128)(2,1)} %bitcast.10), calls=%async_computation | async-start | bytes 2621440 | tf_op jit(solution)/shard_map/all_to_all | solution.py:143
  22.0 1.0 shard_map.29
  23.0 3.4 %collective-permute-start.1 = (bf16[768,256]{1,0:T(8,128)(2,1)S(1)}, bf16[768,256]{1,0:T(8,128)(2,1)S(1)}, u32[]{:S(2)}, u32[]{:S(2)}) collective-permute-start(bf16[768,256]{1,0:T(8,128)(2,1)S(1)} %get-tuple-element.12), channel_id=1, source_target_pairs={{0,264},{8,0},{256,8},{264,256},{1,265},{9,1},{257,9},{265,257},{2... | collective-permute-start | bytes 1179656 | tf_op jit(solution)/shard_map/ppermute | solution.py:137
  26.4 3.2 %collective-permute-start.2 = (bf16[1792,256]{1,0:T(8,128)(2,1)}, bf16[1792,256]{1,0:T(8,128)(2,1)}, u32[]{:S(2)}, u32[]{:S(2)}) collective-permute-start(bf16[1792,256]{1,0:T(8,128)(2,1)} %get-tuple-element.14), channel_id=1, source_target_pairs={{0,264},{8,0},{256,8},{264,256},{1,265},{9,1},{257,9},{265,257},{2... | collective-permute-start | bytes 2752520 | tf_op jit(solution)/shard_map/ppermute | solution.py:138
  29.6 5.2 %collective-permute-done.1.refs_0_ = bf16[768,256]{1,0:T(8,128)(2,1)S(1)} collective-permute-done((bf16[768,256]{1,0:T(8,128)(2,1)S(1)}, bf16[768,256]{1,0:T(8,128)(2,1)S(1)}, u32[]{:S(2)}, u32[]{:S(2)}) %collective-permute-start.1) | collective-permute-done | bytes 393248 | tf_op jit(solution)/shard_map/ppermute | solution.py:137
  34.7 0.8 shard_map.30.refs_3_
  35.5 4.5 %collective-permute-start.5 = (bf16[768,256]{1,0:T(8,128)(2,1)}, bf16[768,256]{1,0:T(8,128)(2,1)}, u32[]{:S(2)}, u32[]{:S(2)}) collective-permute-start(bf16[768,256]{1,0:T(8,128)(2,1)} %shard_map.30.refs_3_), channel_id=1, source_target_pairs={{0,264},{8,0},{256,8},{264,256},{1,265},{9,1},{257,9},{265,257},{2... | collective-permute-start | bytes 1179656 | tf_op jit(solution)/shard_map/ppermute | solution.py:142
  40.0 0.0 collective-permute-done.refs_0_.refs_1_
  40.0 2.3 %shard_map.28 = bf16[1792,256]{1,0:T(8,128)(2,1)} custom-call(bf16[2560,256]{1,0:T(8,128)(2,1)} %collective-permute-done.refs_0_.refs_1_), custom_call_target="tpu_custom_call" | custom-call | flops 17999998976 | bytes 2097152 | tf_op jit(solution)/shard_map/pallas_call | solution.py:28
  42.3 1.9 %collective-permute-start.4 = (bf16[1792,256]{1,0:T(8,128)(2,1)}, bf16[1792,256]{1,0:T(8,128)(2,1)S(1)}, u32[]{:S(2)}, u32[]{:S(2)}) collective-permute-start(bf16[1792,256]{1,0:T(8,128)(2,1)} %shard_map.28), channel_id=1, source_target_pairs={{0,8},{8,256},{256,264},{264,0},{1,9},{9,257},{257,265},{265,1},{2... | collective-permute-start | bytes 2752520 | tf_op jit(solution)/shard_map/ppermute | solution.py:141
  44.2 13.9 %all-to-all-done = bf16[2,128,2560]{2,0,1:T(2,128)(2,1)S(1)} async-done(((bf16[2,128,2560]{2,0,1:T(2,128)(2,1)}), bf16[2,128,2560]{2,0,1:T(2,128)(2,1)S(1)}, u32[]{:S(2)}, u32[]{:S(2)}) %all-to-all-start) | async-done | bytes 1310752 | tf_op jit(solution)/shard_map/all_to_all | solution.py:143
  58.1 2.0 %collective-permute-start.3 = (bf16[2,128,2560]{2,0,1:T(2,128)(2,1)S(1)}, bf16[2,128,2560]{2,0,1:T(2,128)(2,1)S(1)}, u32[]{:S(2)}, u32[]{:S(2)}) collective-permute-start(bf16[2,128,2560]{2,0,1:T(2,128)(2,1)S(1)} %all-to-all-done), channel_id=1, source_target_pairs={{0,128},{128,0},{1,129},{129,1},{2,130},{130,2},{3,131},{131,3},{4... | collective-permute-start | bytes 3932168 | tf_op jit(solution)/shard_map/ppermute | solution.py:145
  60.1 0.0 collective-permute-done.2.refs_2_
  60.1 2.7 %shard_map.31 = (bf16[256,2560]{1,0:T(8,128)(2,1)S(1)}, f32[2,256,256]{2,1,0:T(8,128)S(1)}) custom-call(bf16[128,2,2560]{2,1,0:T(2,128)(2,1)S(1)} %bitcast.7, bf16[2560,256]{1,0:T(8,128)(2,1)S(1)} %copy-done, bf16[2560,256]{1,0:T(8,128)(2,1)} %collective-permute-done.refs_0_.refs_1_, bf16[1792,256]{1,0:T(8,128)(2,1)} %collective-permute-done.2.refs_2_, ...), custom_call_target="tpu_custom_call" | custom-call | flops 99999997952 | bytes 4194304 | tf_op jit(solution)/shard_map/pallas_call | solution.py:123
  62.8 0.2 collective-permute-done.3
  63.0 2.3 %shard_map.32 = (bf16[256,2560]{1,0:T(8,128)(2,1)S(1)}, f32[2,256,256]{2,1,0:T(8,128)S(1)}) custom-call(f32[2,256,256]{2,1,0:T(8,128)S(1)} %get-tuple-element.15.first_ref, bf16[128,2,2560]{2,1,0:T(2,128)(2,1)S(1)} %bitcast.8, bf16[2560,256]{1,0:T(8,128)(2,1)S(1)} %copy-done, bf16[2560,256]{1,0:T(8,128)(2,1)} %collective-permute-done.refs_0_.refs_1_, ...), custom_call_target="tpu_custom_call" | custom-call | flops 4000000000 | bytes 4194304 | tf_op jit(solution)/shard_map/pallas_call | solution.py:123
  65.3 0.0 collective-permute-done.5.far_low
  65.3 0.0 collective-permute-done.4.far_top
  65.4 1.6 %shard_map.33 = f32[1024,128]{1,0:T(8,128)S(1)} custom-call(f32[2,256,256]{2,1,0:T(8,128)S(1)} %get-tuple-element.16.near_ref, bf16[256,2560]{1,0:T(8,128)(2,1)S(1)} %get-tuple-element.17.own, bf16[256,2560]{1,0:T(8,128)(2,1)S(1)} %get-tuple-element.18.other, bf16[1792,256]{1,0:T(8,128)(2,1)S(1)} %collective-permute-done.4.far_top, ...), custom_call_target="tpu_custom_call" | custom-call | flops 1000000000 | bytes 4194304 | tf_op jit(solution)/shard_map/pallas_call | solution.py:123
  66.9 36.2 %all_to_all.10 = f32[128,8,128]{2,1,0:T(8,128)S(1)} all-to-all(f32[128,8,128]{2,1,0:T(8,128)S(1)} %bitcast.6), channel_id=1, replica_groups=mesh['xh'=2,'core'=2,'z'=8,'xl'=2,'y'=8] {'z','core','y'}, dimensions={0} | all-to-all | bytes 1048576 | tf_op jit(solution)/shard_map/all_to_all | solution.py:153
  103.2 0.1 reduce_sum.9
  103.3 0.6 reshape.19
  (4 shorter events, 0.0 us)
Async XLA Ops:
  0.0 40.0 %collective-permute-start = (bf16[2560,256]{1,0:T(8,128)(2,1)}, bf16[2560,256]{1,0:T(8,128)(2,1)}, u32[]{:S(2)}, u32[]{:S(2)}) collective-permute-start(bf16[2560,256]{1,0:T(8,128)(2,1)} %refs_0_.3), channel_id=1, source_target_pairs={{0,8},{8,256},{256,264},{264,0},{1,9},{9,257},{257,265},{265,1},{2... | collective-permute-start | bytes 3932168 | tf_op jit(solution)/shard_map/ppermute | solution.py:136
  3.9 18.0 %copy-start = (bf16[2560,256]{1,0:T(8,128)(2,1)S(1)}, bf16[2560,256]{1,0:T(8,128)(2,1)}, u32[]{:S(2)}) copy-start(bf16[2560,256]{1,0:T(8,128)(2,1)} %refs_0_.3) | copy-start | bytes 3932164
  4.0 54.1 %all-to-all-start = ((bf16[2,128,2560]{2,0,1:T(2,128)(2,1)}), bf16[2,128,2560]{2,0,1:T(2,128)(2,1)S(1)}, u32[]{:S(2)}, u32[]{:S(2)}) async-start(bf16[2,128,2560]{2,0,1:T(2,128)(2,1)} %bitcast.10), calls=%async_computation | async-start | bytes 2621440 | tf_op jit(solution)/shard_map/all_to_all | solution.py:143
  23.0 11.7 %collective-permute-start.1 = (bf16[768,256]{1,0:T(8,128)(2,1)S(1)}, bf16[768,256]{1,0:T(8,128)(2,1)S(1)}, u32[]{:S(2)}, u32[]{:S(2)}) collective-permute-start(bf16[768,256]{1,0:T(8,128)(2,1)S(1)} %get-tuple-element.12), channel_id=1, source_target_pairs={{0,264},{8,0},{256,8},{264,256},{1,265},{9,1},{257,9},{265,257},{2... | collective-permute-start | bytes 1179656 | tf_op jit(solution)/shard_map/ppermute | solution.py:137
  26.4 33.7 %collective-permute-start.2 = (bf16[1792,256]{1,0:T(8,128)(2,1)}, bf16[1792,256]{1,0:T(8,128)(2,1)}, u32[]{:S(2)}, u32[]{:S(2)}) collective-permute-start(bf16[1792,256]{1,0:T(8,128)(2,1)} %get-tuple-element.14), channel_id=1, source_target_pairs={{0,264},{8,0},{256,8},{264,256},{1,265},{9,1},{257,9},{265,257},{2... | collective-permute-start | bytes 2752520 | tf_op jit(solution)/shard_map/ppermute | solution.py:138
  35.5 29.8 %collective-permute-start.5 = (bf16[768,256]{1,0:T(8,128)(2,1)}, bf16[768,256]{1,0:T(8,128)(2,1)}, u32[]{:S(2)}, u32[]{:S(2)}) collective-permute-start(bf16[768,256]{1,0:T(8,128)(2,1)} %shard_map.30.refs_3_), channel_id=1, source_target_pairs={{0,264},{8,0},{256,8},{264,256},{1,265},{9,1},{257,9},{265,257},{2... | collective-permute-start | bytes 1179656 | tf_op jit(solution)/shard_map/ppermute | solution.py:142
  42.3 23.0 %collective-permute-start.4 = (bf16[1792,256]{1,0:T(8,128)(2,1)}, bf16[1792,256]{1,0:T(8,128)(2,1)S(1)}, u32[]{:S(2)}, u32[]{:S(2)}) collective-permute-start(bf16[1792,256]{1,0:T(8,128)(2,1)} %shard_map.28), channel_id=1, source_target_pairs={{0,8},{8,256},{256,264},{264,0},{1,9},{9,257},{257,265},{265,1},{2... | collective-permute-start | bytes 2752520 | tf_op jit(solution)/shard_map/ppermute | solution.py:141
  58.1 4.9 %collective-permute-start.3 = (bf16[2,128,2560]{2,0,1:T(2,128)(2,1)S(1)}, bf16[2,128,2560]{2,0,1:T(2,128)(2,1)S(1)}, u32[]{:S(2)}, u32[]{:S(2)}) collective-permute-start(bf16[2,128,2560]{2,0,1:T(2,128)(2,1)S(1)} %all-to-all-done), channel_id=1, source_target_pairs={{0,128},{128,0},{1,129},{129,1},{2,130},{130,2},{3,131},{131,3},{4... | collective-permute-start | bytes 3932168 | tf_op jit(solution)/shard_map/ppermute | solution.py:145

commit v7 on v6

--- a/solution.py
+++ b/solution.py
@@ -10,29 +10,31 @@
 LEFT = [(i, (i + 3) % 4) for i in range(4)]
 SWAP = [(0, 1), (1, 0)]
 VMEM = pl.BlockSpec(memory_space=pltpu.VMEM)
+ANY = pl.BlockSpec(memory_space=pl.ANY)
 LIMIT = 20 * 2**20
 H_LIMIT = 8 * 2**20
-SPLIT = 1792
+SPLIT = 1920
 G_FLOPS = 18 * 10**9
-B_FLOPS = 10**9
 FLOPS = 10**11
 N_FLOPS = 4 * 10**9
 
 
-def keep(*refs):
-    for source, target in zip(refs[: len(refs) // 2], refs[len(refs) // 2 :]):
-        target[...] = source[: target.shape[0]]
+def keep(left, top_ref, sem):
+    top = pltpu.make_async_copy(left.at[:SPLIT], top_ref, sem)
+    top.start()
+    top.wait()
 
 
-def kept(flops, *pieces, rows=None):
+def kept(left):
     return pl.pallas_call(
         keep,
-        out_shape=[jax.ShapeDtypeStruct((rows or piece.shape[0], 256), piece.dtype) for piece in pieces],
-        in_specs=[VMEM] * len(pieces),
-        out_specs=[VMEM] * len(pieces),
+        out_shape=jax.ShapeDtypeStruct((SPLIT, 256), jnp.bfloat16),
+        in_specs=[ANY],
+        out_specs=VMEM,
+        scratch_shapes=[pltpu.SemaphoreType.DMA],
         compiler_params=pltpu.CompilerParams(vmem_limit_bytes=H_LIMIT),
-        cost_estimate=pl.CostEstimate(flops=flops, bytes_accessed=2**21, transcendentals=0),
-    )(*pieces)
+        cost_estimate=pl.CostEstimate(flops=G_FLOPS, bytes_accessed=2**21, transcendentals=0),
+    )(left)
 
 
 def halves(blocks, top_ref, low_ref):
@@ -136,12 +138,11 @@
     left = lax.ppermute(integrals, RING, RIGHT)
     right_low = lax.ppermute(low, RING, LEFT)
     right_top = lax.ppermute(top, RING, LEFT)
-    (left_top,) = kept(G_FLOPS, left, rows=SPLIT)
-    (right_low,) = kept(B_FLOPS, right_low)
+    left_top = kept(left)
     far_top = lax.ppermute(left_top, RING, RIGHT)
     far_low = lax.ppermute(right_low, RING, LEFT)
     raw = lax.all_to_all(amplitudes.reshape(2, 128, 2560), ("z", "core", "y"), split_axis=1, concat_axis=1, tiled=True)
-    raw, _, _ = lax.optimization_barrier((raw, left_top, right_low))
+    raw, _ = lax.optimization_barrier((raw, left_top))
     raw_other = lax.ppermute(raw, "core", SWAP)
     near = (integrals, left, right_top, right_low)
     own, first = run(own_near, FLOPS, [ROWS, SUMS], [], raw.transpose(1, 0, 2), *near)

time: 104 us -> 104 us (level)
    all_to_all x1, waiting for transfers between devices: 13.9 us -> 16.2 us  [shards(): lax.all_to_all(amplitudes.reshape(2, 128, 2560), ('z', 'core', 'y'), spli...]
    ppermute x1, waiting for transfers between devices: 5.17 us -> 3.76 us  [shards(): right_low = lax.ppermute(low, RING, LEFT)]
    pallas_call x2 -> x1, Pallas kernels: 3.09 us -> 2.15 us  [kept(): pl.pallas_call(keep, out_shape=jax.ShapeDtypeStruct((SPLIT, 256), jnp.bfl...]
  transfers between devices with their start and end apart: 7 -> 7, of which waited for: 3 -> 3; matrix products, arithmetic and copies ran while one was open for 0% -> 0% of each run, Pallas kernels for 9% -> 8%
where the time goes in v7:
time: 104 us; the launch traced here: 103 us
  starting transfers between devices  36.9 us (35%)
  blocking collectives  35.5 us (34%)
  waiting for transfers between devices  20.2 us (19%)
  Pallas kernels  9.84 us (9%)
    all_to_all x1, blocking collectives, shards(): lax.all_to_all(partial, ('z', 'core', 'y'), split_axis=0, concat_axis=0,...  35.5 us
    all_to_all x1, starting transfers between devices, shards(): lax.all_to_all(amplitudes.reshape(2, 128, 2560), ('z', 'core', 'y'), spli...  18 us
    all_to_all x1, waiting for transfers between devices, shards(): lax.all_to_all(amplitudes.reshape(2, 128, 2560), ('z', 'core', 'y'), spli...  16.2 us
    pallas_call x3, Pallas kernels, run(): pl.pallas_call(kernel, out_shape=outs, in_specs=[VMEM] * len(operands), o...  6.66 us
    ppermute x1, starting transfers between devices, shards(): far_low = lax.ppermute(right_low, RING, LEFT)  4.47 us
    ppermute x1, starting transfers between devices, shards(): left = lax.ppermute(integrals, RING, RIGHT)  3.94 us
    ppermute x1, waiting for transfers between devices, shards(): right_low = lax.ppermute(low, RING, LEFT)  3.76 us
    ppermute x1, starting transfers between devices, shards(): right_low = lax.ppermute(low, RING, LEFT)  3.36 us
  transfers between devices with their start and end apart: 7, of which 3 were waited for; matrix products, arithmetic and copies ran while one was open for 0% of the time, Pallas kernels for 8%

profile of v7, /device:TPU:1, one launch (start us, length us, event | category | flops | bytes accessed | tf_op | source)
XLA Modules:
  0.0 103.3 jit_solution(9939980553985558081)
XLA Ops:
  0.0 3.9 %collective-permute-start = (bf16[2560,256]{1,0:T(8,128)(2,1)}, bf16[2560,256]{1,0:T(8,128)(2,1)}, u32[]{:S(2)}, u32[]{:S(2)}) collective-permute-start(bf16[2560,256]{1,0:T(8,128)(2,1)} %refs_0_.3), channel_id=1, source_target_pairs={{0,8},{8,256},{256,264},{264,0},{1,9},{9,257},{257,265},{265,1},{2... | collective-permute-start | bytes 3932168 | tf_op jit(solution)/shard_map/ppermute | solution.py:138
  3.9 0.0 copy-start
  4.0 18.0 %all-to-all-start = ((bf16[2,128,2560]{2,0,1:T(2,128)(2,1)}), bf16[2,128,2560]{2,0,1:T(2,128)(2,1)S(1)}, u32[]{:S(2)}, u32[]{:S(2)}) async-start(bf16[2,128,2560]{2,0,1:T(2,128)(2,1)} %bitcast.10), calls=%async_computation | async-start | bytes 2621440 | tf_op jit(solution)/shard_map/all_to_all | solution.py:144
  22.0 0.0 copy-done
  22.0 1.0 shard_map.29
  23.0 3.4 %collective-permute-start.2 = (bf16[640,256]{1,0:T(8,128)(2,1)S(1)}, bf16[640,256]{1,0:T(8,128)(2,1)S(1)}, u32[]{:S(2)}, u32[]{:S(2)}) collective-permute-start(bf16[640,256]{1,0:T(8,128)(2,1)S(1)} %get-tuple-element.14), channel_id=1, source_target_pairs={{0,264},{8,0},{256,8},{264,256},{1,265},{9,1},{257,9},{265,257},{2... | collective-permute-start | bytes 983048 | tf_op jit(solution)/shard_map/ppermute | solution.py:139
  26.4 3.2 %collective-permute-start.1 = (bf16[1920,256]{1,0:T(8,128)(2,1)}, bf16[1920,256]{1,0:T(8,128)(2,1)}, u32[]{:S(2)}, u32[]{:S(2)}) collective-permute-start(bf16[1920,256]{1,0:T(8,128)(2,1)} %get-tuple-element.13), channel_id=1, source_target_pairs={{0,264},{8,0},{256,8},{264,256},{1,265},{9,1},{257,9},{265,257},{2... | collective-permute-start | bytes 2949128 | tf_op jit(solution)/shard_map/ppermute | solution.py:140
  29.6 3.8 %collective-permute-done.2.refs_3_ = bf16[640,256]{1,0:T(8,128)(2,1)S(1)} collective-permute-done((bf16[640,256]{1,0:T(8,128)(2,1)S(1)}, bf16[640,256]{1,0:T(8,128)(2,1)S(1)}, u32[]{:S(2)}, u32[]{:S(2)}) %collective-permute-start.2) | collective-permute-done | bytes 327712 | tf_op jit(solution)/shard_map/ppermute | solution.py:139
  33.3 4.5 %collective-permute-start.5 = (bf16[640,256]{1,0:T(8,128)(2,1)S(1)}, bf16[640,256]{1,0:T(8,128)(2,1)S(1)}, u32[]{:S(2)}, u32[]{:S(2)}) collective-permute-start(bf16[640,256]{1,0:T(8,128)(2,1)S(1)} %collective-permute-done.2.refs_3_), channel_id=1, source_target_pairs={{0,264},{8,0},{256,8},{264,256},{1,265},{9,1},{257,9},{265,257},{2... | collective-permute-start | bytes 983048 | tf_op jit(solution)/shard_map/ppermute | solution.py:143
  37.8 0.0 collective-permute-done.left.refs_1_
  37.8 2.2 %shard_map.28 = bf16[1920,256]{1,0:T(8,128)(2,1)} custom-call(bf16[2560,256]{1,0:T(8,128)(2,1)} %collective-permute-done.left.refs_1_), custom_call_target="tpu_custom_call" | custom-call | flops 17999998976 | bytes 2097152 | tf_op jit(solution)/shard_map/pallas_call | solution.py:29
  40.0 1.9 %collective-permute-start.4 = (bf16[1920,256]{1,0:T(8,128)(2,1)}, bf16[1920,256]{1,0:T(8,128)(2,1)}, u32[]{:S(2)}, u32[]{:S(2)}) collective-permute-start(bf16[1920,256]{1,0:T(8,128)(2,1)} %shard_map.28), channel_id=1, source_target_pairs={{0,8},{8,256},{256,264},{264,0},{1,9},{9,257},{257,265},{265,1},{2... | collective-permute-start | bytes 2949128 | tf_op jit(solution)/shard_map/ppermute | solution.py:142
  41.9 16.2 %all-to-all-done = bf16[2,128,2560]{2,0,1:T(2,128)(2,1)S(1)} async-done(((bf16[2,128,2560]{2,0,1:T(2,128)(2,1)}), bf16[2,128,2560]{2,0,1:T(2,128)(2,1)S(1)}, u32[]{:S(2)}, u32[]{:S(2)}) %all-to-all-start) | async-done | bytes 1310752 | tf_op jit(solution)/shard_map/all_to_all | solution.py:144
  58.1 2.0 %collective-permute-start.3 = (bf16[2,128,2560]{2,0,1:T(2,128)(2,1)S(1)}, bf16[2,128,2560]{2,0,1:T(2,128)(2,1)S(1)}, u32[]{:S(2)}, u32[]{:S(2)}) collective-permute-start(bf16[2,128,2560]{2,0,1:T(2,128)(2,1)S(1)} %all-to-all-done), channel_id=1, source_target_pairs={{0,128},{128,0},{1,129},{129,1},{2,130},{130,2},{3,131},{131,3},{4... | collective-permute-start | bytes 3932168 | tf_op jit(solution)/shard_map/ppermute | solution.py:146
  60.1 0.0 collective-permute-done.1.refs_2_
  60.1 2.6 %shard_map.30 = (bf16[256,2560]{1,0:T(8,128)(2,1)S(1)}, f32[2,256,256]{2,1,0:T(8,128)S(1)}) custom-call(bf16[128,2,2560]{2,1,0:T(2,128)(2,1)S(1)} %bitcast.7, bf16[2560,256]{1,0:T(8,128)(2,1)S(1)} %copy-done, bf16[2560,256]{1,0:T(8,128)(2,1)} %collective-permute-done.left.refs_1_, bf16[1920,256]{1,0:T(8,128)(2,1)} %collective-permute-done.1.refs_2_, ...), custom_call_target="tpu_custom_call" | custom-call | flops 99999997952 | bytes 4194304 | tf_op jit(solution)/shard_map/pallas_call | solution.py:125
  62.7 0.3 collective-permute-done.3
  63.0 2.2 %shard_map.31 = (bf16[256,2560]{1,0:T(8,128)(2,1)S(1)}, f32[2,256,256]{2,1,0:T(8,128)S(1)}) custom-call(f32[2,256,256]{2,1,0:T(8,128)S(1)} %get-tuple-element.15.first_ref, bf16[128,2,2560]{2,1,0:T(2,128)(2,1)S(1)} %bitcast.8, bf16[2560,256]{1,0:T(8,128)(2,1)S(1)} %copy-done, bf16[2560,256]{1,0:T(8,128)(2,1)} %collective-permute-done.left.refs_1_, ...), custom_call_target="tpu_custom_call" | custom-call | flops 4000000000 | bytes 4194304 | tf_op jit(solution)/shard_map/pallas_call | solution.py:125
  65.3 0.0 collective-permute-done.5.far_low
  65.3 0.0 collective-permute-done.4.far_top
  65.3 1.8 %shard_map.32 = f32[1024,128]{1,0:T(8,128)S(1)} custom-call(f32[2,256,256]{2,1,0:T(8,128)S(1)} %get-tuple-element.16.near_ref, bf16[256,2560]{1,0:T(8,128)(2,1)S(1)} %get-tuple-element.17.own, bf16[256,2560]{1,0:T(8,128)(2,1)S(1)} %get-tuple-element.18.other, bf16[1920,256]{1,0:T(8,128)(2,1)} %collective-permute-done.4.far_top, ...), custom_call_target="tpu_custom_call" | custom-call | flops 1000000000 | bytes 4194304 | tf_op jit(solution)/shard_map/pallas_call | solution.py:125
  67.1 35.5 %all_to_all.10 = f32[128,8,128]{2,1,0:T(8,128)S(1)} all-to-all(f32[128,8,128]{2,1,0:T(8,128)S(1)} %bitcast.6), channel_id=1, replica_groups=mesh['xh'=2,'core'=2,'z'=8,'xl'=2,'y'=8] {'z','core','y'}, dimensions={0} | all-to-all | bytes 1048576 | tf_op jit(solution)/shard_map/all_to_all | solution.py:154
  102.6 0.1 reduce_sum.9
  102.7 0.6 reshape.19
  (3 shorter events, 0.0 us)
Async XLA Ops:
  0.0 37.8 %collective-permute-start = (bf16[2560,256]{1,0:T(8,128)(2,1)}, bf16[2560,256]{1,0:T(8,128)(2,1)}, u32[]{:S(2)}, u32[]{:S(2)}) collective-permute-start(bf16[2560,256]{1,0:T(8,128)(2,1)} %refs_0_.3), channel_id=1, source_target_pairs={{0,8},{8,256},{256,264},{264,0},{1,9},{9,257},{257,265},{265,1},{2... | collective-permute-start | bytes 3932168 | tf_op jit(solution)/shard_map/ppermute | solution.py:138
  3.9 18.0 %copy-start = (bf16[2560,256]{1,0:T(8,128)(2,1)S(1)}, bf16[2560,256]{1,0:T(8,128)(2,1)}, u32[]{:S(2)}) copy-start(bf16[2560,256]{1,0:T(8,128)(2,1)} %refs_0_.3) | copy-start | bytes 3932164
  4.0 54.1 %all-to-all-start = ((bf16[2,128,2560]{2,0,1:T(2,128)(2,1)}), bf16[2,128,2560]{2,0,1:T(2,128)(2,1)S(1)}, u32[]{:S(2)}, u32[]{:S(2)}) async-start(bf16[2,128,2560]{2,0,1:T(2,128)(2,1)} %bitcast.10), calls=%async_computation | async-start | bytes 2621440 | tf_op jit(solution)/shard_map/all_to_all | solution.py:144
  23.0 10.3 %collective-permute-start.2 = (bf16[640,256]{1,0:T(8,128)(2,1)S(1)}, bf16[640,256]{1,0:T(8,128)(2,1)S(1)}, u32[]{:S(2)}, u32[]{:S(2)}) collective-permute-start(bf16[640,256]{1,0:T(8,128)(2,1)S(1)} %get-tuple-element.14), channel_id=1, source_target_pairs={{0,264},{8,0},{256,8},{264,256},{1,265},{9,1},{257,9},{265,257},{2... | collective-permute-start | bytes 983048 | tf_op jit(solution)/shard_map/ppermute | solution.py:139
  26.4 33.7 %collective-permute-start.1 = (bf16[1920,256]{1,0:T(8,128)(2,1)}, bf16[1920,256]{1,0:T(8,128)(2,1)}, u32[]{:S(2)}, u32[]{:S(2)}) collective-permute-start(bf16[1920,256]{1,0:T(8,128)(2,1)} %get-tuple-element.13), channel_id=1, source_target_pairs={{0,264},{8,0},{256,8},{264,256},{1,265},{9,1},{257,9},{265,257},{2... | collective-permute-start | bytes 2949128 | tf_op jit(solution)/shard_map/ppermute | solution.py:140
  33.3 31.9 %collective-permute-start.5 = (bf16[640,256]{1,0:T(8,128)(2,1)S(1)}, bf16[640,256]{1,0:T(8,128)(2,1)S(1)}, u32[]{:S(2)}, u32[]{:S(2)}) collective-permute-start(bf16[640,256]{1,0:T(8,128)(2,1)S(1)} %collective-permute-done.2.refs_3_), channel_id=1, source_target_pairs={{0,264},{8,0},{256,8},{264,256},{1,265},{9,1},{257,9},{265,257},{2... | collective-permute-start | bytes 983048 | tf_op jit(solution)/shard_map/ppermute | solution.py:143
  40.0 25.3 %collective-permute-start.4 = (bf16[1920,256]{1,0:T(8,128)(2,1)}, bf16[1920,256]{1,0:T(8,128)(2,1)}, u32[]{:S(2)}, u32[]{:S(2)}) collective-permute-start(bf16[1920,256]{1,0:T(8,128)(2,1)} %shard_map.28), channel_id=1, source_target_pairs={{0,8},{8,256},{256,264},{264,0},{1,9},{9,257},{257,265},{265,1},{2... | collective-permute-start | bytes 2949128 | tf_op jit(solution)/shard_map/ppermute | solution.py:142
  58.1 4.9 %collective-permute-start.3 = (bf16[2,128,2560]{2,0,1:T(2,128)(2,1)S(1)}, bf16[2,128,2560]{2,0,1:T(2,128)(2,1)S(1)}, u32[]{:S(2)}, u32[]{:S(2)}) collective-permute-start(bf16[2,128,2560]{2,0,1:T(2,128)(2,1)S(1)} %all-to-all-done), channel_id=1, source_target_pairs={{0,128},{128,0},{1,129},{129,1},{2,130},{130,2},{3,131},{131,3},{4... | collective-permute-start | bytes 3932168 | tf_op jit(solution)/shard_map/ppermute | solution.py:146

commit v8 on v7

--- a/solution.py
+++ b/solution.py
@@ -13,7 +13,7 @@
 ANY = pl.BlockSpec(memory_space=pl.ANY)
 LIMIT = 20 * 2**20
 H_LIMIT = 8 * 2**20
-SPLIT = 1920
+SPLIT = 1792
 G_FLOPS = 18 * 10**9
 FLOPS = 10**11
 N_FLOPS = 4 * 10**9
@@ -113,8 +113,11 @@
         sum_ref[1 - xh] = near_ref[1 - xh] + times(other, (far_top, far_low))
 
     for block in range(2):
-        for half in range(2):
-            out_ref[pl.ds(2 * block + half, 256, stride=4), :] = sum_ref[block, :, 128 * half : 128 * half + 128]
+        total = sum_ref[block].reshape(8, 2, 16, 256)
+        for core in range(2):
+            for half in range(2):
+                piece = total[:, core, :, 128 * half : 128 * half + 128].reshape(128, 128)
+                out_ref[pl.ds(512 * core + 2 * block + half, 128, stride=4), :] = piece
 
 
 SUMS = jax.ShapeDtypeStruct((2, 256, 256), jnp.float32)
@@ -151,8 +154,8 @@
     scratch = [pltpu.VMEM((2, 256, 256), jnp.float32)]
     (partial,) = run(with_far, 10**9, [partial], scratch, second, own, other, far_top, far_low)
     partial = partial.reshape(128, 8, 128)
-    parts = lax.all_to_all(partial, ("z", "core", "y"), split_axis=0, concat_axis=0, tiled=True)
-    total = 0.5 * jnp.sum(parts.reshape(8, 2, 8, 8, 128), axis=(0, 2))
+    parts = lax.all_to_all(partial, ("core", "z", "y"), split_axis=0, concat_axis=0, tiled=True)
+    total = 0.5 * jnp.sum(parts.reshape(2, 64, 8, 128), axis=1)
     return total.reshape(2, 2, 2, 256).transpose(1, 2, 0, 3).reshape(2, 1024)
 
 

time: 104 us -> 105 us (level)
  blocking collectives: 35.5 us -> 36.9 us
    all_to_all x1, waiting for transfers between devices: 16.2 us -> 14.7 us  [shards(): lax.all_to_all(amplitudes.reshape(2, 128, 2560), ('z', 'core', 'y'), spli...]
    all_to_all x1, blocking collectives: 35.5 us -> 36.9 us  [shards(): lax.all_to_all(partial, ('core', 'z', 'y'), split_axis=0, concat_axis=0,...]
    ppermute x1, waiting for transfers between devices: 3.76 us -> 5.17 us  [shards(): right_low = lax.ppermute(low, RING, LEFT)]
where the time goes in v8:
time: 105 us
  starting transfers between devices  37 us (35%)
  blocking collectives  36.9 us (35%)
  waiting for transfers between devices  20.1 us (19%)
  Pallas kernels  9.69 us (9%)
    all_to_all x1, blocking collectives, shards(): lax.all_to_all(partial, ('core', 'z', 'y'), split_axis=0, concat_axis=0,...  36.9 us
    all_to_all x1, starting transfers between devices, shards(): lax.all_to_all(amplitudes.reshape(2, 128, 2560), ('z', 'core', 'y'), spli...  18 us
    all_to_all x1, waiting for transfers between devices, shards(): lax.all_to_all(amplitudes.reshape(2, 128, 2560), ('z', 'core', 'y'), spli...  14.7 us
    pallas_call x3, Pallas kernels, run(): pl.pallas_call(kernel, out_shape=outs, in_specs=[VMEM] * len(operands), o...  6.54 us
    ppermute x1, waiting for transfers between devices, shards(): right_low = lax.ppermute(low, RING, LEFT)  5.17 us
    ppermute x1, starting transfers between devices, shards(): far_low = lax.ppermute(right_low, RING, LEFT)  4.57 us
    ppermute x1, starting transfers between devices, shards(): left = lax.ppermute(integrals, RING, RIGHT)  3.94 us
    ppermute x1, starting transfers between devices, shards(): right_low = lax.ppermute(low, RING, LEFT)  3.36 us
  transfers between devices with their start and end apart: 7, of which 3 were waited for; matrix products, arithmetic and copies ran while one was open for 0% of the time, Pallas kernels for 8%

profile of v8, /device:TPU:1, one launch (start us, length us, event | category | flops | bytes accessed | tf_op | source)
XLA Modules:
  0.0 104.6 jit_solution(3969069991222816328)
XLA Ops:
  0.0 3.9 %collective-permute-start = (bf16[2560,256]{1,0:T(8,128)(2,1)}, bf16[2560,256]{1,0:T(8,128)(2,1)}, u32[]{:S(2)}, u32[]{:S(2)}) collective-permute-start(bf16[2560,256]{1,0:T(8,128)(2,1)} %refs_0_.3), channel_id=1, source_target_pairs={{0,8},{8,256},{256,264},{264,0},{1,9},{9,257},{257,265},{265,1},{2... | collective-permute-start | bytes 3932168 | tf_op jit(solution)/shard_map/ppermute | solution.py:141
  3.9 0.0 copy-start
  4.0 18.0 %all-to-all-start = ((bf16[2,128,2560]{2,0,1:T(2,128)(2,1)}), bf16[2,128,2560]{2,0,1:T(2,128)(2,1)S(1)}, u32[]{:S(2)}, u32[]{:S(2)}) async-start(bf16[2,128,2560]{2,0,1:T(2,128)(2,1)} %bitcast.10), calls=%async_computation | async-start | bytes 2621440 | tf_op jit(solution)/shard_map/all_to_all | solution.py:147
  22.0 0.0 copy-done
  22.0 1.0 shard_map.29
  23.0 3.4 %collective-permute-start.2 = (bf16[768,256]{1,0:T(8,128)(2,1)S(1)}, bf16[768,256]{1,0:T(8,128)(2,1)}, u32[]{:S(2)}, u32[]{:S(2)}) collective-permute-start(bf16[768,256]{1,0:T(8,128)(2,1)S(1)} %get-tuple-element.14), channel_id=1, source_target_pairs={{0,264},{8,0},{256,8},{264,256},{1,265},{9,1},{257,9},{265,257},{2... | collective-permute-start | bytes 1179656 | tf_op jit(solution)/shard_map/ppermute | solution.py:142
  26.4 3.2 %collective-permute-start.1 = (bf16[1792,256]{1,0:T(8,128)(2,1)}, bf16[1792,256]{1,0:T(8,128)(2,1)}, u32[]{:S(2)}, u32[]{:S(2)}) collective-permute-start(bf16[1792,256]{1,0:T(8,128)(2,1)} %get-tuple-element.13), channel_id=1, source_target_pairs={{0,264},{8,0},{256,8},{264,256},{1,265},{9,1},{257,9},{265,257},{2... | collective-permute-start | bytes 2752520 | tf_op jit(solution)/shard_map/ppermute | solution.py:143
  29.6 5.2 %collective-permute-done.2.refs_3_ = bf16[768,256]{1,0:T(8,128)(2,1)} collective-permute-done((bf16[768,256]{1,0:T(8,128)(2,1)S(1)}, bf16[768,256]{1,0:T(8,128)(2,1)}, u32[]{:S(2)}, u32[]{:S(2)}) %collective-permute-start.2) | collective-permute-done | bytes 393248 | tf_op jit(solution)/shard_map/ppermute | solution.py:142
  34.7 4.6 %collective-permute-start.5 = (bf16[768,256]{1,0:T(8,128)(2,1)}, bf16[768,256]{1,0:T(8,128)(2,1)}, u32[]{:S(2)}, u32[]{:S(2)}) collective-permute-start(bf16[768,256]{1,0:T(8,128)(2,1)} %collective-permute-done.2.refs_3_), channel_id=1, source_target_pairs={{0,264},{8,0},{256,8},{264,256},{1,265},{9,1},{257,9},{265,257},{2... | collective-permute-start | bytes 1179656 | tf_op jit(solution)/shard_map/ppermute | solution.py:146
  39.3 0.0 collective-permute-done.left.refs_1_
  39.3 2.1 %shard_map.28 = bf16[1792,256]{1,0:T(8,128)(2,1)} custom-call(bf16[2560,256]{1,0:T(8,128)(2,1)} %collective-permute-done.left.refs_1_), custom_call_target="tpu_custom_call" | custom-call | flops 17999998976 | bytes 2097152 | tf_op jit(solution)/shard_map/pallas_call | solution.py:29
  41.5 1.9 %collective-permute-start.4 = (bf16[1792,256]{1,0:T(8,128)(2,1)}, bf16[1792,256]{1,0:T(8,128)(2,1)S(1)}, u32[]{:S(2)}, u32[]{:S(2)}) collective-permute-start(bf16[1792,256]{1,0:T(8,128)(2,1)} %shard_map.28), channel_id=1, source_target_pairs={{0,8},{8,256},{256,264},{264,0},{1,9},{9,257},{257,265},{265,1},{2... | collective-permute-start | bytes 2752520 | tf_op jit(solution)/shard_map/ppermute | solution.py:145
  43.4 14.7 %all-to-all-done = bf16[2,128,2560]{2,0,1:T(2,128)(2,1)S(1)} async-done(((bf16[2,128,2560]{2,0,1:T(2,128)(2,1)}), bf16[2,128,2560]{2,0,1:T(2,128)(2,1)S(1)}, u32[]{:S(2)}, u32[]{:S(2)}) %all-to-all-start) | async-done | bytes 1310752 | tf_op jit(solution)/shard_map/all_to_all | solution.py:147
  58.1 2.0 %collective-permute-start.3 = (bf16[2,128,2560]{2,0,1:T(2,128)(2,1)S(1)}, bf16[2,128,2560]{2,0,1:T(2,128)(2,1)S(1)}, u32[]{:S(2)}, u32[]{:S(2)}) collective-permute-start(bf16[2,128,2560]{2,0,1:T(2,128)(2,1)S(1)} %all-to-all-done), channel_id=1, source_target_pairs={{0,128},{128,0},{1,129},{129,1},{2,130},{130,2},{3,131},{131,3},{4... | collective-permute-start | bytes 3932168 | tf_op jit(solution)/shard_map/ppermute | solution.py:149
  60.1 0.0 collective-permute-done.1.refs_2_
  60.1 2.7 %shard_map.30 = (bf16[256,2560]{1,0:T(8,128)(2,1)S(1)}, f32[2,256,256]{2,1,0:T(8,128)S(1)}) custom-call(bf16[128,2,2560]{2,1,0:T(2,128)(2,1)S(1)} %bitcast.8, bf16[2560,256]{1,0:T(8,128)(2,1)S(1)} %copy-done, bf16[2560,256]{1,0:T(8,128)(2,1)} %collective-permute-done.left.refs_1_, bf16[1792,256]{1,0:T(8,128)(2,1)} %collective-permute-done.1.refs_2_, ...), custom_call_target="tpu_custom_call" | custom-call | flops 99999997952 | bytes 4194304 | tf_op jit(solution)/shard_map/pallas_call | solution.py:128
  62.8 0.2 collective-permute-done.3
  63.0 2.3 %shard_map.31 = (bf16[256,2560]{1,0:T(8,128)(2,1)S(1)}, f32[2,256,256]{2,1,0:T(8,128)S(1)}) custom-call(f32[2,256,256]{2,1,0:T(8,128)S(1)} %get-tuple-element.15.first_ref, bf16[128,2,2560]{2,1,0:T(2,128)(2,1)S(1)} %bitcast.9, bf16[2560,256]{1,0:T(8,128)(2,1)S(1)} %copy-done, bf16[2560,256]{1,0:T(8,128)(2,1)} %collective-permute-done.left.refs_1_, ...), custom_call_target="tpu_custom_call" | custom-call | flops 4000000000 | bytes 4194304 | tf_op jit(solution)/shard_map/pallas_call | solution.py:128
  65.3 0.0 collective-permute-done.5.far_low
  65.3 0.0 collective-permute-done.4.far_top
  65.4 1.6 %shard_map.32 = f32[1024,128]{1,0:T(8,128)S(1)} custom-call(f32[2,256,256]{2,1,0:T(8,128)S(1)} %get-tuple-element.16.near_ref, bf16[256,2560]{1,0:T(8,128)(2,1)S(1)} %get-tuple-element.17.own, bf16[256,2560]{1,0:T(8,128)(2,1)S(1)} %get-tuple-element.18.other, bf16[1792,256]{1,0:T(8,128)(2,1)S(1)} %collective-permute-done.4.far_top, ...), custom_call_target="tpu_custom_call" | custom-call | flops 1000000000 | bytes 4194304 | tf_op jit(solution)/shard_map/pallas_call | solution.py:128
  66.9 36.9 %all_to_all.10 = f32[128,8,128]{2,1,0:T(8,128)S(1)} all-to-all(f32[128,8,128]{2,1,0:T(8,128)S(1)} %bitcast.7), channel_id=1, replica_groups=mesh['xh'=2,'core'=2,'z'=8,'xl'=2,'y'=8] {'core','z','y'}, dimensions={0} | all-to-all | bytes 1048576 | tf_op jit(solution)/shard_map/all_to_all | solution.py:157
  103.9 0.1 bitcast_reduce_fusion
  104.0 0.6 reshape.19
  (3 shorter events, 0.0 us)
Async XLA Ops:
  0.0 39.3 %collective-permute-start = (bf16[2560,256]{1,0:T(8,128)(2,1)}, bf16[2560,256]{1,0:T(8,128)(2,1)}, u32[]{:S(2)}, u32[]{:S(2)}) collective-permute-start(bf16[2560,256]{1,0:T(8,128)(2,1)} %refs_0_.3), channel_id=1, source_target_pairs={{0,8},{8,256},{256,264},{264,0},{1,9},{9,257},{257,265},{265,1},{2... | collective-permute-start | bytes 3932168 | tf_op jit(solution)/shard_map/ppermute | solution.py:141
  3.9 18.0 %copy-start = (bf16[2560,256]{1,0:T(8,128)(2,1)S(1)}, bf16[2560,256]{1,0:T(8,128)(2,1)}, u32[]{:S(2)}) copy-start(bf16[2560,256]{1,0:T(8,128)(2,1)} %refs_0_.3) | copy-start | bytes 3932164
  4.0 54.1 %all-to-all-start = ((bf16[2,128,2560]{2,0,1:T(2,128)(2,1)}), bf16[2,128,2560]{2,0,1:T(2,128)(2,1)S(1)}, u32[]{:S(2)}, u32[]{:S(2)}) async-start(bf16[2,128,2560]{2,0,1:T(2,128)(2,1)} %bitcast.10), calls=%async_computation | async-start | bytes 2621440 | tf_op jit(solution)/shard_map/all_to_all | solution.py:147
  23.0 11.7 %collective-permute-start.2 = (bf16[768,256]{1,0:T(8,128)(2,1)S(1)}, bf16[768,256]{1,0:T(8,128)(2,1)}, u32[]{:S(2)}, u32[]{:S(2)}) collective-permute-start(bf16[768,256]{1,0:T(8,128)(2,1)S(1)} %get-tuple-element.14), channel_id=1, source_target_pairs={{0,264},{8,0},{256,8},{264,256},{1,265},{9,1},{257,9},{265,257},{2... | collective-permute-start | bytes 1179656 | tf_op jit(solution)/shard_map/ppermute | solution.py:142
  26.4 33.7 %collective-permute-start.1 = (bf16[1792,256]{1,0:T(8,128)(2,1)}, bf16[1792,256]{1,0:T(8,128)(2,1)}, u32[]{:S(2)}, u32[]{:S(2)}) collective-permute-start(bf16[1792,256]{1,0:T(8,128)(2,1)} %get-tuple-element.13), channel_id=1, source_target_pairs={{0,264},{8,0},{256,8},{264,256},{1,265},{9,1},{257,9},{265,257},{2... | collective-permute-start | bytes 2752520 | tf_op jit(solution)/shard_map/ppermute | solution.py:143
  34.7 30.6 %collective-permute-start.5 = (bf16[768,256]{1,0:T(8,128)(2,1)}, bf16[768,256]{1,0:T(8,128)(2,1)}, u32[]{:S(2)}, u32[]{:S(2)}) collective-permute-start(bf16[768,256]{1,0:T(8,128)(2,1)} %collective-permute-done.2.refs_3_), channel_id=1, source_target_pairs={{0,264},{8,0},{256,8},{264,256},{1,265},{9,1},{257,9},{265,257},{2... | collective-permute-start | bytes 1179656 | tf_op jit(solution)/shard_map/ppermute | solution.py:146
  41.5 23.9 %collective-permute-start.4 = (bf16[1792,256]{1,0:T(8,128)(2,1)}, bf16[1792,256]{1,0:T(8,128)(2,1)S(1)}, u32[]{:S(2)}, u32[]{:S(2)}) collective-permute-start(bf16[1792,256]{1,0:T(8,128)(2,1)} %shard_map.28), channel_id=1, source_target_pairs={{0,8},{8,256},{256,264},{264,0},{1,9},{9,257},{257,265},{265,1},{2... | collective-permute-start | bytes 2752520 | tf_op jit(solution)/shard_map/ppermute | solution.py:145
  58.1 4.9 %collective-permute-start.3 = (bf16[2,128,2560]{2,0,1:T(2,128)(2,1)S(1)}, bf16[2,128,2560]{2,0,1:T(2,128)(2,1)S(1)}, u32[]{:S(2)}, u32[]{:S(2)}) collective-permute-start(bf16[2,128,2560]{2,0,1:T(2,128)(2,1)S(1)} %all-to-all-done), channel_id=1, source_target_pairs={{0,128},{128,0},{1,129},{129,1},{2,130},{130,2},{3,131},{131,3},{4... | collective-permute-start | bytes 3932168 | tf_op jit(solution)/shard_map/ppermute | solution.py:149

commit v9 on v8

--- a/solution.py
+++ b/solution.py
@@ -16,6 +16,8 @@
 SPLIT = 1792
 G_FLOPS = 18 * 10**9
 FLOPS = 10**11
+L_FLOPS = 10**9
+B_FLOPS = 10**9
 N_FLOPS = 4 * 10**9
 
 
@@ -35,6 +37,21 @@
         compiler_params=pltpu.CompilerParams(vmem_limit_bytes=H_LIMIT),
         cost_estimate=pl.CostEstimate(flops=G_FLOPS, bytes_accessed=2**21, transcendentals=0),
     )(left)
+
+
+def follow(right_low, left_top, low_ref):
+    low_ref[...] = right_low[...]
+
+
+def followed(right_low, left_top):
+    return pl.pallas_call(
+        follow,
+        out_shape=jax.ShapeDtypeStruct(right_low.shape, right_low.dtype),
+        in_specs=[VMEM, ANY],
+        out_specs=VMEM,
+        compiler_params=pltpu.CompilerParams(vmem_limit_bytes=H_LIMIT),
+        cost_estimate=pl.CostEstimate(flops=B_FLOPS, bytes_accessed=2**20, transcendentals=0),
+    )(right_low, left_top)
 
 
 def halves(blocks, top_ref, low_ref):
@@ -100,17 +117,30 @@
         sum_ref[1 - xh] = first_ref[1 - xh]
 
 
-def with_far(near_ref, own, other, far_top, far_low, out_ref, sum_ref):
+def with_far_top(near_ref, own, other, far_top, sum_ref):
     xh = lax.axis_index("xh")
     sum_ref[xh] = near_ref[xh]
 
     @pl.when(same())
     def _():
-        sum_ref[1 - xh] = near_ref[1 - xh] + times(own, (far_top, far_low))
+        sum_ref[1 - xh] = near_ref[1 - xh] + jnp.dot(own[:, :SPLIT], far_top[...], preferred_element_type=jnp.float32)
 
     @pl.when(jnp.logical_not(same()))
     def _():
-        sum_ref[1 - xh] = near_ref[1 - xh] + times(other, (far_top, far_low))
+        sum_ref[1 - xh] = near_ref[1 - xh] + jnp.dot(other[:, :SPLIT], far_top[...], preferred_element_type=jnp.float32)
+
+
+def with_far_low(most_ref, own, other, far_low, out_ref, sum_ref):
+    xh = lax.axis_index("xh")
+    sum_ref[xh] = most_ref[xh]
+
+    @pl.when(same())
+    def _():
+        sum_ref[1 - xh] = most_ref[1 - xh] + jnp.dot(own[:, SPLIT:], far_low[...], preferred_element_type=jnp.float32)
+
+    @pl.when(jnp.logical_not(same()))
+    def _():
+        sum_ref[1 - xh] = most_ref[1 - xh] + jnp.dot(other[:, SPLIT:], far_low[...], preferred_element_type=jnp.float32)
 
     for block in range(2):
         total = sum_ref[block].reshape(8, 2, 16, 256)
@@ -142,6 +172,7 @@
     right_low = lax.ppermute(low, RING, LEFT)
     right_top = lax.ppermute(top, RING, LEFT)
     left_top = kept(left)
+    right_low = followed(right_low, left_top)
     far_top = lax.ppermute(left_top, RING, RIGHT)
     far_low = lax.ppermute(right_low, RING, LEFT)
     raw = lax.all_to_all(amplitudes.reshape(2, 128, 2560), ("z", "core", "y"), split_axis=1, concat_axis=1, tiled=True)
@@ -152,7 +183,8 @@
     other, second = run(other_near, N_FLOPS, [ROWS, SUMS], [], first, raw_other.transpose(1, 0, 2), *near)
     partial = jax.ShapeDtypeStruct((1024, 128), jnp.float32)
     scratch = [pltpu.VMEM((2, 256, 256), jnp.float32)]
-    (partial,) = run(with_far, 10**9, [partial], scratch, second, own, other, far_top, far_low)
+    (third,) = run(with_far_top, 10**9, [SUMS], [], second, own, other, far_top)
+    (partial,) = run(with_far_low, L_FLOPS, [partial], scratch, third, own, other, far_low)
     partial = partial.reshape(128, 8, 128)
     parts = lax.all_to_all(partial, ("core", "z", "y"), split_axis=0, concat_axis=0, tiled=True)
     total = 0.5 * jnp.sum(parts.reshape(2, 64, 8, 128), axis=1)

time: 105 us -> 103 us (0.981)
  waiting for transfers between devices: 20.1 us -> 16.5 us
  starting transfers between devices: 37 us -> 39.9 us
  blocking collectives: 36.9 us -> 34.4 us
    ppermute x1, waiting for transfers between devices: 5.17 us -> 0.01 us  [shards(): right_low = lax.ppermute(low, RING, LEFT)]
    ppermute x1, starting transfers between devices: 1.92 us -> 5.22 us  [shards(): far_top = lax.ppermute(left_top, RING, RIGHT)]
    all_to_all x1, blocking collectives: 36.9 us -> 34.4 us  [shards(): lax.all_to_all(partial, ('core', 'z', 'y'), split_axis=0, concat_axis=0,...]
    all_to_all x1, waiting for transfers between devices: 14.7 us -> 16.2 us  [shards(): lax.all_to_all(amplitudes.reshape(2, 128, 2560), ('z', 'core', 'y'), spli...]
    pallas_call x3 -> x4, Pallas kernels: 6.54 us -> 6.74 us  [run(): pl.pallas_call(kernel, out_shape=outs, in_specs=[VMEM] * len(operands), o...]
  transfers between devices with their start and end apart: 7 -> 7, of which waited for: 3 -> 2; matrix products, arithmetic and copies ran while one was open for 0% -> 0% of each run, Pallas kernels for 8% -> 9%
where the time goes in v9:
time: 103 us; the launch traced here: 102 us
  starting transfers between devices  39.9 us (39%)
  blocking collectives  34.4 us (33%)
  waiting for transfers between devices  16.5 us (16%)
  Pallas kernels  10.6 us (10%)
    all_to_all x1, blocking collectives, shards(): lax.all_to_all(partial, ('core', 'z', 'y'), split_axis=0, concat_axis=0,...  34.4 us
    all_to_all x1, starting transfers between devices, shards(): lax.all_to_all(amplitudes.reshape(2, 128, 2560), ('z', 'core', 'y'), spli...  18 us
    all_to_all x1, waiting for transfers between devices, shards(): lax.all_to_all(amplitudes.reshape(2, 128, 2560), ('z', 'core', 'y'), spli...  16.2 us
    pallas_call x4, Pallas kernels, run(): pl.pallas_call(kernel, out_shape=outs, in_specs=[VMEM] * len(operands), o...  6.74 us
    ppermute x1, starting transfers between devices, shards(): far_top = lax.ppermute(left_top, RING, RIGHT)  5.22 us
    ppermute x1, starting transfers between devices, shards(): far_low = lax.ppermute(right_low, RING, LEFT)  4.17 us
    ppermute x1, starting transfers between devices, shards(): left = lax.ppermute(integrals, RING, RIGHT)  3.94 us
    ppermute x1, starting transfers between devices, shards(): right_low = lax.ppermute(low, RING, LEFT)  3.36 us
  transfers between devices with their start and end apart: 7, of which 2 were waited for; matrix products, arithmetic and copies ran while one was open for 0% of the time, Pallas kernels for 9%

profile of v9, /device:TPU:1, one launch (start us, length us, event | category | flops | bytes accessed | tf_op | source)
XLA Modules:
  0.0 102.3 jit_solution(8365868191954153801)
XLA Ops:
  0.0 3.9 %collective-permute-start = (bf16[2560,256]{1,0:T(8,128)(2,1)}, bf16[2560,256]{1,0:T(8,128)(2,1)}, u32[]{:S(2)}, u32[]{:S(2)}) collective-permute-start(bf16[2560,256]{1,0:T(8,128)(2,1)} %refs_0_.3), channel_id=1, source_target_pairs={{0,8},{8,256},{256,264},{264,0},{1,9},{9,257},{257,265},{265,1},{2... | collective-permute-start | bytes 3932168 | tf_op jit(solution)/shard_map/ppermute | solution.py:171
  4.0 18.0 %all-to-all-start = ((bf16[2,128,2560]{2,0,1:T(2,128)(2,1)}), bf16[2,128,2560]{2,0,1:T(2,128)(2,1)S(1)}, u32[]{:S(2)}, u32[]{:S(2)}) async-start(bf16[2,128,2560]{2,0,1:T(2,128)(2,1)} %bitcast.10), calls=%async_computation | async-start | bytes 2621440 | tf_op jit(solution)/shard_map/all_to_all | solution.py:178
  22.0 1.0 %shard_map.29 = (bf16[1792,256]{1,0:T(8,128)(2,1)}, bf16[768,256]{1,0:T(8,128)(2,1)S(1)}) custom-call(bf16[2560,256]{1,0:T(8,128)(2,1)S(1)} %copy-done), custom_call_target="tpu_custom_call" | custom-call | tf_op jit(solution)/shard_map/pallas_call | solution.py:63
  23.0 3.4 %collective-permute-start.2 = (bf16[768,256]{1,0:T(8,128)(2,1)S(1)}, bf16[768,256]{1,0:T(8,128)(2,1)S(1)}, u32[]{:S(2)}, u32[]{:S(2)}) collective-permute-start(bf16[768,256]{1,0:T(8,128)(2,1)S(1)} %get-tuple-element.14), channel_id=1, source_target_pairs={{0,264},{8,0},{256,8},{264,256},{1,265},{9,1},{257,9},{265,257},{2... | collective-permute-start | bytes 1179656 | tf_op jit(solution)/shard_map/ppermute | solution.py:172
  26.4 3.2 %collective-permute-start.1 = (bf16[1792,256]{1,0:T(8,128)(2,1)}, bf16[1792,256]{1,0:T(8,128)(2,1)}, u32[]{:S(2)}, u32[]{:S(2)}) collective-permute-start(bf16[1792,256]{1,0:T(8,128)(2,1)} %get-tuple-element.13), channel_id=1, source_target_pairs={{0,264},{8,0},{256,8},{264,256},{1,265},{9,1},{257,9},{265,257},{2... | collective-permute-start | bytes 2752520 | tf_op jit(solution)/shard_map/ppermute | solution.py:173
  29.6 0.0 collective-permute-done.left.refs_1_
  29.6 2.1 %shard_map.28.left_top = bf16[1792,256]{1,0:T(8,128)(2,1)} custom-call(bf16[2560,256]{1,0:T(8,128)(2,1)} %collective-permute-done.left.refs_1_), custom_call_target="tpu_custom_call" | custom-call | flops 17999998976 | bytes 2097152 | tf_op jit(solution)/shard_map/pallas_call | solution.py:31
  31.7 5.2 %collective-permute-start.4 = (bf16[1792,256]{1,0:T(8,128)(2,1)}, bf16[1792,256]{1,0:T(8,128)(2,1)S(1)}, u32[]{:S(2)}, u32[]{:S(2)}) collective-permute-start(bf16[1792,256]{1,0:T(8,128)(2,1)} %shard_map.28.left_top), channel_id=1, source_target_pairs={{0,8},{8,256},{256,264},{264,0},{1,9},{9,257},{257,265},{265,1},{2... | collective-permute-start | bytes 2752520 | tf_op jit(solution)/shard_map/ppermute | solution.py:176
  36.9 0.0 collective-permute-done.2.right_low
  36.9 0.8 shard_map.30.refs_3_
  37.7 4.2 %collective-permute-start.5 = (bf16[768,256]{1,0:T(8,128)(2,1)}, bf16[768,256]{1,0:T(8,128)(2,1)}, u32[]{:S(2)}, u32[]{:S(2)}) collective-permute-start(bf16[768,256]{1,0:T(8,128)(2,1)} %shard_map.30.refs_3_), channel_id=1, source_target_pairs={{0,264},{8,0},{256,8},{264,256},{1,265},{9,1},{257,9},{265,257},{2... | collective-permute-start | bytes 1179656 | tf_op jit(solution)/shard_map/ppermute | solution.py:177
  41.9 16.2 %all-to-all-done = bf16[2,128,2560]{2,0,1:T(2,128)(2,1)S(1)} async-done(((bf16[2,128,2560]{2,0,1:T(2,128)(2,1)}), bf16[2,128,2560]{2,0,1:T(2,128)(2,1)S(1)}, u32[]{:S(2)}, u32[]{:S(2)}) %all-to-all-start) | async-done | bytes 1310752 | tf_op jit(solution)/shard_map/all_to_all | solution.py:178
  58.1 2.0 %collective-permute-start.3 = (bf16[2,128,2560]{2,0,1:T(2,128)(2,1)S(1)}, bf16[2,128,2560]{2,0,1:T(2,128)(2,1)S(1)}, u32[]{:S(2)}, u32[]{:S(2)}) collective-permute-start(bf16[2,128,2560]{2,0,1:T(2,128)(2,1)S(1)} %all-to-all-done), channel_id=1, source_target_pairs={{0,128},{128,0},{1,129},{129,1},{2,130},{130,2},{3,131},{131,3},{4... | collective-permute-start | bytes 3932168 | tf_op jit(solution)/shard_map/ppermute | solution.py:180
  60.1 0.0 collective-permute-done.1.refs_2_
  60.1 2.7 %shard_map.31 = (bf16[256,2560]{1,0:T(8,128)(2,1)S(1)}, f32[2,256,256]{2,1,0:T(8,128)S(1)}) custom-call(bf16[128,2,2560]{2,1,0:T(2,128)(2,1)S(1)} %bitcast.8, bf16[2560,256]{1,0:T(8,128)(2,1)S(1)} %copy-done, bf16[2560,256]{1,0:T(8,128)(2,1)} %collective-permute-done.left.refs_1_, bf16[1792,256]{1,0:T(8,128)(2,1)} %collective-permute-done.1.refs_2_, ...), custom_call_target="tpu_custom_call" | custom-call | flops 99999997952 | bytes 4194304 | tf_op jit(solution)/shard_map/pallas_call | solution.py:158
  62.8 0.2 collective-permute-done.3
  63.0 2.3 %shard_map.32 = (bf16[256,2560]{1,0:T(8,128)(2,1)S(1)}, f32[2,256,256]{2,1,0:T(8,128)S(1)}) custom-call(f32[2,256,256]{2,1,0:T(8,128)S(1)} %get-tuple-element.15.first_ref, bf16[128,2,2560]{2,1,0:T(2,128)(2,1)S(1)} %bitcast.9, bf16[2560,256]{1,0:T(8,128)(2,1)S(1)} %copy-done, bf16[2560,256]{1,0:T(8,128)(2,1)} %collective-permute-done.left.refs_1_, ...), custom_call_target="tpu_custom_call" | custom-call | flops 4000000000 | bytes 4194304 | tf_op jit(solution)/shard_map/pallas_call | solution.py:158
  65.3 0.0 collective-permute-done.4.far_top
  65.3 0.4 shard_map.33.most_ref
  65.8 0.0 collective-permute-done.5.far_low
  65.8 1.3 %shard_map.34 = f32[1024,128]{1,0:T(8,128)S(1)} custom-call(f32[2,256,256]{2,1,0:T(8,128)S(1)} %shard_map.33.most_ref, bf16[256,2560]{1,0:T(8,128)(2,1)S(1)} %get-tuple-element.17.own, bf16[256,2560]{1,0:T(8,128)(2,1)S(1)} %get-tuple-element.18.other, bf16[768,256]{1,0:T(8,128)(2,1)} %collective-permute-done.5.far_low), custom_call_target="tpu_custom_call" | custom-call | flops 1000000000 | bytes 4194304 | tf_op jit(solution)/shard_map/pallas_call | solution.py:158
  67.1 34.4 %all_to_all.10 = f32[128,8,128]{2,1,0:T(8,128)S(1)} all-to-all(f32[128,8,128]{2,1,0:T(8,128)S(1)} %bitcast.7), channel_id=1, replica_groups=mesh['xh'=2,'core'=2,'z'=8,'xl'=2,'y'=8] {'core','z','y'}, dimensions={0} | all-to-all | bytes 1048576 | tf_op jit(solution)/shard_map/all_to_all | solution.py:189
  101.5 0.1 bitcast_reduce_fusion
  101.7 0.6 reshape.19
  (5 shorter events, 0.0 us)
Async XLA Ops:
  0.0 29.6 %collective-permute-start = (bf16[2560,256]{1,0:T(8,128)(2,1)}, bf16[2560,256]{1,0:T(8,128)(2,1)}, u32[]{:S(2)}, u32[]{:S(2)}) collective-permute-start(bf16[2560,256]{1,0:T(8,128)(2,1)} %refs_0_.3), channel_id=1, source_target_pairs={{0,8},{8,256},{256,264},{264,0},{1,9},{9,257},{257,265},{265,1},{2... | collective-permute-start | bytes 3932168 | tf_op jit(solution)/shard_map/ppermute | solution.py:171
  3.9 18.0 %copy-start = (bf16[2560,256]{1,0:T(8,128)(2,1)S(1)}, bf16[2560,256]{1,0:T(8,128)(2,1)}, u32[]{:S(2)}) copy-start(bf16[2560,256]{1,0:T(8,128)(2,1)} %refs_0_.3) | copy-start | bytes 3932164
  4.0 54.1 %all-to-all-start = ((bf16[2,128,2560]{2,0,1:T(2,128)(2,1)}), bf16[2,128,2560]{2,0,1:T(2,128)(2,1)S(1)}, u32[]{:S(2)}, u32[]{:S(2)}) async-start(bf16[2,128,2560]{2,0,1:T(2,128)(2,1)} %bitcast.10), calls=%async_computation | async-start | bytes 2621440 | tf_op jit(solution)/shard_map/all_to_all | solution.py:178
  23.0 13.9 %collective-permute-start.2 = (bf16[768,256]{1,0:T(8,128)(2,1)S(1)}, bf16[768,256]{1,0:T(8,128)(2,1)S(1)}, u32[]{:S(2)}, u32[]{:S(2)}) collective-permute-start(bf16[768,256]{1,0:T(8,128)(2,1)S(1)} %get-tuple-element.14), channel_id=1, source_target_pairs={{0,264},{8,0},{256,8},{264,256},{1,265},{9,1},{257,9},{265,257},{2... | collective-permute-start | bytes 1179656 | tf_op jit(solution)/shard_map/ppermute | solution.py:172
  26.4 33.7 %collective-permute-start.1 = (bf16[1792,256]{1,0:T(8,128)(2,1)}, bf16[1792,256]{1,0:T(8,128)(2,1)}, u32[]{:S(2)}, u32[]{:S(2)}) collective-permute-start(bf16[1792,256]{1,0:T(8,128)(2,1)} %get-tuple-element.13), channel_id=1, source_target_pairs={{0,264},{8,0},{256,8},{264,256},{1,265},{9,1},{257,9},{265,257},{2... | collective-permute-start | bytes 2752520 | tf_op jit(solution)/shard_map/ppermute | solution.py:173
  31.7 33.6 %collective-permute-start.4 = (bf16[1792,256]{1,0:T(8,128)(2,1)}, bf16[1792,256]{1,0:T(8,128)(2,1)S(1)}, u32[]{:S(2)}, u32[]{:S(2)}) collective-permute-start(bf16[1792,256]{1,0:T(8,128)(2,1)} %shard_map.28.left_top), channel_id=1, source_target_pairs={{0,8},{8,256},{256,264},{264,0},{1,9},{9,257},{257,265},{265,1},{2... | collective-permute-start | bytes 2752520 | tf_op jit(solution)/shard_map/ppermute | solution.py:176
  37.7 28.1 %collective-permute-start.5 = (bf16[768,256]{1,0:T(8,128)(2,1)}, bf16[768,256]{1,0:T(8,128)(2,1)}, u32[]{:S(2)}, u32[]{:S(2)}) collective-permute-start(bf16[768,256]{1,0:T(8,128)(2,1)} %shard_map.30.refs_3_), channel_id=1, source_target_pairs={{0,264},{8,0},{256,8},{264,256},{1,265},{9,1},{257,9},{265,257},{2... | collective-permute-start | bytes 1179656 | tf_op jit(solution)/shard_map/ppermute | solution.py:177
  58.1 4.9 %collective-permute-start.3 = (bf16[2,128,2560]{2,0,1:T(2,128)(2,1)S(1)}, bf16[2,128,2560]{2,0,1:T(2,128)(2,1)S(1)}, u32[]{:S(2)}, u32[]{:S(2)}) collective-permute-start(bf16[2,128,2560]{2,0,1:T(2,128)(2,1)S(1)} %all-to-all-done), channel_id=1, source_target_pairs={{0,128},{128,0},{1,129},{129,1},{2,130},{130,2},{3,131},{131,3},{4... | collective-permute-start | bytes 3932168 | tf_op jit(solution)/shard_map/ppermute | solution.py:180

commit v10 on v9

--- a/solution.py
+++ b/solution.py
@@ -13,7 +13,7 @@
 ANY = pl.BlockSpec(memory_space=pl.ANY)
 LIMIT = 20 * 2**20
 H_LIMIT = 8 * 2**20
-SPLIT = 1792
+SPLIT = 1664
 G_FLOPS = 18 * 10**9
 FLOPS = 10**11
 L_FLOPS = 10**9

time: 103 us -> 103 us (level)
  no operation moved by 1% of the time
where the time goes in v10:
time: 103 us; the launch traced here: 102 us
  starting transfers between devices  39.9 us (39%)
  blocking collectives  34.3 us (33%)
  waiting for transfers between devices  16.4 us (16%)
  Pallas kernels  10.7 us (10%)
    all_to_all x1, blocking collectives, shards(): lax.all_to_all(partial, ('core', 'z', 'y'), split_axis=0, concat_axis=0,...  34.3 us
    all_to_all x1, starting transfers between devices, shards(): lax.all_to_all(amplitudes.reshape(2, 128, 2560), ('z', 'core', 'y'), spli...  18 us
    all_to_all x1, waiting for transfers between devices, shards(): lax.all_to_all(amplitudes.reshape(2, 128, 2560), ('z', 'core', 'y'), spli...  16.2 us
    pallas_call x4, Pallas kernels, run(): pl.pallas_call(kernel, out_shape=outs, in_specs=[VMEM] * len(operands), o...  6.83 us
    ppermute x1, starting transfers between devices, shards(): far_top = lax.ppermute(left_top, RING, RIGHT)  5.27 us
    ppermute x1, starting transfers between devices, shards(): far_low = lax.ppermute(right_low, RING, LEFT)  4.17 us
    ppermute x1, starting transfers between devices, shards(): left = lax.ppermute(integrals, RING, RIGHT)  3.94 us
    ppermute x1, starting transfers between devices, shards(): right_low = lax.ppermute(low, RING, LEFT)  3.36 us
  transfers between devices with their start and end apart: 7, of which 2 were waited for; matrix products, arithmetic and copies ran while one was open for 0% of the time, Pallas kernels for 9%

profile of v10, /device:TPU:1, one launch (start us, length us, event | category | flops | bytes accessed | tf_op | source)
XLA Modules:
  0.0 102.2 jit_solution(13416490486484724158)
XLA Ops:
  0.0 3.9 %collective-permute-start = (bf16[2560,256]{1,0:T(8,128)(2,1)}, bf16[2560,256]{1,0:T(8,128)(2,1)}, u32[]{:S(2)}, u32[]{:S(2)}) collective-permute-start(bf16[2560,256]{1,0:T(8,128)(2,1)} %refs_0_.3), channel_id=1, source_target_pairs={{0,8},{8,256},{256,264},{264,0},{1,9},{9,257},{257,265},{265,1},{2... | collective-permute-start | bytes 3932168 | tf_op jit(solution)/shard_map/ppermute | solution.py:171
  4.0 18.0 %all-to-all-start = ((bf16[2,128,2560]{2,0,1:T(2,128)(2,1)}), bf16[2,128,2560]{2,0,1:T(2,128)(2,1)S(1)}, u32[]{:S(2)}, u32[]{:S(2)}) async-start(bf16[2,128,2560]{2,0,1:T(2,128)(2,1)} %bitcast.10), calls=%async_computation | async-start | bytes 2621440 | tf_op jit(solution)/shard_map/all_to_all | solution.py:178
  22.0 1.0 shard_map.29
  23.0 3.4 %collective-permute-start.2 = (bf16[896,256]{1,0:T(8,128)(2,1)S(1)}, bf16[896,256]{1,0:T(8,128)(2,1)S(1)}, u32[]{:S(2)}, u32[]{:S(2)}) collective-permute-start(bf16[896,256]{1,0:T(8,128)(2,1)S(1)} %get-tuple-element.14), channel_id=1, source_target_pairs={{0,264},{8,0},{256,8},{264,256},{1,265},{9,1},{257,9},{265,257},{2... | collective-permute-start | bytes 1376264 | tf_op jit(solution)/shard_map/ppermute | solution.py:172
  26.3 3.2 %collective-permute-start.1 = (bf16[1664,256]{1,0:T(8,128)(2,1)}, bf16[1664,256]{1,0:T(8,128)(2,1)}, u32[]{:S(2)}, u32[]{:S(2)}) collective-permute-start(bf16[1664,256]{1,0:T(8,128)(2,1)} %get-tuple-element.13), channel_id=1, source_target_pairs={{0,264},{8,0},{256,8},{264,256},{1,265},{9,1},{257,9},{265,257},{2... | collective-permute-start | bytes 2555912 | tf_op jit(solution)/shard_map/ppermute | solution.py:173
  29.5 0.0 collective-permute-done.left.refs_1_
  29.5 2.1 %shard_map.28.left_top = bf16[1664,256]{1,0:T(8,128)(2,1)} custom-call(bf16[2560,256]{1,0:T(8,128)(2,1)} %collective-permute-done.left.refs_1_), custom_call_target="tpu_custom_call" | custom-call | flops 17999998976 | bytes 2097152 | tf_op jit(solution)/shard_map/pallas_call | solution.py:31
  31.6 5.3 %collective-permute-start.4 = (bf16[1664,256]{1,0:T(8,128)(2,1)}, bf16[1664,256]{1,0:T(8,128)(2,1)S(1)}, u32[]{:S(2)}, u32[]{:S(2)}) collective-permute-start(bf16[1664,256]{1,0:T(8,128)(2,1)} %shard_map.28.left_top), channel_id=1, source_target_pairs={{0,8},{8,256},{256,264},{264,0},{1,9},{9,257},{257,265},{265,1},{2... | collective-permute-start | bytes 2555912 | tf_op jit(solution)/shard_map/ppermute | solution.py:176
  36.9 0.0 collective-permute-done.2.right_low
  36.9 0.8 shard_map.30.refs_3_
  37.7 4.2 %collective-permute-start.5 = (bf16[896,256]{1,0:T(8,128)(2,1)}, bf16[896,256]{1,0:T(8,128)(2,1)}, u32[]{:S(2)}, u32[]{:S(2)}) collective-permute-start(bf16[896,256]{1,0:T(8,128)(2,1)} %shard_map.30.refs_3_), channel_id=1, source_target_pairs={{0,264},{8,0},{256,8},{264,256},{1,265},{9,1},{257,9},{265,257},{2... | collective-permute-start | bytes 1376264 | tf_op jit(solution)/shard_map/ppermute | solution.py:177
  41.9 16.2 %all-to-all-done = bf16[2,128,2560]{2,0,1:T(2,128)(2,1)S(1)} async-done(((bf16[2,128,2560]{2,0,1:T(2,128)(2,1)}), bf16[2,128,2560]{2,0,1:T(2,128)(2,1)S(1)}, u32[]{:S(2)}, u32[]{:S(2)}) %all-to-all-start) | async-done | bytes 1310752 | tf_op jit(solution)/shard_map/all_to_all | solution.py:178
  58.1 2.0 %collective-permute-start.3 = (bf16[2,128,2560]{2,0,1:T(2,128)(2,1)S(1)}, bf16[2,128,2560]{2,0,1:T(2,128)(2,1)S(1)}, u32[]{:S(2)}, u32[]{:S(2)}) collective-permute-start(bf16[2,128,2560]{2,0,1:T(2,128)(2,1)S(1)} %all-to-all-done), channel_id=1, source_target_pairs={{0,128},{128,0},{1,129},{129,1},{2,130},{130,2},{3,131},{131,3},{4... | collective-permute-start | bytes 3932168 | tf_op jit(solution)/shard_map/ppermute | solution.py:180
  60.1 0.0 collective-permute-done.1.refs_2_
  60.1 2.7 %shard_map.31 = (bf16[256,2560]{1,0:T(8,128)(2,1)S(1)}, f32[2,256,256]{2,1,0:T(8,128)S(1)}) custom-call(bf16[128,2,2560]{2,1,0:T(2,128)(2,1)S(1)} %bitcast.8, bf16[2560,256]{1,0:T(8,128)(2,1)S(1)} %copy-done, bf16[2560,256]{1,0:T(8,128)(2,1)} %collective-permute-done.left.refs_1_, bf16[1664,256]{1,0:T(8,128)(2,1)} %collective-permute-done.1.refs_2_, ...), custom_call_target="tpu_custom_call" | custom-call | flops 99999997952 | bytes 4194304 | tf_op jit(solution)/shard_map/pallas_call | solution.py:158
  62.8 0.2 collective-permute-done.3
  63.0 2.3 %shard_map.32 = (bf16[256,2560]{1,0:T(8,128)(2,1)S(1)}, f32[2,256,256]{2,1,0:T(8,128)S(1)}) custom-call(f32[2,256,256]{2,1,0:T(8,128)S(1)} %get-tuple-element.15.first_ref, bf16[128,2,2560]{2,1,0:T(2,128)(2,1)S(1)} %bitcast.9, bf16[2560,256]{1,0:T(8,128)(2,1)S(1)} %copy-done, bf16[2560,256]{1,0:T(8,128)(2,1)} %collective-permute-done.left.refs_1_, ...), custom_call_target="tpu_custom_call" | custom-call | flops 4000000000 | bytes 4194304 | tf_op jit(solution)/shard_map/pallas_call | solution.py:158
  65.3 0.0 collective-permute-done.4.far_top
  65.3 0.4 shard_map.33.most_ref
  65.8 0.0 collective-permute-done.5.far_low
  65.8 1.4 %shard_map.34 = f32[1024,128]{1,0:T(8,128)S(1)} custom-call(f32[2,256,256]{2,1,0:T(8,128)S(1)} %shard_map.33.most_ref, bf16[256,2560]{1,0:T(8,128)(2,1)S(1)} %get-tuple-element.17.own, bf16[256,2560]{1,0:T(8,128)(2,1)S(1)} %get-tuple-element.18.other, bf16[896,256]{1,0:T(8,128)(2,1)} %collective-permute-done.5.far_low), custom_call_target="tpu_custom_call" | custom-call | flops 1000000000 | bytes 4194304 | tf_op jit(solution)/shard_map/pallas_call | solution.py:158
  67.2 34.3 %all_to_all.10 = f32[128,8,128]{2,1,0:T(8,128)S(1)} all-to-all(f32[128,8,128]{2,1,0:T(8,128)S(1)} %bitcast.7), channel_id=1, replica_groups=mesh['xh'=2,'core'=2,'z'=8,'xl'=2,'y'=8] {'core','z','y'}, dimensions={0} | all-to-all | bytes 1048576 | tf_op jit(solution)/shard_map/all_to_all | solution.py:189
  101.5 0.1 bitcast_reduce_fusion
  101.6 0.6 reshape.19
  (5 shorter events, 0.0 us)
Async XLA Ops:
  0.0 29.5 %collective-permute-start = (bf16[2560,256]{1,0:T(8,128)(2,1)}, bf16[2560,256]{1,0:T(8,128)(2,1)}, u32[]{:S(2)}, u32[]{:S(2)}) collective-permute-start(bf16[2560,256]{1,0:T(8,128)(2,1)} %refs_0_.3), channel_id=1, source_target_pairs={{0,8},{8,256},{256,264},{264,0},{1,9},{9,257},{257,265},{265,1},{2... | collective-permute-start | bytes 3932168 | tf_op jit(solution)/shard_map/ppermute | solution.py:171
  3.9 18.0 %copy-start = (bf16[2560,256]{1,0:T(8,128)(2,1)S(1)}, bf16[2560,256]{1,0:T(8,128)(2,1)}, u32[]{:S(2)}) copy-start(bf16[2560,256]{1,0:T(8,128)(2,1)} %refs_0_.3) | copy-start | bytes 3932164
  4.0 54.1 %all-to-all-start = ((bf16[2,128,2560]{2,0,1:T(2,128)(2,1)}), bf16[2,128,2560]{2,0,1:T(2,128)(2,1)S(1)}, u32[]{:S(2)}, u32[]{:S(2)}) async-start(bf16[2,128,2560]{2,0,1:T(2,128)(2,1)} %bitcast.10), calls=%async_computation | async-start | bytes 2621440 | tf_op jit(solution)/shard_map/all_to_all | solution.py:178
  23.0 13.9 %collective-permute-start.2 = (bf16[896,256]{1,0:T(8,128)(2,1)S(1)}, bf16[896,256]{1,0:T(8,128)(2,1)S(1)}, u32[]{:S(2)}, u32[]{:S(2)}) collective-permute-start(bf16[896,256]{1,0:T(8,128)(2,1)S(1)} %get-tuple-element.14), channel_id=1, source_target_pairs={{0,264},{8,0},{256,8},{264,256},{1,265},{9,1},{257,9},{265,257},{2... | collective-permute-start | bytes 1376264 | tf_op jit(solution)/shard_map/ppermute | solution.py:172
  26.3 33.8 %collective-permute-start.1 = (bf16[1664,256]{1,0:T(8,128)(2,1)}, bf16[1664,256]{1,0:T(8,128)(2,1)}, u32[]{:S(2)}, u32[]{:S(2)}) collective-permute-start(bf16[1664,256]{1,0:T(8,128)(2,1)} %get-tuple-element.13), channel_id=1, source_target_pairs={{0,264},{8,0},{256,8},{264,256},{1,265},{9,1},{257,9},{265,257},{2... | collective-permute-start | bytes 2555912 | tf_op jit(solution)/shard_map/ppermute | solution.py:173
  31.6 33.7 %collective-permute-start.4 = (bf16[1664,256]{1,0:T(8,128)(2,1)}, bf16[1664,256]{1,0:T(8,128)(2,1)S(1)}, u32[]{:S(2)}, u32[]{:S(2)}) collective-permute-start(bf16[1664,256]{1,0:T(8,128)(2,1)} %shard_map.28.left_top), channel_id=1, source_target_pairs={{0,8},{8,256},{256,264},{264,0},{1,9},{9,257},{257,265},{265,1},{2... | collective-permute-start | bytes 2555912 | tf_op jit(solution)/shard_map/ppermute | solution.py:176
  37.7 28.1 %collective-permute-start.5 = (bf16[896,256]{1,0:T(8,128)(2,1)}, bf16[896,256]{1,0:T(8,128)(2,1)}, u32[]{:S(2)}, u32[]{:S(2)}) collective-permute-start(bf16[896,256]{1,0:T(8,128)(2,1)} %shard_map.30.refs_3_), channel_id=1, source_target_pairs={{0,264},{8,0},{256,8},{264,256},{1,265},{9,1},{257,9},{265,257},{2... | collective-permute-start | bytes 1376264 | tf_op jit(solution)/shard_map/ppermute | solution.py:177
  58.1 4.9 %collective-permute-start.3 = (bf16[2,128,2560]{2,0,1:T(2,128)(2,1)S(1)}, bf16[2,128,2560]{2,0,1:T(2,128)(2,1)S(1)}, u32[]{:S(2)}, u32[]{:S(2)}) collective-permute-start(bf16[2,128,2560]{2,0,1:T(2,128)(2,1)S(1)} %all-to-all-done), channel_id=1, source_target_pairs={{0,128},{128,0},{1,129},{129,1},{2,130},{130,2},{3,131},{131,3},{4... | collective-permute-start | bytes 3932168 | tf_op jit(solution)/shard_map/ppermute | solution.py:180

commit v11 on v9

--- a/solution.py
+++ b/solution.py
@@ -21,10 +21,18 @@
 N_FLOPS = 4 * 10**9
 
 
-def keep(left, top_ref, sem):
-    top = pltpu.make_async_copy(left.at[:SPLIT], top_ref, sem)
-    top.start()
-    top.wait()
+def keep(left, top_ref, passing, sems):
+    rows = SPLIT // 4
+    spans = [pl.ds(rows * n, rows) for n in range(4)]
+    reads = [pltpu.make_async_copy(left.at[span], passing.at[n], sems.at[n]) for n, span in enumerate(spans)]
+    writes = [pltpu.make_async_copy(passing.at[n], top_ref.at[span], sems.at[4 + n]) for n, span in enumerate(spans)]
+    for read in reads:
+        read.start()
+    for read, write in zip(reads, writes):
+        read.wait()
+        write.start()
+    for write in writes:
+        write.wait()
 
 
 def kept(left):
@@ -32,8 +40,8 @@
         keep,
         out_shape=jax.ShapeDtypeStruct((SPLIT, 256), jnp.bfloat16),
         in_specs=[ANY],
-        out_specs=VMEM,
-        scratch_shapes=[pltpu.SemaphoreType.DMA],
+        out_specs=ANY,
+        scratch_shapes=[pltpu.VMEM((4, SPLIT // 4, 256), jnp.bfloat16), pltpu.SemaphoreType.DMA((8,))],
         compiler_params=pltpu.CompilerParams(vmem_limit_bytes=H_LIMIT),
         cost_estimate=pl.CostEstimate(flops=G_FLOPS, bytes_accessed=2**21, transcendentals=0),
     )(left)

time: 103 us -> 103 us (level)
  no operation moved by 1% of the time
where the time goes in v11:
time: 103 us; the launch traced here: 102 us
  starting transfers between devices  39.9 us (39%)
  blocking collectives  34.3 us (33%)
  waiting for transfers between devices  16.5 us (16%)
  Pallas kernels  10.6 us (10%)
    all_to_all x1, blocking collectives, shards(): lax.all_to_all(partial, ('core', 'z', 'y'), split_axis=0, concat_axis=0,...  34.3 us
    all_to_all x1, starting transfers between devices, shards(): lax.all_to_all(amplitudes.reshape(2, 128, 2560), ('z', 'core', 'y'), spli...  18 us
    all_to_all x1, waiting for transfers between devices, shards(): lax.all_to_all(amplitudes.reshape(2, 128, 2560), ('z', 'core', 'y'), spli...  16.3 us
    pallas_call x4, Pallas kernels, run(): pl.pallas_call(kernel, out_shape=outs, in_specs=[VMEM] * len(operands), o...  6.74 us
    ppermute x1, starting transfers between devices, shards(): far_top = lax.ppermute(left_top, RING, RIGHT)  5.22 us
    ppermute x1, starting transfers between devices, shards(): far_low = lax.ppermute(right_low, RING, LEFT)  4.17 us
    ppermute x1, starting transfers between devices, shards(): left = lax.ppermute(integrals, RING, RIGHT)  3.94 us
    ppermute x1, starting transfers between devices, shards(): right_low = lax.ppermute(low, RING, LEFT)  3.36 us
  transfers between devices with their start and end apart: 7, of which 2 were waited for; matrix products, arithmetic and copies ran while one was open for 0% of the time, Pallas kernels for 9%

profile of v11, /device:TPU:1, one launch (start us, length us, event | category | flops | bytes accessed | tf_op | source)
XLA Modules:
  0.0 102.2 jit_solution(1694551906211129017)
XLA Ops:
  0.0 3.9 %collective-permute-start = (bf16[2560,256]{1,0:T(8,128)(2,1)}, bf16[2560,256]{1,0:T(8,128)(2,1)}, u32[]{:S(2)}, u32[]{:S(2)}) collective-permute-start(bf16[2560,256]{1,0:T(8,128)(2,1)} %refs_0_.3), channel_id=1, source_target_pairs={{0,8},{8,256},{256,264},{264,0},{1,9},{9,257},{257,265},{265,1},{2... | collective-permute-start | bytes 3932168 | tf_op jit(solution)/shard_map/ppermute | solution.py:179
  4.0 18.0 %all-to-all-start = ((bf16[2,128,2560]{2,0,1:T(2,128)(2,1)}), bf16[2,128,2560]{2,0,1:T(2,128)(2,1)S(1)}, u32[]{:S(2)}, u32[]{:S(2)}) async-start(bf16[2,128,2560]{2,0,1:T(2,128)(2,1)} %bitcast.10), calls=%async_computation | async-start | bytes 2621440 | tf_op jit(solution)/shard_map/all_to_all | solution.py:186
  22.0 1.0 %shard_map.29 = (bf16[1792,256]{1,0:T(8,128)(2,1)}, bf16[768,256]{1,0:T(8,128)(2,1)S(1)}) custom-call(bf16[2560,256]{1,0:T(8,128)(2,1)S(1)} %copy-done), custom_call_target="tpu_custom_call" | custom-call | tf_op jit(solution)/shard_map/pallas_call | solution.py:71
  23.0 3.4 %collective-permute-start.2 = (bf16[768,256]{1,0:T(8,128)(2,1)S(1)}, bf16[768,256]{1,0:T(8,128)(2,1)S(1)}, u32[]{:S(2)}, u32[]{:S(2)}) collective-permute-start(bf16[768,256]{1,0:T(8,128)(2,1)S(1)} %get-tuple-element.14), channel_id=1, source_target_pairs={{0,264},{8,0},{256,8},{264,256},{1,265},{9,1},{257,9},{265,257},{2... | collective-permute-start | bytes 1179656 | tf_op jit(solution)/shard_map/ppermute | solution.py:180
  26.4 3.2 %collective-permute-start.1 = (bf16[1792,256]{1,0:T(8,128)(2,1)}, bf16[1792,256]{1,0:T(8,128)(2,1)}, u32[]{:S(2)}, u32[]{:S(2)}) collective-permute-start(bf16[1792,256]{1,0:T(8,128)(2,1)} %get-tuple-element.13), channel_id=1, source_target_pairs={{0,264},{8,0},{256,8},{264,256},{1,265},{9,1},{257,9},{265,257},{2... | collective-permute-start | bytes 2752520 | tf_op jit(solution)/shard_map/ppermute | solution.py:181
  29.6 0.0 collective-permute-done.left.refs_1_
  29.6 2.0 %shard_map.28.left_top = bf16[1792,256]{1,0:T(8,128)(2,1)} custom-call(bf16[2560,256]{1,0:T(8,128)(2,1)} %collective-permute-done.left.refs_1_), custom_call_target="tpu_custom_call" | custom-call | flops 17999998976 | bytes 2097152 | tf_op jit(solution)/shard_map/pallas_call | solution.py:39
  31.6 5.2 %collective-permute-start.4 = (bf16[1792,256]{1,0:T(8,128)(2,1)}, bf16[1792,256]{1,0:T(8,128)(2,1)S(1)}, u32[]{:S(2)}, u32[]{:S(2)}) collective-permute-start(bf16[1792,256]{1,0:T(8,128)(2,1)} %shard_map.28.left_top), channel_id=1, source_target_pairs={{0,8},{8,256},{256,264},{264,0},{1,9},{9,257},{257,265},{265,1},{2... | collective-permute-start | bytes 2752520 | tf_op jit(solution)/shard_map/ppermute | solution.py:184
  36.9 0.0 collective-permute-done.2.right_low
  36.9 0.8 shard_map.30.refs_3_
  37.6 4.2 %collective-permute-start.5 = (bf16[768,256]{1,0:T(8,128)(2,1)}, bf16[768,256]{1,0:T(8,128)(2,1)}, u32[]{:S(2)}, u32[]{:S(2)}) collective-permute-start(bf16[768,256]{1,0:T(8,128)(2,1)} %shard_map.30.refs_3_), channel_id=1, source_target_pairs={{0,264},{8,0},{256,8},{264,256},{1,265},{9,1},{257,9},{265,257},{2... | collective-permute-start | bytes 1179656 | tf_op jit(solution)/shard_map/ppermute | solution.py:185
  41.8 16.3 %all-to-all-done = bf16[2,128,2560]{2,0,1:T(2,128)(2,1)S(1)} async-done(((bf16[2,128,2560]{2,0,1:T(2,128)(2,1)}), bf16[2,128,2560]{2,0,1:T(2,128)(2,1)S(1)}, u32[]{:S(2)}, u32[]{:S(2)}) %all-to-all-start) | async-done | bytes 1310752 | tf_op jit(solution)/shard_map/all_to_all | solution.py:186
  58.1 2.0 %collective-permute-start.3 = (bf16[2,128,2560]{2,0,1:T(2,128)(2,1)S(1)}, bf16[2,128,2560]{2,0,1:T(2,128)(2,1)S(1)}, u32[]{:S(2)}, u32[]{:S(2)}) collective-permute-start(bf16[2,128,2560]{2,0,1:T(2,128)(2,1)S(1)} %all-to-all-done), channel_id=1, source_target_pairs={{0,128},{128,0},{1,129},{129,1},{2,130},{130,2},{3,131},{131,3},{4... | collective-permute-start | bytes 3932168 | tf_op jit(solution)/shard_map/ppermute | solution.py:188
  60.1 0.0 collective-permute-done.1.refs_2_
  60.1 2.7 %shard_map.31 = (bf16[256,2560]{1,0:T(8,128)(2,1)S(1)}, f32[2,256,256]{2,1,0:T(8,128)S(1)}) custom-call(bf16[128,2,2560]{2,1,0:T(2,128)(2,1)S(1)} %bitcast.8, bf16[2560,256]{1,0:T(8,128)(2,1)S(1)} %copy-done, bf16[2560,256]{1,0:T(8,128)(2,1)} %collective-permute-done.left.refs_1_, bf16[1792,256]{1,0:T(8,128)(2,1)} %collective-permute-done.1.refs_2_, ...), custom_call_target="tpu_custom_call" | custom-call | flops 99999997952 | bytes 4194304 | tf_op jit(solution)/shard_map/pallas_call | solution.py:166
  62.8 0.2 collective-permute-done.3
  63.0 2.3 %shard_map.32 = (bf16[256,2560]{1,0:T(8,128)(2,1)S(1)}, f32[2,256,256]{2,1,0:T(8,128)S(1)}) custom-call(f32[2,256,256]{2,1,0:T(8,128)S(1)} %get-tuple-element.15.first_ref, bf16[128,2,2560]{2,1,0:T(2,128)(2,1)S(1)} %bitcast.9, bf16[2560,256]{1,0:T(8,128)(2,1)S(1)} %copy-done, bf16[2560,256]{1,0:T(8,128)(2,1)} %collective-permute-done.left.refs_1_, ...), custom_call_target="tpu_custom_call" | custom-call | flops 4000000000 | bytes 4194304 | tf_op jit(solution)/shard_map/pallas_call | solution.py:166
  65.3 0.0 collective-permute-done.4.far_top
  65.3 0.4 shard_map.33.most_ref
  65.8 0.0 collective-permute-done.5.far_low
  65.8 1.3 %shard_map.34 = f32[1024,128]{1,0:T(8,128)S(1)} custom-call(f32[2,256,256]{2,1,0:T(8,128)S(1)} %shard_map.33.most_ref, bf16[256,2560]{1,0:T(8,128)(2,1)S(1)} %get-tuple-element.17.own, bf16[256,2560]{1,0:T(8,128)(2,1)S(1)} %get-tuple-element.18.other, bf16[768,256]{1,0:T(8,128)(2,1)} %collective-permute-done.5.far_low), custom_call_target="tpu_custom_call" | custom-call | flops 1000000000 | bytes 4194304 | tf_op jit(solution)/shard_map/pallas_call | solution.py:166
  67.1 34.3 %all_to_all.10 = f32[128,8,128]{2,1,0:T(8,128)S(1)} all-to-all(f32[128,8,128]{2,1,0:T(8,128)S(1)} %bitcast.7), channel_id=1, replica_groups=mesh['xh'=2,'core'=2,'z'=8,'xl'=2,'y'=8] {'core','z','y'}, dimensions={0} | all-to-all | bytes 1048576 | tf_op jit(solution)/shard_map/all_to_all | solution.py:197
  101.5 0.1 bitcast_reduce_fusion
  101.6 0.6 reshape.19
  (5 shorter events, 0.0 us)
Async XLA Ops:
  0.0 29.6 %collective-permute-start = (bf16[2560,256]{1,0:T(8,128)(2,1)}, bf16[2560,256]{1,0:T(8,128)(2,1)}, u32[]{:S(2)}, u32[]{:S(2)}) collective-permute-start(bf16[2560,256]{1,0:T(8,128)(2,1)} %refs_0_.3), channel_id=1, source_target_pairs={{0,8},{8,256},{256,264},{264,0},{1,9},{9,257},{257,265},{265,1},{2... | collective-permute-start | bytes 3932168 | tf_op jit(solution)/shard_map/ppermute | solution.py:179
  3.9 18.0 %copy-start = (bf16[2560,256]{1,0:T(8,128)(2,1)S(1)}, bf16[2560,256]{1,0:T(8,128)(2,1)}, u32[]{:S(2)}) copy-start(bf16[2560,256]{1,0:T(8,128)(2,1)} %refs_0_.3) | copy-start | bytes 3932164
  4.0 54.1 %all-to-all-start = ((bf16[2,128,2560]{2,0,1:T(2,128)(2,1)}), bf16[2,128,2560]{2,0,1:T(2,128)(2,1)S(1)}, u32[]{:S(2)}, u32[]{:S(2)}) async-start(bf16[2,128,2560]{2,0,1:T(2,128)(2,1)} %bitcast.10), calls=%async_computation | async-start | bytes 2621440 | tf_op jit(solution)/shard_map/all_to_all | solution.py:186
  23.0 13.9 %collective-permute-start.2 = (bf16[768,256]{1,0:T(8,128)(2,1)S(1)}, bf16[768,256]{1,0:T(8,128)(2,1)S(1)}, u32[]{:S(2)}, u32[]{:S(2)}) collective-permute-start(bf16[768,256]{1,0:T(8,128)(2,1)S(1)} %get-tuple-element.14), channel_id=1, source_target_pairs={{0,264},{8,0},{256,8},{264,256},{1,265},{9,1},{257,9},{265,257},{2... | collective-permute-start | bytes 1179656 | tf_op jit(solution)/shard_map/ppermute | solution.py:180
  26.4 33.7 %collective-permute-start.1 = (bf16[1792,256]{1,0:T(8,128)(2,1)}, bf16[1792,256]{1,0:T(8,128)(2,1)}, u32[]{:S(2)}, u32[]{:S(2)}) collective-permute-start(bf16[1792,256]{1,0:T(8,128)(2,1)} %get-tuple-element.13), channel_id=1, source_target_pairs={{0,264},{8,0},{256,8},{264,256},{1,265},{9,1},{257,9},{265,257},{2... | collective-permute-start | bytes 2752520 | tf_op jit(solution)/shard_map/ppermute | solution.py:181
  31.6 33.7 %collective-permute-start.4 = (bf16[1792,256]{1,0:T(8,128)(2,1)}, bf16[1792,256]{1,0:T(8,128)(2,1)S(1)}, u32[]{:S(2)}, u32[]{:S(2)}) collective-permute-start(bf16[1792,256]{1,0:T(8,128)(2,1)} %shard_map.28.left_top), channel_id=1, source_target_pairs={{0,8},{8,256},{256,264},{264,0},{1,9},{9,257},{257,265},{265,1},{2... | collective-permute-start | bytes 2752520 | tf_op jit(solution)/shard_map/ppermute | solution.py:184
  37.6 28.1 %collective-permute-start.5 = (bf16[768,256]{1,0:T(8,128)(2,1)}, bf16[768,256]{1,0:T(8,128)(2,1)}, u32[]{:S(2)}, u32[]{:S(2)}) collective-permute-start(bf16[768,256]{1,0:T(8,128)(2,1)} %shard_map.30.refs_3_), channel_id=1, source_target_pairs={{0,264},{8,0},{256,8},{264,256},{1,265},{9,1},{257,9},{265,257},{2... | collective-permute-start | bytes 1179656 | tf_op jit(solution)/shard_map/ppermute | solution.py:185
  58.1 4.9 %collective-permute-start.3 = (bf16[2,128,2560]{2,0,1:T(2,128)(2,1)S(1)}, bf16[2,128,2560]{2,0,1:T(2,128)(2,1)S(1)}, u32[]{:S(2)}, u32[]{:S(2)}) collective-permute-start(bf16[2,128,2560]{2,0,1:T(2,128)(2,1)S(1)} %all-to-all-done), channel_id=1, source_target_pairs={{0,128},{128,0},{1,129},{129,1},{2,130},{130,2},{3,131},{131,3},{4... | collective-permute-start | bytes 3932168 | tf_op jit(solution)/shard_map/ppermute | solution.py:188
